TPU v7x, 32 devices: a whole 2x2x4 slice. The times are simulated.
32 devices in a mesh: seq: 16 (over z, y, x), head: 2 (over core).
Axes of the slice: x: 2, y: 2, z: 4, core: 2. Of those that a mesh axis runs over, the one named last changes fastest.
Arguments:
- query_one: bfloat16 [2048, 32, 128], P('seq', 'head'), may hold values from -6 to 6
- key_one: bfloat16 [2048, 32, 128], P('seq', 'head'), may hold values from -6 to 6
- value_one: bfloat16 [2048, 32, 128], P('seq', 'head'), may hold values from -160 to 160
- log_decay: float32 [32, 2048], P('head', 'seq'), may hold values from -1 to 0
- query_two: bfloat16 [2048, 32, 128], P('seq', 'head'), may hold values from -24 to 24
- key_two: bfloat16 [2048, 32, 128], P('seq', 'head'), may hold values from -24 to 24
- out_grad: bfloat16 [2048, 32, 128], P('seq', 'head'), may hold values from -6 to 6
- doc_ids: int32 [16], replicated, may hold values from 0 to 3, never falling along the last dimension, each value on 1 to 8 neighbouring positions
Outputs:
- grad_query_one: float32 [2048, 32, 128], P('seq', 'head')
- grad_key_one: float32 [2048, 32, 128], P('seq', 'head')
- grad_value_one: float32 [2048, 32, 128], P('seq', 'head')
- grad_query_two: float32 [2048, 32, 128], P('seq', 'head')
- grad_key_two: float32 [2048, 32, 128], P('seq', 'head')
Inputs may be any that keep to these rules, and one draw needn't show every extreme that they name: doc_ids never fall along the sequence; one document covers at most 8 blocks.
All inputs are finite; a program needn't handle non-finite values.
Results may differ from a plain program's by a relative error of at most 0.0096.
Values may be sent and summed in bfloat16 or wider, within the bound.
No kernel may reach another device: no remote copies, remote signals or barrier semaphores. Data moves between devices by JAX's collectives and lax.ppermute only.
A program may use at most 128 MiB of HBM per device.

v0:
```python
from functools import partial
import math

import jax
import jax.numpy as jnp
from jax import lax
from jax.sharding import PartitionSpec as P

BLOCK = 128
REACH = 8


exact_precision = lax.Precision.HIGHEST
floor_score = -1e30
norm_epsilon = 1e-05


def prefix(value, axis, join, neutral, backward):
    count, mine = (lax.axis_size(axis), lax.axis_index(axis))
    pieces = jax.tree.map(lambda part: lax.all_gather(part, axis), value)
    if backward:
        pieces = jax.tree.map(lambda part: part[::-1], pieces)
        mine = count - 1 - mine
    total = jax.tree.map(
        lambda part, zero: jnp.full_like(part, 0) + jnp.asarray(zero, part.dtype), value, neutral
    )

    def hop(position, total):
        longer = join(total, jax.tree.map(lambda part: part[position], pieces))
        return jax.tree.map(lambda new, old: jnp.where(position < mine, new, old), longer, total)

    return lax.fori_loop(0, count - 1, hop, total)


def from_behind(block, axis, distance):
    devices = range(lax.axis_size(axis))
    route = [(i - distance, i) for i in devices if i - distance in devices]
    return lax.ppermute(block, axis, route)


def for_sending(shard):
    return jax.tree.map(lambda a: a.astype(jnp.bfloat16) if a.dtype == jnp.float32 else a, shard)


def lower_mask(length):
    return lax.broadcasted_iota(jnp.int32, (length, length), 0) >= lax.broadcasted_iota(
        jnp.int32, (length, length), 1
    )


def shard_output(q_float, k_float, v_float, cumulative, incoming):
    lower = lower_mask(q_float.shape[0])[None]
    gaps = cumulative[:, :, None] - cumulative[:, None, :]
    weights = jnp.where(lower, jnp.exp(jnp.where(lower, gaps, 0.0)), 0.0)
    scores = jnp.einsum("thd,uhd->htu", q_float, k_float, precision=exact_precision) * weights
    inner_part = jnp.einsum("htu,uhe->the", scores, v_float, precision=exact_precision)
    outer_part = jnp.einsum(
        "thd,hde->the",
        q_float * jnp.exp(cumulative).T[:, :, None],
        incoming,
        precision=exact_precision,
    )
    return inner_part + outer_part


def shard_state(k_float, v_float, cumulative):
    tail_decay = jnp.exp(cumulative[:, -1:] - cumulative)
    return jnp.einsum(
        "uhd,uhe->hde", k_float * tail_decay.T[:, :, None], v_float, precision=exact_precision
    )


def chain_join(earlier, later):
    return (earlier[0] * later[0], later[0][:, None, None] * earlier[1] + later[1])


def scores_work(query_two, keys_block, allowed, scale):
    raw_scores = (
        jnp.einsum("thd,uhd->htu", query_two, keys_block, preferred_element_type=jnp.float32)
        * scale
    )
    return jnp.where(allowed[None], raw_scores, floor_score)


def probs_work(tile_scores, log_mass, allowed, values_block):
    prob = jnp.where(allowed[None], jnp.exp(tile_scores - log_mass[:, :, None]), 0.0)
    part_out = jnp.einsum(
        "htu,uhd->thd", prob.astype(jnp.bfloat16), values_block, preferred_element_type=jnp.float32
    )
    return (prob, part_out)


def grads_work(prob, query_two, out_grad, keys_block, values_block, delta, scale):
    grad_prob = jnp.einsum(
        "thd,uhd->htu", out_grad, values_block, preferred_element_type=jnp.float32
    )
    grad_score = (prob * (grad_prob - delta.T[:, :, None]) * scale).astype(jnp.bfloat16)
    query_grad = jnp.einsum(
        "htu,uhd->thd", grad_score, keys_block, preferred_element_type=jnp.float32
    )
    key_grad = jnp.einsum("htu,thd->uhd", grad_score, query_two, preferred_element_type=jnp.float32)
    value_grad = jnp.einsum(
        "htu,thd->uhd", prob.astype(jnp.bfloat16), out_grad, preferred_element_type=jnp.float32
    )
    return (query_grad, key_grad, value_grad)


def body(query_one, key_one, value_one, log_decay, query_two, key_two, out_grad, doc_ids):
    length, heads_here, width = query_one.shape
    shards = lax.axis_size("seq")
    token_position = lax.axis_index("seq")
    features = heads_here * lax.axis_size("head") * width
    q_float = query_one.astype(jnp.float32)
    k_float = key_one.astype(jnp.float32)
    v_float = value_one.astype(jnp.float32)
    cumulative = jnp.cumsum(log_decay, axis=1)
    carry_decay = jnp.exp(cumulative[:, -1])
    local_state, state_pull = jax.vjp(partial(shard_state, cumulative=cumulative), k_float, v_float)
    identity = (jnp.ones_like(carry_decay), jnp.zeros_like(local_state))
    incoming = prefix((carry_decay, local_state), "seq", chain_join, identity, False)[1]
    raw_out, output_pull = jax.vjp(
        partial(shard_output, cumulative=cumulative, incoming=incoming), q_float, k_float, v_float
    )
    square_sum = lax.psum(jnp.sum(raw_out * raw_out, axis=(1, 2)), "head")
    inverse = 1.0 / jnp.sqrt(square_sum / features + norm_epsilon)
    normed = raw_out * inverse[:, None, None]
    values_two = normed.astype(jnp.bfloat16)
    blocks_here = length // BLOCK
    scale = 1.0 / math.sqrt(width)
    offsets = jnp.arange(length, dtype=jnp.int32)
    query_doc = jnp.repeat(
        lax.dynamic_slice_in_dim(doc_ids, token_position * blocks_here, blocks_here), BLOCK
    )
    query_pos = token_position * length + offsets
    masks = []
    for distance in range(REACH + 1):
        source = (token_position - distance) % shards
        key_doc = jnp.repeat(
            lax.dynamic_slice_in_dim(doc_ids, source * blocks_here, blocks_here), BLOCK
        )
        key_pos = source * length + offsets
        masks.append(
            (key_pos[None, :] <= query_pos[:, None]) & (key_doc[None, :] == query_doc[:, None])
        )
    blocks = [(key_two, values_two)]
    current = (key_two, values_two)
    for distance in range(1, REACH + 1):
        current = from_behind((current[0], current[1]), "seq", 1)
        blocks.append(current)
    row_shape = (length, heads_here, width)
    peak_now = jnp.full((heads_here, length), floor_score, jnp.float32)
    mass_now = jnp.zeros((heads_here, length), jnp.float32)
    tile_list = []
    for distance in range(REACH + 1):
        allowed = masks[distance]
        tile_scores = scores_work(query_two, blocks[distance][0], allowed, scale)
        peak_next = jnp.maximum(peak_now, jnp.max(tile_scores, axis=2))
        fresh_mass = jnp.sum(
            jnp.where(allowed[None], jnp.exp(tile_scores - peak_next[:, :, None]), 0.0), axis=2
        )
        mass_now = mass_now * jnp.exp(peak_now - peak_next) + fresh_mass
        peak_now = peak_next
        tile_list.append(tile_scores)
    log_mass = peak_now + jnp.log(mass_now)
    attended = jnp.zeros(row_shape, jnp.float32)
    prob_list = []
    for distance in range(REACH + 1):
        allowed = masks[distance]
        prob, part_out = probs_work(tile_list[distance], log_mass, allowed, blocks[distance][1])
        attended = attended + part_out
        prob_list.append(prob)
    delta = jnp.sum(out_grad.astype(jnp.float32) * attended, axis=2)
    grad_query_two = jnp.zeros(row_shape, jnp.float32)
    carried = None
    for distance in range(REACH, -1, -1):
        keys_block, values_block = blocks[distance]
        query_grad, key_grad, value_grad = grads_work(
            prob_list[distance], query_two, out_grad, keys_block, values_block, delta, scale
        )
        grad_query_two = grad_query_two + query_grad
        if carried is None:
            carried = (key_grad, value_grad)
        else:
            moved = jax.tree.map(
                lambda part, own: part.astype(own.dtype),
                from_behind(for_sending(carried), "seq", -1),
                carried,
            )
            carried = (moved[0] + key_grad, moved[1] + value_grad)
    grad_key_two, grad_values_two = carried
    cross_sum = lax.psum(jnp.sum(raw_out * grad_values_two, axis=(1, 2)), "head")
    grad_raw = (
        inverse[:, None, None] * grad_values_two
        - raw_out * (inverse**3 * cross_sum / features)[:, None, None]
    )
    direct_state = jnp.einsum(
        "thd,the->hde",
        q_float * jnp.exp(cumulative).T[:, :, None],
        grad_raw,
        precision=exact_precision,
    )
    later_grad = prefix((carry_decay, direct_state), "seq", chain_join, identity, True)[1]
    grad_query_one, grad_key_out, grad_value_out = output_pull(grad_raw)
    grad_key_state, grad_value_state = state_pull(later_grad)
    return (
        grad_query_one,
        grad_key_out + grad_key_state,
        grad_value_out + grad_value_state,
        grad_query_two,
        grad_key_two,
    )


def solution(mesh):
    placed = (
        P("seq", "head", None),
        P("seq", "head", None),
        P("seq", "head", None),
        P("head", "seq"),
        P("seq", "head", None),
        P("seq", "head", None),
        P("seq", "head", None),
        P(),
    )
    return jax.shard_map(
        body,
        mesh=mesh,
        in_specs=placed,
        out_specs=(
            P("seq", "head", None),
            P("seq", "head", None),
            P("seq", "head", None),
            P("seq", "head", None),
            P("seq", "head", None),
        ),
        check_vma=False,
    )
```

profile of v0, /device:TPU:16, one launch (start us, length us, event | category | flops | bytes accessed | tf_op | source)
XLA Modules:
  0.0 903.4 jit_solution(13959338959294358134)
XLA Ops:
  16.6 23.7 %collective-permute-done = bf16[128,16,128]{2,0,1:T(8,128)(2,1)S(1)} collective-permute-done((bf16[128,16,128]{2,0,1:T(8,128)(2,1)S(1)}, bf16[128,16,128]{2,0,1:T(8,128)(2,1)S(1)}, u32[]{:S(2)}, u32[]{:S(2)}) %collective-permute-start) | collective-permute-done | bytes 524320 | tf_op jit(solution)/shard_map/ppermute | solution.py:38
  66.3 34.6 %collective-permute-done.2 = bf16[128,16,128]{2,0,1:T(8,128)(2,1)S(1)} collective-permute-done((bf16[128,16,128]{2,0,1:T(8,128)(2,1)S(1)}, bf16[128,16,128]{2,0,1:T(8,128)(2,1)S(1)}, u32[]{:S(2)}, u32[]{:S(2)}) %collective-permute-start.2) | collective-permute-done | bytes 524320 | tf_op jit(solution)/shard_map/ppermute | solution.py:38
  103.0 25.6 %collective-permute-done.3 = bf16[128,16,128]{2,0,1:T(8,128)(2,1)S(1)} collective-permute-done((bf16[128,16,128]{2,0,1:T(8,128)(2,1)S(1)}, bf16[128,16,128]{2,0,1:T(8,128)(2,1)S(1)}, u32[]{:S(2)}, u32[]{:S(2)}) %collective-permute-start.3) | collective-permute-done | bytes 524320 | tf_op jit(solution)/shard_map/ppermute | solution.py:38
  134.3 13.0 %collective-permute-done.4 = bf16[128,16,128]{2,0,1:T(8,128)(2,1)S(1)} collective-permute-done((bf16[128,16,128]{2,0,1:T(8,128)(2,1)S(1)}, bf16[128,16,128]{2,0,1:T(8,128)(2,1)S(1)}, u32[]{:S(2)}, u32[]{:S(2)}) %collective-permute-start.4) | collective-permute-done | bytes 524320 | tf_op jit(solution)/shard_map/ppermute | solution.py:38
  152.9 33.6 %collective-permute-done.5 = bf16[128,16,128]{2,0,1:T(8,128)(2,1)S(1)} collective-permute-done((bf16[128,16,128]{2,0,1:T(8,128)(2,1)S(1)}, bf16[128,16,128]{2,0,1:T(8,128)(2,1)S(1)}, u32[]{:S(2)}, u32[]{:S(2)}) %collective-permute-start.5) | collective-permute-done | bytes 524320 | tf_op jit(solution)/shard_map/ppermute | solution.py:38
  192.1 33.8 %collective-permute-done.6 = bf16[128,16,128]{2,0,1:T(8,128)(2,1)S(1)} collective-permute-done((bf16[128,16,128]{2,0,1:T(8,128)(2,1)S(1)}, bf16[128,16,128]{2,0,1:T(8,128)(2,1)S(1)}, u32[]{:S(2)}, u32[]{:S(2)}) %collective-permute-start.6) | collective-permute-done | bytes 524320 | tf_op jit(solution)/shard_map/ppermute | solution.py:38
  229.1 20.7 %collective-permute-done.7 = bf16[128,16,128]{2,0,1:T(8,128)(2,1)S(1)} collective-permute-done((bf16[128,16,128]{2,0,1:T(8,128)(2,1)S(1)}, bf16[128,16,128]{2,0,1:T(8,128)(2,1)S(1)}, u32[]{:S(2)}, u32[]{:S(2)}) %collective-permute-start.7) | collective-permute-done | bytes 524320 | tf_op jit(solution)/shard_map/ppermute | solution.py:38
  259.8 25.3 %collective-permute-done.8 = bf16[128,16,128]{0,2,1:T(8,128)(2,1)S(1)} collective-permute-done((bf16[128,16,128]{0,2,1:T(8,128)(2,1)S(1)}, bf16[128,16,128]{0,2,1:T(8,128)(2,1)S(1)}, u32[]{:S(2)}, u32[]{:S(2)}) %collective-permute-start.8) | collective-permute-done | bytes 524320 | tf_op jit(solution)/shard_map/ppermute | solution.py:38
  307.1 19.3 %collective-permute-done.10 = bf16[128,16,128]{0,2,1:T(8,128)(2,1)S(1)} collective-permute-done((bf16[128,16,128]{0,2,1:T(8,128)(2,1)S(1)}, bf16[128,16,128]{0,2,1:T(8,128)(2,1)S(1)}, u32[]{:S(2)}, u32[]{:S(2)}) %collective-permute-start.10) | collective-permute-done | bytes 524320 | tf_op jit(solution)/shard_map/ppermute | solution.py:38
  332.1 40.0 %all-reduce = f32[256]{0:T(256)S(1)} all-reduce(f32[256]{0:T(256)S(1)} %dynamic-update-slice), channel_id=2, replica_groups=mesh['seq'=16,'head'=2] {'seq'}, use_global_device_ids=true, to_apply=%add | all-reduce | flops 256 | bytes 2048
  432.9 22.5 %while.28 = (s32[]{:T(128)}, f32[16,128,128]{2,1,0:T(8,128)S(1)}, s32[]{:T(128)}, f32[16,16]{1,0:T(8,128)S(1)}, f32[16,16,128,128]{3,2,1,0:T(8,128)}, /*index=5*/s32[]{:T(128)}, s32[]{:T(128)}) while((s32[]{:T(128)}, f32[16,128,128]{2,1,0:T(8,128)S(1)}, s32[]{:T(128)}, f32[16,16]{1,0:T(8,128)S(1)}, f32[16,16,128,128]{3,2,1,0:T(8,128)}, ...), condition=%wide.region_2.3_spmd.clone, body=%wide.region_1.2_spmd.clone.sunk | while | flops 1048580 | bytes 3146025 | solution.py:32
  472.3 24.4 %collective-permute-done.16 = bf16[128,16,128]{0,2,1:T(8,128)(2,1)} collective-permute-done((bf16[128,16,128]{0,2,1:T(8,128)(2,1)}, bf16[128,16,128]{0,2,1:T(8,128)(2,1)}, u32[]{:S(2)}, u32[]{:S(2)}) %collective-permute-start.16) | collective-permute-done | bytes 524320 | tf_op jit(solution)/shard_map/ppermute | solution.py:38
  501.3 20.8 %collective-permute-done.17 = bf16[128,16,128]{0,2,1:T(8,128)(2,1)} collective-permute-done((bf16[128,16,128]{0,2,1:T(8,128)(2,1)}, bf16[128,16,128]{0,2,1:T(8,128)(2,1)}, u32[]{:S(2)}, u32[]{:S(2)}) %collective-permute-start.17) | collective-permute-done | bytes 524320 | tf_op jit(solution)/shard_map/ppermute | solution.py:38
  531.0 28.1 %collective-permute-done.18 = bf16[128,16,128]{0,2,1:T(8,128)(2,1)S(1)} collective-permute-done((bf16[128,16,128]{0,2,1:T(8,128)(2,1)}, bf16[128,16,128]{0,2,1:T(8,128)(2,1)S(1)}, u32[]{:S(2)}, u32[]{:S(2)}) %collective-permute-start.18) | collective-permute-done | bytes 524320 | tf_op jit(solution)/shard_map/ppermute | solution.py:38
  565.6 23.5 %collective-permute-done.19 = bf16[128,16,128]{0,2,1:T(8,128)(2,1)S(1)} collective-permute-done((bf16[128,16,128]{0,2,1:T(8,128)(2,1)S(1)}, bf16[128,16,128]{0,2,1:T(8,128)(2,1)S(1)}, u32[]{:S(2)}, u32[]{:S(2)}) %collective-permute-start.19) | collective-permute-done | bytes 524320 | tf_op jit(solution)/shard_map/ppermute | solution.py:38
  594.7 11.1 %collective-permute-done.20 = bf16[128,16,128]{0,2,1:T(8,128)(2,1)S(1)} collective-permute-done((bf16[128,16,128]{0,2,1:T(8,128)(2,1)S(1)}, bf16[128,16,128]{0,2,1:T(8,128)(2,1)S(1)}, u32[]{:S(2)}, u32[]{:S(2)}) %collective-permute-start.20) | collective-permute-done | bytes 524320 | tf_op jit(solution)/shard_map/ppermute | solution.py:38
  609.9 35.6 %collective-permute-done.21 = bf16[128,16,128]{0,2,1:T(8,128)(2,1)S(1)} collective-permute-done((bf16[128,16,128]{0,2,1:T(8,128)(2,1)S(1)}, bf16[128,16,128]{0,2,1:T(8,128)(2,1)S(1)}, u32[]{:S(2)}, u32[]{:S(2)}) %collective-permute-start.21) | collective-permute-done | bytes 524320 | tf_op jit(solution)/shard_map/ppermute | solution.py:38
  648.8 36.3 %collective-permute-done.22 = bf16[128,16,128]{0,2,1:T(8,128)(2,1)S(1)} collective-permute-done((bf16[128,16,128]{0,2,1:T(8,128)(2,1)S(1)}, bf16[128,16,128]{0,2,1:T(8,128)(2,1)S(1)}, u32[]{:S(2)}, u32[]{:S(2)}) %collective-permute-start.22) | collective-permute-done | bytes 524320 | tf_op jit(solution)/shard_map/ppermute | solution.py:38
  688.1 13.5 %collective-permute-done.23 = bf16[128,16,128]{0,2,1:T(8,128)(2,1)S(1)} collective-permute-done((bf16[128,16,128]{0,2,1:T(8,128)(2,1)S(1)}, bf16[128,16,128]{0,2,1:T(8,128)(2,1)S(1)}, u32[]{:S(2)}, u32[]{:S(2)}) %collective-permute-start.23) | collective-permute-done | bytes 524320 | tf_op jit(solution)/shard_map/ppermute | solution.py:38
  715.9 25.4 %collective-permute-done.24 = bf16[128,16,128]{2,0,1:T(8,128)(2,1)S(1)} collective-permute-done((bf16[128,16,128]{2,0,1:T(8,128)(2,1)S(1)}, bf16[128,16,128]{2,0,1:T(8,128)(2,1)S(1)}, u32[]{:S(2)}, u32[]{:S(2)}) %collective-permute-start.24) | collective-permute-done | bytes 524320 | tf_op jit(solution)/shard_map/ppermute | solution.py:38
  766.7 11.2 %collective-permute-done.26 = bf16[128,16,128]{2,0,1:T(8,128)(2,1)S(1)} collective-permute-done((bf16[128,16,128]{2,0,1:T(8,128)(2,1)S(1)}, bf16[128,16,128]{2,0,1:T(8,128)(2,1)S(1)}, u32[]{:S(2)}, u32[]{:S(2)}) %collective-permute-start.26) | collective-permute-done | bytes 524320 | tf_op jit(solution)/shard_map/ppermute | solution.py:38
  780.5 12.1 %collective-permute-done.27 = bf16[128,16,128]{2,0,1:T(8,128)(2,1)S(1)} collective-permute-done((bf16[128,16,128]{2,0,1:T(8,128)(2,1)S(1)}, bf16[128,16,128]{2,0,1:T(8,128)(2,1)S(1)}, u32[]{:S(2)}, u32[]{:S(2)}) %collective-permute-start.27) | collective-permute-done | bytes 524320 | tf_op jit(solution)/shard_map/ppermute | solution.py:38
  852.0 11.7 %rev.7 = f32[16,16,128,128]{3,2,1,0:T(8,128)} reverse(f32[16,16,128,128]{3,2,1,0:T(8,128)} %bitcast.250), dimensions={0} | reverse | bytes 33554432 | tf_op jit(solution)/shard_map/rev | solution.py:22
  863.7 22.5 %while.29 = (s32[]{:T(128)}, f32[16,128,128]{2,1,0:T(8,128)S(1)}, s32[]{:T(128)}, f32[16,16]{1,0:T(8,128)S(1)}, f32[16,16,128,128]{3,2,1,0:T(8,128)}, /*index=5*/s32[]{:T(128)}, s32[]{:T(128)}) while((s32[]{:T(128)}, f32[16,128,128]{2,1,0:T(8,128)S(1)}, s32[]{:T(128)}, f32[16,16]{1,0:T(8,128)S(1)}, ...), condition=%wide.region_26.27_spmd.clone, body=%wide.region_25.26_spmd.clone.sunk | while | flops 1048580 | bytes 3146025 | solution.py:32
  (327 shorter events, 351.8 us)
Async XLA Ops:
  7.2 425.7 %all-gather.6.cloned.1.call-start = ((), (), s32[]{:S(2)}) async-start(), calls=%async_computation | async-start | bytes 17825792 | tf_op jit(solution)/shard_map/all_gather | solution.py:20
  12.0 840.0 %all-gather.8.cloned.1.call-start = ((), (), s32[]{:S(2)}) async-start(), calls=%async_computation.1 | async-start | bytes 17825792 | tf_op jit(solution)/shard_map/all_gather | solution.py:20
  13.2 27.2 %collective-permute-start = (bf16[128,16,128]{2,0,1:T(8,128)(2,1)S(1)}, bf16[128,16,128]{2,0,1:T(8,128)(2,1)S(1)}, u32[]{:S(2)}, u32[]{:S(2)}) collective-permute-start(bf16[128,16,128]{2,0,1:T(8,128)(2,1)S(1)} %copy.253), channel_id=1, source_target_pairs={{0,2},{2,4},{4,6},{6,8},{8,10},{10,12},{12,14},{14,16},{16,18},{18... | collective-permute-start | bytes 1572872 | tf_op jit(solution)/shard_map/ppermute | solution.py:38
  40.4 23.9 %collective-permute-start.1 = (bf16[128,16,128]{2,0,1:T(8,128)(2,1)S(1)}, bf16[128,16,128]{2,0,1:T(8,128)(2,1)S(1)}, u32[]{:S(2)}, u32[]{:S(2)}) collective-permute-start(bf16[128,16,128]{2,0,1:T(8,128)(2,1)S(1)} %collective-permute-done), channel_id=1, source_target_pairs={{0,2},{2,4},{4,6},{6,8},{8,10},{10,12},{12,14},{14,16},{16,18},{18... | collective-permute-start | bytes 1572872 | tf_op jit(solution)/shard_map/ppermute | solution.py:38
  64.3 36.6 %collective-permute-start.2 = (bf16[128,16,128]{2,0,1:T(8,128)(2,1)S(1)}, bf16[128,16,128]{2,0,1:T(8,128)(2,1)S(1)}, u32[]{:S(2)}, u32[]{:S(2)}) collective-permute-start(bf16[128,16,128]{2,0,1:T(8,128)(2,1)S(1)} %collective-permute-done.1), channel_id=1, source_target_pairs={{0,2},{2,4},{4,6},{6,8},{8,10},{10,12},{12,14},{14,16},{16,18},{18... | collective-permute-start | bytes 1572872 | tf_op jit(solution)/shard_map/ppermute | solution.py:38
  100.8 27.8 %collective-permute-start.3 = (bf16[128,16,128]{2,0,1:T(8,128)(2,1)S(1)}, bf16[128,16,128]{2,0,1:T(8,128)(2,1)S(1)}, u32[]{:S(2)}, u32[]{:S(2)}) collective-permute-start(bf16[128,16,128]{2,0,1:T(8,128)(2,1)S(1)} %collective-permute-done.2), channel_id=1, source_target_pairs={{0,2},{2,4},{4,6},{6,8},{8,10},{10,12},{12,14},{14,16},{16,18},{18... | collective-permute-start | bytes 1572872 | tf_op jit(solution)/shard_map/ppermute | solution.py:38
  128.6 18.7 %collective-permute-start.4 = (bf16[128,16,128]{2,0,1:T(8,128)(2,1)S(1)}, bf16[128,16,128]{2,0,1:T(8,128)(2,1)S(1)}, u32[]{:S(2)}, u32[]{:S(2)}) collective-permute-start(bf16[128,16,128]{2,0,1:T(8,128)(2,1)S(1)} %collective-permute-done.3), channel_id=1, source_target_pairs={{0,2},{2,4},{4,6},{6,8},{8,10},{10,12},{12,14},{14,16},{16,18},{18... | collective-permute-start | bytes 1572872 | tf_op jit(solution)/shard_map/ppermute | solution.py:38
  147.3 39.2 %collective-permute-start.5 = (bf16[128,16,128]{2,0,1:T(8,128)(2,1)S(1)}, bf16[128,16,128]{2,0,1:T(8,128)(2,1)S(1)}, u32[]{:S(2)}, u32[]{:S(2)}) collective-permute-start(bf16[128,16,128]{2,0,1:T(8,128)(2,1)S(1)} %collective-permute-done.4), channel_id=1, source_target_pairs={{0,2},{2,4},{4,6},{6,8},{8,10},{10,12},{12,14},{14,16},{16,18},{18... | collective-permute-start | bytes 1572872 | tf_op jit(solution)/shard_map/ppermute | solution.py:38
  186.5 39.4 %collective-permute-start.6 = (bf16[128,16,128]{2,0,1:T(8,128)(2,1)S(1)}, bf16[128,16,128]{2,0,1:T(8,128)(2,1)S(1)}, u32[]{:S(2)}, u32[]{:S(2)}) collective-permute-start(bf16[128,16,128]{2,0,1:T(8,128)(2,1)S(1)} %collective-permute-done.5), channel_id=1, source_target_pairs={{0,2},{2,4},{4,6},{6,8},{8,10},{10,12},{12,14},{14,16},{16,18},{18... | collective-permute-start | bytes 1572872 | tf_op jit(solution)/shard_map/ppermute | solution.py:38
  225.9 23.9 %collective-permute-start.7 = (bf16[128,16,128]{2,0,1:T(8,128)(2,1)S(1)}, bf16[128,16,128]{2,0,1:T(8,128)(2,1)S(1)}, u32[]{:S(2)}, u32[]{:S(2)}) collective-permute-start(bf16[128,16,128]{2,0,1:T(8,128)(2,1)S(1)} %collective-permute-done.6), channel_id=1, source_target_pairs={{0,2},{2,4},{4,6},{6,8},{8,10},{10,12},{12,14},{14,16},{16,18},{18... | collective-permute-start | bytes 1572872 | tf_op jit(solution)/shard_map/ppermute | solution.py:38
  257.3 27.8 %collective-permute-start.8 = (bf16[128,16,128]{0,2,1:T(8,128)(2,1)S(1)}, bf16[128,16,128]{0,2,1:T(8,128)(2,1)S(1)}, u32[]{:S(2)}, u32[]{:S(2)}) collective-permute-start(bf16[128,16,128]{0,2,1:T(8,128)(2,1)S(1)} %fusion.64), channel_id=1, source_target_pairs={{2,0},{4,2},{6,4},{8,6},{10,8},{12,10},{14,12},{16,14},{18,16},{20... | collective-permute-start | bytes 1572872 | tf_op jit(solution)/shard_map/ppermute | solution.py:38
  300.2 26.2 %collective-permute-start.10 = (bf16[128,16,128]{0,2,1:T(8,128)(2,1)S(1)}, bf16[128,16,128]{0,2,1:T(8,128)(2,1)S(1)}, u32[]{:S(2)}, u32[]{:S(2)}) collective-permute-start(bf16[128,16,128]{0,2,1:T(8,128)(2,1)S(1)} %add_convert_fusion.12), channel_id=1, source_target_pairs={{2,0},{4,2},{6,4},{8,6},{10,8},{12,10},{14,12},{16,14},{18,16},{20... | collective-permute-start | bytes 1572872 | tf_op jit(solution)/shard_map/ppermute | solution.py:38
  327.3 46.9 %collective-permute-start.11 = (bf16[128,16,128]{0,2,1:T(8,128)(2,1)}, bf16[128,16,128]{0,2,1:T(8,128)(2,1)}, u32[]{:S(2)}, u32[]{:S(2)}) collective-permute-start(bf16[128,16,128]{0,2,1:T(8,128)(2,1)} %add_convert_fusion.11), channel_id=1, source_target_pairs={{2,0},{4,2},{6,4},{8,6},{10,8},{12,10},{14,12},{16,14},{18,16},{20... | collective-permute-start | bytes 1572872 | tf_op jit(solution)/shard_map/ppermute | solution.py:38
  407.3 18.4 %collective-permute-start.14 = (bf16[128,16,128]{0,2,1:T(8,128)(2,1)S(1)}, bf16[128,16,128]{0,2,1:T(8,128)(2,1)S(1)}, u32[]{:S(2)}, u32[]{:S(2)}) collective-permute-start(bf16[128,16,128]{0,2,1:T(8,128)(2,1)S(1)} %add_convert_fusion.8), channel_id=1, source_target_pairs={{2,0},{4,2},{6,4},{8,6},{10,8},{12,10},{14,12},{16,14},{18,16},{20... | collective-permute-start | bytes 1572872 | tf_op jit(solution)/shard_map/ppermute | solution.py:38
  426.7 28.7 %collective-permute-start.15 = (bf16[128,16,128]{0,2,1:T(8,128)(2,1)}, bf16[128,16,128]{0,2,1:T(8,128)(2,1)}, u32[]{:S(2)}, u32[]{:S(2)}) collective-permute-start(bf16[128,16,128]{0,2,1:T(8,128)(2,1)} %add_convert_fusion.7), channel_id=1, source_target_pairs={{2,0},{4,2},{6,4},{8,6},{10,8},{12,10},{14,12},{16,14},{18,16},{20... | collective-permute-start | bytes 1572872 | tf_op jit(solution)/shard_map/ppermute | solution.py:38
  470.4 26.3 %collective-permute-start.16 = (bf16[128,16,128]{0,2,1:T(8,128)(2,1)}, bf16[128,16,128]{0,2,1:T(8,128)(2,1)}, u32[]{:S(2)}, u32[]{:S(2)}) collective-permute-start(bf16[128,16,128]{0,2,1:T(8,128)(2,1)} %get-tuple-element.280), channel_id=1, source_target_pairs={{0,2},{2,4},{4,6},{6,8},{8,10},{10,12},{12,14},{14,16},{16,18},{18... | collective-permute-start | bytes 1572872 | tf_op jit(solution)/shard_map/ppermute | solution.py:38
  496.7 25.4 %collective-permute-start.17 = (bf16[128,16,128]{0,2,1:T(8,128)(2,1)}, bf16[128,16,128]{0,2,1:T(8,128)(2,1)}, u32[]{:S(2)}, u32[]{:S(2)}) collective-permute-start(bf16[128,16,128]{0,2,1:T(8,128)(2,1)} %collective-permute-done.16), channel_id=1, source_target_pairs={{0,2},{2,4},{4,6},{6,8},{8,10},{10,12},{12,14},{14,16},{16,18},{18... | collective-permute-start | bytes 1572872 | tf_op jit(solution)/shard_map/ppermute | solution.py:38
  522.1 37.0 %collective-permute-start.18 = (bf16[128,16,128]{0,2,1:T(8,128)(2,1)}, bf16[128,16,128]{0,2,1:T(8,128)(2,1)S(1)}, u32[]{:S(2)}, u32[]{:S(2)}) collective-permute-start(bf16[128,16,128]{0,2,1:T(8,128)(2,1)} %collective-permute-done.17), channel_id=1, source_target_pairs={{0,2},{2,4},{4,6},{6,8},{8,10},{10,12},{12,14},{14,16},{16,18},{18... | collective-permute-start | bytes 1572872 | tf_op jit(solution)/shard_map/ppermute | solution.py:38
  559.0 30.1 %collective-permute-start.19 = (bf16[128,16,128]{0,2,1:T(8,128)(2,1)S(1)}, bf16[128,16,128]{0,2,1:T(8,128)(2,1)S(1)}, u32[]{:S(2)}, u32[]{:S(2)}) collective-permute-start(bf16[128,16,128]{0,2,1:T(8,128)(2,1)S(1)} %collective-permute-done.18), channel_id=1, source_target_pairs={{0,2},{2,4},{4,6},{6,8},{8,10},{10,12},{12,14},{14,16},{16,18},{18... | collective-permute-start | bytes 1572872 | tf_op jit(solution)/shard_map/ppermute | solution.py:38
  605.8 39.7 %collective-permute-start.21 = (bf16[128,16,128]{0,2,1:T(8,128)(2,1)S(1)}, bf16[128,16,128]{0,2,1:T(8,128)(2,1)S(1)}, u32[]{:S(2)}, u32[]{:S(2)}) collective-permute-start(bf16[128,16,128]{0,2,1:T(8,128)(2,1)S(1)} %collective-permute-done.20), channel_id=1, source_target_pairs={{0,2},{2,4},{4,6},{6,8},{8,10},{10,12},{12,14},{14,16},{16,18},{18... | collective-permute-start | bytes 1572872 | tf_op jit(solution)/shard_map/ppermute | solution.py:38
  645.5 39.5 %collective-permute-start.22 = (bf16[128,16,128]{0,2,1:T(8,128)(2,1)S(1)}, bf16[128,16,128]{0,2,1:T(8,128)(2,1)S(1)}, u32[]{:S(2)}, u32[]{:S(2)}) collective-permute-start(bf16[128,16,128]{0,2,1:T(8,128)(2,1)S(1)} %collective-permute-done.21), channel_id=1, source_target_pairs={{0,2},{2,4},{4,6},{6,8},{8,10},{10,12},{12,14},{14,16},{16,18},{18... | collective-permute-start | bytes 1572872 | tf_op jit(solution)/shard_map/ppermute | solution.py:38
  703.5 37.8 %collective-permute-start.24 = (bf16[128,16,128]{2,0,1:T(8,128)(2,1)S(1)}, bf16[128,16,128]{2,0,1:T(8,128)(2,1)S(1)}, u32[]{:S(2)}, u32[]{:S(2)}) collective-permute-start(bf16[128,16,128]{2,0,1:T(8,128)(2,1)S(1)} %fusion.65), channel_id=1, source_target_pairs={{2,0},{4,2},{6,4},{8,6},{10,8},{12,10},{14,12},{16,14},{18,16},{20... | collective-permute-start | bytes 1572872 | tf_op jit(solution)/shard_map/ppermute | solution.py:38
  741.7 17.4 %collective-permute-start.25 = (bf16[128,16,128]{2,0,1:T(8,128)(2,1)S(1)}, bf16[128,16,128]{2,0,1:T(8,128)(2,1)S(1)}, u32[]{:S(2)}, u32[]{:S(2)}) collective-permute-start(bf16[128,16,128]{2,0,1:T(8,128)(2,1)S(1)} %add_convert_fusion.6), channel_id=1, source_target_pairs={{2,0},{4,2},{6,4},{8,6},{10,8},{12,10},{14,12},{16,14},{18,16},{20... | collective-permute-start | bytes 1572872 | tf_op jit(solution)/shard_map/ppermute | solution.py:38
  759.2 18.6 %collective-permute-start.26 = (bf16[128,16,128]{2,0,1:T(8,128)(2,1)S(1)}, bf16[128,16,128]{2,0,1:T(8,128)(2,1)S(1)}, u32[]{:S(2)}, u32[]{:S(2)}) collective-permute-start(bf16[128,16,128]{2,0,1:T(8,128)(2,1)S(1)} %add_convert_fusion.5), channel_id=1, source_target_pairs={{2,0},{4,2},{6,4},{8,6},{10,8},{12,10},{14,12},{16,14},{18,16},{20... | collective-permute-start | bytes 1572872 | tf_op jit(solution)/shard_map/ppermute | solution.py:38
  (59 other events, 5132.2 us)
Sparse Core Ops, SparseCore 0:
  12.1 271.6 all-gather.5
  470.5 272.8 all-gather.7
where the time goes:
time: 920 us; the launch traced here: 903 us
  waiting for transfers between devices  556 us (60%)
  starting transfers between devices  108 us (12%)
  matrix products  81.9 us (9%)
  other arithmetic  58.1 us (6%)
  blocking collectives  42.6 us (5%)
  local copies, waits for them, and re-layouts  27.6 us (3%)
  between operations  27.6 us (3%)
    ppermute x32, waiting for transfers between devices, from_behind(): return lax.ppermute(block, axis, route)  556 us
    ppermute x32, starting transfers between devices, from_behind(): return lax.ppermute(block, axis, route)  108 us
    select_n x30, other arithmetic, hop(): jnp.where(position < mine, new, old)  43.7 us
    unnamed x1, blocking collectives  40 us
  transfers between devices with their start and end apart: 34, of which 30 were waited for; matrix products, arithmetic and copies ran while one was open for 12% of the time, Pallas kernels for 0%

commit v1 on v0

--- a/solution.py
+++ b/solution.py
@@ -4,6 +4,8 @@
 import jax
 import jax.numpy as jnp
 from jax import lax
+from jax.experimental import pallas as pl
+from jax.experimental.pallas import tpu as pltpu
 from jax.sharding import PartitionSpec as P
 
 BLOCK = 128
@@ -105,7 +107,7 @@
     return (query_grad, key_grad, value_grad)
 
 
-def body(query_one, key_one, value_one, log_decay, query_two, key_two, out_grad, doc_ids):
+def ring_body(query_one, key_one, value_one, log_decay, query_two, key_two, out_grad, doc_ids):
     length, heads_here, width = query_one.shape
     shards = lax.axis_size("seq")
     token_position = lax.axis_index("seq")
@@ -211,6 +213,277 @@
     )
 
 
+f32, bf16 = (jnp.float32, jnp.bfloat16)
+LOG2E = math.log2(math.e)
+PART_ROWS = 16
+
+
+def dot(a, b):
+    return lax.dot_general(a, b, (((1,), (0,)), ((), ())), preferred_element_type=f32)
+
+
+def dot_nt(a, b):
+    return lax.dot_general(a, b, (((1,), (1,)), ((), ())), preferred_element_type=f32)
+
+
+def dot_tn(a, b):
+    return lax.dot_general(a, b, (((0,), (0,)), ((), ())), preferred_element_type=f32)
+
+
+def two_parts(value):
+    high = value.astype(bf16)
+    return high, (value - high.astype(f32)).astype(bf16)
+
+
+def row_sums(value):
+    ones = jnp.ones((PART_ROWS, value.shape[1]), bf16)
+    high, low = two_parts(value)
+    return dot_nt(ones, high) + dot_nt(ones, low)
+
+
+def chunk_decays(parts):
+    lower = lower_mask(BLOCK)
+    log_row = jnp.sum(parts.astype(f32), axis=0, keepdims=True)
+    column = jnp.sum(jnp.where(lower, log_row, 0.0), axis=1, keepdims=True)
+    upper = lax.broadcasted_iota(jnp.int32, (BLOCK, BLOCK), 0) <= lax.broadcasted_iota(
+        jnp.int32, (BLOCK, BLOCK), 1
+    )
+    row = jnp.sum(dot(parts, jnp.where(upper, 1.0, 0.0).astype(bf16)), axis=0, keepdims=True)
+    last = column[BLOCK - 1 : BLOCK, :]
+    weights = jnp.exp(jnp.where(lower, column - row, floor_score))
+    return weights, jnp.exp(column), jnp.exp(last - column), jnp.exp(last)
+
+
+def linear_forward(first_ref, raw_ref, state_ref, sums_ref):
+    chunks = first_ref.shape[0]
+    width = first_ref.shape[2]
+    rows = lax.broadcasted_iota(jnp.int32, (chunks, BLOCK), 0)
+    state = jnp.zeros((width, width), f32)
+    sums = jnp.zeros((chunks, BLOCK), f32)
+    for c in range(chunks):
+        q = first_ref[c, 0:BLOCK, :]
+        k = first_ref[c, BLOCK : 2 * BLOCK, :]
+        v = first_ref[c, 2 * BLOCK : 3 * BLOCK, :]
+        weights, grow, tail, whole = chunk_decays(first_ref[c, 3 * BLOCK :, :])
+        prob = (dot_nt(q, k) * weights).astype(bf16)
+        state_low = state.astype(bf16)
+        raw = dot(prob, v) + grow * dot(q, state_low)
+        state_ref[c] = state_low
+        state = whole * state + dot_tn(k, (v.astype(f32) * tail).astype(bf16))
+        raw_ref[c * BLOCK : (c + 1) * BLOCK, :] = raw
+        sums = sums + jnp.where(rows == c, row_sums(raw * raw)[0:1, :], 0.0)
+    high, low = two_parts(sums)
+    sums_ref[0:chunks, :] = high
+    sums_ref[chunks : 2 * chunks, :] = low
+
+
+def softmax_both(
+    features, starts_ref, second_ref, raw_ref, sums_ref, out_ref, value_grad_ref,
+    key_s, key_t_s, value_s, value_t_s, key_grad_s,
+):
+    chunks = second_ref.shape[0]
+    width = second_ref.shape[2]
+    scale = 1.0 / math.sqrt(width)
+    inverse = 1.0 / jnp.sqrt(sums_ref[...] / features + norm_epsilon)
+    columns = inverse.T
+    for c in range(chunks):
+        here = slice(c * BLOCK, (c + 1) * BLOCK)
+        k = second_ref[c, BLOCK : 2 * BLOCK, :]
+        v = (raw_ref[here, :] * columns[:, c : c + 1]).astype(bf16)
+        key_s[here, :] = k
+        key_t_s[:, here] = k.T
+        value_s[here, :] = v
+        value_t_s[:, here] = v.T
+    key_grad_s[...] = jnp.zeros_like(key_grad_s)
+    value_grad_ref[...] = jnp.zeros_like(value_grad_ref)
+
+    def window(t, first, blocks):
+        length = blocks * BLOCK
+        begin = pl.multiple_of(jnp.maximum(t - (blocks - 1), 0) * BLOCK, BLOCK)
+        rows = pl.ds(begin, length)
+        q = second_ref[t, 0:BLOCK, :]
+        g = second_ref[t, 2 * BLOCK : 3 * BLOCK, :]
+        q_t, g_t = (q.T, g.T)
+        scores = dot(key_s[rows, :], q_t) * (scale * LOG2E)
+        u_pos = begin + lax.broadcasted_iota(jnp.int32, (length, BLOCK), 0)
+        t_pos = t * BLOCK + lax.broadcasted_iota(jnp.int32, (length, BLOCK), 1)
+        allowed = (u_pos <= t_pos) & (u_pos >= first * BLOCK)
+        scores = jnp.where(allowed, scores, floor_score)
+        peak = jnp.max(scores, axis=0, keepdims=True)
+        mass = jnp.exp2(scores - peak)
+        prob = mass * (1.0 / jnp.sum(mass, axis=0, keepdims=True))
+        prob_low = prob.astype(bf16)
+        attended = dot(value_t_s[:, rows], prob_low)
+        delta = jnp.sum(g_t.astype(f32) * attended, axis=0, keepdims=True)
+        grad_prob = dot(value_s[rows, :], g_t)
+        grad_score = (prob * (grad_prob - delta) * scale).astype(bf16)
+        out_ref[t, 0:BLOCK, :] = dot(key_t_s[:, rows], grad_score).T.astype(bf16)
+        key_grad_s[rows, :] += dot(grad_score, q)
+        value_grad_ref[rows, :] += dot(prob_low, g)
+
+    def step(t, carry):
+        first = starts_ref[t]
+        need = t - first + 1
+        sizes = [n for n in (1, 2, 4, 8) if n <= chunks]
+        least = 0
+        for n in sizes:
+            pl.when((need > least) & (need <= n))(partial(window, t, first, n))
+            least = n
+        return carry
+
+    lax.fori_loop(0, chunks, step, 0)
+    rows = lax.broadcasted_iota(jnp.int32, (chunks, BLOCK), 0)
+    cross = jnp.zeros((chunks, BLOCK), f32)
+    for c in range(chunks):
+        here = slice(c * BLOCK, (c + 1) * BLOCK)
+        out_ref[c, BLOCK : 2 * BLOCK, :] = key_grad_s[here, :].astype(bf16)
+        part = row_sums(raw_ref[here, :] * value_grad_ref[here, :])[0:1, :]
+        cross = cross + jnp.where(rows == c, part, 0.0)
+    high, low = two_parts(cross)
+    for c in range(chunks):
+        out_ref[c, 2 * BLOCK : 2 * BLOCK + chunks, :] = high
+        out_ref[c, 2 * BLOCK + chunks :, :] = low
+
+
+def linear_backward(
+    features, first_ref, raw_ref, state_ref, sums_ref, cross_ref, value_grad_ref, out_ref
+):
+    chunks = first_ref.shape[0]
+    width = first_ref.shape[2]
+    inverse = 1.0 / jnp.sqrt(sums_ref[...] / features + norm_epsilon)
+    inverse_columns = inverse.T
+    cross_columns = (inverse * inverse * inverse * cross_ref[...] / features).T
+    state_grad = jnp.zeros((width, width), f32)
+    for c in range(chunks - 1, -1, -1):
+        here = slice(c * BLOCK, (c + 1) * BLOCK)
+        q = first_ref[c, 0:BLOCK, :]
+        k = first_ref[c, BLOCK : 2 * BLOCK, :]
+        v = first_ref[c, 2 * BLOCK : 3 * BLOCK, :]
+        weights, grow, tail, whole = chunk_decays(first_ref[c, 3 * BLOCK :, :])
+        grad = (
+            inverse_columns[:, c : c + 1] * value_grad_ref[here, :]
+            - raw_ref[here, :] * cross_columns[:, c : c + 1]
+        )
+        grad_low = grad.astype(bf16)
+        grad_grown = (grad * grow).astype(bf16)
+        prob = (dot_nt(q, k) * weights).astype(bf16)
+        grad_score = (dot_nt(grad_low, v) * weights).astype(bf16)
+        state_low = state_grad.astype(bf16)
+        query_grad = dot(grad_score, k) + grow * dot_nt(grad_low, state_ref[c])
+        key_grad = dot_tn(grad_score, q) + tail * dot_nt(v, state_low)
+        value_grad = dot_tn(prob, grad_low) + tail * dot(k, state_low)
+        state_grad = whole * state_grad + dot_tn(q, grad_grown)
+        out_ref[c, 0:BLOCK, :] = query_grad.astype(bf16)
+        out_ref[c, BLOCK : 2 * BLOCK, :] = key_grad.astype(bf16)
+        out_ref[c, 2 * BLOCK : 3 * BLOCK, :] = value_grad.astype(bf16)
+
+
+def call(kernel, outs, scratch, *operands, prefetch=0):
+    vmem = pl.BlockSpec(memory_space=pltpu.VMEM)
+    smem = pl.BlockSpec(memory_space=pltpu.SMEM)
+    return pl.pallas_call(
+        kernel,
+        out_shape=[jax.ShapeDtypeStruct(shape, kind) for shape, kind in outs],
+        in_specs=[smem] * prefetch + [vmem] * (len(operands) - prefetch),
+        out_specs=[vmem] * len(outs),
+        scratch_shapes=[pltpu.VMEM(shape, kind) for shape, kind in scratch],
+        compiler_params=pltpu.CompilerParams(vmem_limit_bytes=40 * 1024 * 1024),
+    )(*operands)
+
+
+def heads_first(x):
+    return jnp.swapaxes(x, 0, 1)
+
+
+def exchange(x):
+    return lax.all_to_all(x, "seq", 0, 0, tiled=True)
+
+
+def three_parts(x):
+    high = lax.reduce_precision(x, 8, 7)
+    middle = lax.reduce_precision(x - high, 8, 7)
+    return [part.astype(bf16) for part in (high, middle, x - high - middle)]
+
+
+def over_heads(received, chunks):
+    parts = received.astype(f32)
+    mine = jnp.sum(parts[:, 0:chunks] + parts[:, chunks : 2 * chunks], axis=0)
+    count = lax.axis_size("head")
+    total = mine
+    for step in range(1, count):
+        total = total + lax.ppermute(mine, "head", [(i, (i + step) % count) for i in range(count)])
+    return total
+
+
+def body(query_one, key_one, value_one, log_decay, query_two, key_two, out_grad, doc_ids):
+    length, heads_here, width = query_one.shape
+    shards = lax.axis_size("seq")
+    if heads_here != shards or length != BLOCK or shards % 16 or width != BLOCK:
+        return ring_body(
+            query_one, key_one, value_one, log_decay, query_two, key_two, out_grad, doc_ids
+        )
+    positions = shards * length
+    features = heads_here * lax.axis_size("head") * width
+    decay_rows = jnp.stack(three_parts(log_decay), axis=1)
+    decay_rows = jnp.pad(decay_rows, ((0, 0), (0, PART_ROWS - 3), (0, 0)))
+    first = exchange(
+        jnp.concatenate([heads_first(x) for x in (query_one, key_one, value_one)] + [decay_rows], axis=1)
+    )
+    raw, states, sums = call(
+        linear_forward,
+        [((positions, width), f32), ((shards, width, width), bf16), ((2 * shards, BLOCK), bf16)],
+        [],
+        first,
+    )
+    sums_rows = jnp.broadcast_to(sums[None], (shards,) + sums.shape)
+    second = exchange(
+        jnp.concatenate([heads_first(x) for x in (query_two, key_two, out_grad)] + [sums_rows], axis=1)
+    )
+    square_sums = over_heads(second[:, 3 * BLOCK :], shards)
+    starts = jnp.sum((doc_ids[None, :] < doc_ids[:, None]).astype(jnp.int32), axis=1)
+    third, value_grad = call(
+        partial(softmax_both, features),
+        [((shards, 2 * BLOCK + 2 * shards, width), bf16), ((positions, width), f32)],
+        [
+            ((positions, width), bf16),
+            ((width, positions), bf16),
+            ((positions, width), bf16),
+            ((width, positions), bf16),
+            ((positions, width), f32),
+        ],
+        starts,
+        second,
+        raw,
+        square_sums,
+        prefetch=1,
+    )
+    third = exchange(third)
+    cross = over_heads(third[:, 2 * BLOCK :], shards)
+    (fourth,) = call(
+        partial(linear_backward, features),
+        [((shards, 3 * BLOCK, width), bf16)],
+        [],
+        first,
+        raw,
+        states,
+        square_sums,
+        cross,
+        value_grad,
+    )
+    fourth = exchange(fourth)
+
+    def result(received, place):
+        return heads_first(received[:, place * BLOCK : (place + 1) * BLOCK]).astype(f32)
+
+    return (
+        result(fourth, 0),
+        result(fourth, 1),
+        result(fourth, 2),
+        result(third, 0),
+        result(third, 1),
+    )
+
+
 def solution(mesh):
     placed = (
         P("seq", "head", None),
@@ -226,12 +499,6 @@
         body,
         mesh=mesh,
         in_specs=placed,
-        out_specs=(
-            P("seq", "head", None),
-            P("seq", "head", None),
-            P("seq", "head", None),
-            P("seq", "head", None),
-            P("seq", "head", None),
-        ),
+        out_specs=(P("seq", "head", None),) * 5,
         check_vma=False,
     )

time: 920 us -> 205 us (0.22); the launches traced: 903 us -> 204 us
  waiting for transfers between devices: 556 us -> 72.6 us
  starting transfers between devices: 108 us -> 13.6 us
  matrix products: 81.9 us -> 0 us
  other arithmetic: 58.1 us -> 3.03 us
  blocking collectives: 42.6 us -> 76.5 us
  between operations: 27.6 us -> 0.78 us
  Pallas kernels: 0 us -> 25.2 us
  local copies, waits for them, and re-layouts: 27.6 us -> 12.2 us
    ppermute x32 -> x2, waiting for transfers between devices: 556 us -> 2.13 us  [over_heads(): lax.ppermute(mine, 'head', [(i, (i + step) % count) for i in range(count)])]
    ppermute x32 -> x2, starting transfers between devices: 108 us -> 0.14 us  [over_heads(): lax.ppermute(mine, 'head', [(i, (i + step) % count) for i in range(count)])]
    dot_general x66 -> x0, matrix products: 81.9 us -> none  [the longest x9 12.8 us: scores_work(): jnp.einsum('thd,uhd->htu', query_two, keys_block, preferred_element_type=...]
    all_to_all x0 -> x2, blocking collectives: none -> 76.5 us  [exchange(): return lax.all_to_all(x, 'seq', 0, 0, tiled=True)]
    all_to_all x0 -> x2, waiting for transfers between devices: none -> 70.4 us  [exchange(): return lax.all_to_all(x, 'seq', 0, 0, tiled=True)]
    select_n x30 -> x0, other arithmetic: 43.7 us -> none  [hop(): jnp.where(position < mine, new, old)]
    unnamed x1 -> x0, blocking collectives: 40 us -> none
    pallas_call x0 -> x3, Pallas kernels: none -> 25.2 us  [call(): pl.pallas_call(kernel, out_shape=[jax.ShapeDtypeStruct(shape, kind) for s...]
  transfers between devices with their start and end apart: 34 -> 4, of which waited for: 30 -> 4; matrix products, arithmetic and copies ran while one was open for 12% -> 3% of each run, Pallas kernels for 0% -> 0%
where the time goes in v1:
time: 205 us; the launch traced here: 204 us
  blocking collectives  76.5 us (37%)
  waiting for transfers between devices  72.6 us (35%)
  Pallas kernels  25.2 us (12%)
  starting transfers between devices  13.6 us (7%)
  local copies, waits for them, and re-layouts  12.2 us (6%)
  other arithmetic  3.03 us (1%)
    all_to_all x2, blocking collectives, exchange(): return lax.all_to_all(x, 'seq', 0, 0, tiled=True)  76.5 us
    all_to_all x2, waiting for transfers between devices, exchange(): return lax.all_to_all(x, 'seq', 0, 0, tiled=True)  70.4 us
    pallas_call x3, Pallas kernels, call(): pl.pallas_call(kernel, out_shape=[jax.ShapeDtypeStruct(shape, kind) for s...  25.2 us
    all_to_all x2, starting transfers between devices, exchange(): return lax.all_to_all(x, 'seq', 0, 0, tiled=True)  13.4 us
    unnamed x11, local copies, waits for them, and re-layouts  9.24 us
  transfers between devices with their start and end apart: 4, of which 4 were waited for; matrix products, arithmetic and copies ran while one was open for 3% of the time, Pallas kernels for 0%

profile of v1, /device:TPU:16, one launch (start us, length us, event | category | flops | bytes accessed | tf_op | source)
XLA Modules:
  0.0 203.9 jit_solution(4356045927371811710)
XLA Ops:
  0.6 0.7 fusion.9
  1.4 1.2 copy.87
  2.6 1.5 copy_bitcast_fusion.3
  4.1 1.3 pad_maximum_fusion.1
  5.4 7.2 %all-to-all-start = ((bf16[16,400,128]{2,1,0:T(8,128)(2,1)}), bf16[16,400,128]{2,1,0:T(8,128)(2,1)S(1)}, u32[]{:S(2)}, u32[]{:S(2)}) async-start(bf16[16,400,128]{2,1,0:T(8,128)(2,1)} %pad_maximum_fusion.1), calls=%async_computation | async-start | bytes 3276800 | tf_op jit(solution)/shard_map/all_to_all | solution.py:399
  12.8 1.5 copy_bitcast_fusion
  14.2 36.1 %all-to-all-done.first_ref = bf16[16,400,128]{2,1,0:T(8,128)(2,1)S(1)} async-done(((bf16[16,400,128]{2,1,0:T(8,128)(2,1)}), bf16[16,400,128]{2,1,0:T(8,128)(2,1)S(1)}, u32[]{:S(2)}, u32[]{:S(2)}) %all-to-all-start) | async-done | bytes 1638432 | tf_op jit(solution)/shard_map/all_to_all | solution.py:399
  50.3 3.6 %shard_map.119 = (f32[2048,128]{1,0:T(8,128)S(1)}, bf16[16,128,128]{2,1,0:T(8,128)(2,1)S(1)}, bf16[32,128]{1,0:T(8,128)(2,1)S(1)}) custom-call(bf16[16,400,128]{2,1,0:T(8,128)(2,1)S(1)} %all-to-all-done.first_ref), custom_call_target="tpu_custom_call" | custom-call | tf_op jit(solution)/shard_map/pallas_call | solution.py:384
  54.1 43.4 %all_to_all.20.second_ref = bf16[16,416,128]{2,1,0:T(8,128)(2,1)S(1)} all-to-all(bf16[16,416,128]{2,1,0:T(8,128)(2,1)S(1)} %pad_maximum_fusion), channel_id=1, replica_groups=mesh['seq'=16,'head'=2] {'seq'}, dimensions={0} | all-to-all | bytes 3407872 | tf_op jit(solution)/shard_map/all_to_all | solution.py:399
  97.6 0.2 convert_reduce_fusion.starts_ref
  97.8 1.0 collective-permute-done
  98.8 16.1 %shard_map.120 = (bf16[16,288,128]{2,1,0:T(8,128)(2,1)S(1)}, f32[2048,128]{1,0:T(8,128)S(1)}) custom-call(s32[16]{0:T(128)S(1)} %convert_reduce_fusion.starts_ref, bf16[16,416,128]{2,1,0:T(8,128)(2,1)S(1)} %all_to_all.20.second_ref, f32[2048,128]{1,0:T(8,128)S(1)} %get-tuple-element.10.raw_ref, f32[16,128]{1,0:T(8,128)S(1)} %add.15.sums_ref), custom_call_target="tpu_custom_call" | custom-call | tf_op jit(solution)/shard_map/pallas_call | solution.py:384
  114.9 33.2 %all_to_all.21 = bf16[16,288,128]{2,1,0:T(8,128)(2,1)S(1)} all-to-all(bf16[16,288,128]{2,1,0:T(8,128)(2,1)S(1)} %get-tuple-element.13), channel_id=1, replica_groups=mesh['seq'=16,'head'=2] {'seq'}, dimensions={0} | all-to-all | bytes 2359296 | tf_op jit(solution)/shard_map/all_to_all | solution.py:399
  148.2 1.2 collective-permute-done.1
  149.4 5.5 %shard_map.121 = bf16[16,384,128]{2,1,0:T(8,128)(2,1)} custom-call(bf16[16,400,128]{2,1,0:T(8,128)(2,1)S(1)} %all-to-all-done.first_ref, f32[2048,128]{1,0:T(8,128)S(1)} %get-tuple-element.10.raw_ref, bf16[16,128,128]{2,1,0:T(8,128)(2,1)S(1)} %get-tuple-element.11.state_ref, f32[16,128]{1,0:T(8,128)S(1)} %add.15.sums_ref, f32[16,128]{1,0:T(8,128)S(1)} %add.17.cross_ref, ...), custom_call_target="tpu_custom_call" | custom-call | tf_op jit(solution)/shard_map/pallas_call | solution.py:384
  154.9 6.2 %all-to-all-start.3 = ((bf16[16,384,128]{2,1,0:T(8,128)(2,1)}), bf16[16,384,128]{2,1,0:T(8,128)(2,1)S(1)}, u32[]{:S(2)}, u32[]{:S(2)}) async-start(bf16[16,384,128]{2,1,0:T(8,128)(2,1)} %shard_map.121), calls=%async_computation.3 | async-start | bytes 3145728 | tf_op jit(solution)/shard_map/all_to_all | solution.py:399
  161.1 0.2 convert_bitcast_fusion
  161.3 1.6 copy.79
  162.9 1.6 copy.78
  164.5 34.3 %all-to-all-done.3 = bf16[16,384,128]{2,1,0:T(8,128)(2,1)S(1)} async-done(((bf16[16,384,128]{2,1,0:T(8,128)(2,1)}), bf16[16,384,128]{2,1,0:T(8,128)(2,1)S(1)}, u32[]{:S(2)}, u32[]{:S(2)}) %all-to-all-start.3) | async-done | bytes 1572896 | tf_op jit(solution)/shard_map/all_to_all | solution.py:399
  198.8 0.4 convert_bitcast_fusion.2
  199.2 1.6 copy.77
  200.8 1.6 copy.76
  202.3 1.6 copy.75
  (19 shorter events, 0.6 us)
Async XLA Ops:
  5.4 7.2 %copy-start = (bf16[128,16,128]{2,1,0:T(8,128)(2,1)S(1)}, bf16[128,16,128]{2,1,0:T(8,128)(2,1)}, u32[]{:S(2)}) copy-start(bf16[128,16,128]{2,1,0:T(8,128)(2,1)} %param.12) | copy-start | bytes 1572868
  5.4 45.0 %all-to-all-start = ((bf16[16,400,128]{2,1,0:T(8,128)(2,1)}), bf16[16,400,128]{2,1,0:T(8,128)(2,1)S(1)}, u32[]{:S(2)}, u32[]{:S(2)}) async-start(bf16[16,400,128]{2,1,0:T(8,128)(2,1)} %pad_maximum_fusion.1), calls=%async_computation | async-start | bytes 3276800 | tf_op jit(solution)/shard_map/all_to_all | solution.py:399
  54.1 43.5 %copy-start.1 = (s32[16]{0:T(128)S(1)}, s32[16]{0:T(128)}, u32[]{:S(2)}) copy-start(s32[16]{0:T(128)} %param.15) | copy-start | bytes 196
  97.6 1.2 collective-permute-start
  148.1 1.2 collective-permute-start.1
  154.9 43.9 %all-to-all-start.3 = ((bf16[16,384,128]{2,1,0:T(8,128)(2,1)}), bf16[16,384,128]{2,1,0:T(8,128)(2,1)S(1)}, u32[]{:S(2)}, u32[]{:S(2)}) async-start(bf16[16,384,128]{2,1,0:T(8,128)(2,1)} %shard_map.121), calls=%async_computation.3 | async-start | bytes 3145728 | tf_op jit(solution)/shard_map/all_to_all | solution.py:399

commit v2 on v0

--- a/solution.py
+++ b/solution.py
@@ -4,6 +4,8 @@
 import jax
 import jax.numpy as jnp
 from jax import lax
+from jax.experimental import pallas as pl
+from jax.experimental.pallas import tpu as pltpu
 from jax.sharding import PartitionSpec as P
 
 BLOCK = 128
@@ -105,7 +107,7 @@
     return (query_grad, key_grad, value_grad)
 
 
-def body(query_one, key_one, value_one, log_decay, query_two, key_two, out_grad, doc_ids):
+def ring_body(query_one, key_one, value_one, log_decay, query_two, key_two, out_grad, doc_ids):
     length, heads_here, width = query_one.shape
     shards = lax.axis_size("seq")
     token_position = lax.axis_index("seq")
@@ -211,6 +213,543 @@
     )
 
 
+f32, bf16 = (jnp.float32, jnp.bfloat16)
+LOG2E = math.log2(math.e)
+PART_ROWS = 16
+
+
+def dot(a, b):
+    return lax.dot_general(a, b, (((1,), (0,)), ((), ())), preferred_element_type=f32)
+
+
+def dot_nt(a, b):
+    return lax.dot_general(a, b, (((1,), (1,)), ((), ())), preferred_element_type=f32)
+
+
+def dot_tn(a, b):
+    return lax.dot_general(a, b, (((0,), (0,)), ((), ())), preferred_element_type=f32)
+
+
+def two_parts(value):
+    high = value.astype(bf16)
+    return high, (value - high.astype(f32)).astype(bf16)
+
+
+def row_sums(value):
+    ones = jnp.ones((PART_ROWS, value.shape[1]), bf16)
+    high, low = two_parts(value)
+    return dot_nt(ones, high) + dot_nt(ones, low)
+
+
+def chunk_decays(parts):
+    lower = lower_mask(BLOCK)
+    log_row = jnp.sum(parts.astype(f32), axis=0, keepdims=True)
+    column = jnp.sum(jnp.where(lower, log_row, 0.0), axis=1, keepdims=True)
+    upper = lax.broadcasted_iota(jnp.int32, (BLOCK, BLOCK), 0) <= lax.broadcasted_iota(
+        jnp.int32, (BLOCK, BLOCK), 1
+    )
+    row = jnp.sum(dot(parts, jnp.where(upper, 1.0, 0.0).astype(bf16)), axis=0, keepdims=True)
+    last = column[BLOCK - 1 : BLOCK, :]
+    weights = jnp.exp(jnp.where(lower, column - row, floor_score))
+    return weights, jnp.exp(column), jnp.exp(last - column), jnp.exp(last)
+
+
+def lightning_piece(ref, place):
+    arrays = [ref[place, n * BLOCK : (n + 1) * BLOCK, :] for n in range(3)]
+    return arrays + [chunk_decays(ref[place, ref.shape[1] - PART_ROWS :, :])]
+
+
+UNROLL = 16
+
+
+def over_chunks(chunks, body, carry, backward=False):
+    unrolled = math.gcd(UNROLL, chunks)
+
+    def step(n, carry):
+        for part in range(unrolled):
+            c = n * unrolled + part
+            carry = body(chunks - 1 - c if backward else c, carry)
+        return carry
+
+    if unrolled == chunks:
+        return step(0, carry)
+    return lax.fori_loop(0, chunks // unrolled, step, carry)
+
+
+def block_rows(c):
+    if isinstance(c, int):
+        return slice(c * BLOCK, (c + 1) * BLOCK)
+    return pl.ds(pl.multiple_of(c * BLOCK, BLOCK), BLOCK)
+
+
+def linear_state(heads, second_ref, state_ref):
+    chunks, width = (second_ref.shape[0] // heads, second_ref.shape[2])
+
+    def chunk(c, states):
+        following = []
+        for head in range(heads):
+            _, k, v, (_, _, tail, whole) = lightning_piece(second_ref, c * heads + head)
+            following.append(
+                whole * states[head] + dot_tn(k, (v.astype(f32) * tail).astype(bf16))
+            )
+        return tuple(following)
+
+    states = over_chunks(chunks, chunk, (jnp.zeros((width, width), f32),) * heads)
+    for head in range(heads):
+        state_ref[head] = states[head]
+
+
+def value_gradient(half, kept_ref, other_ref, head, c):
+    return jnp.where(
+        half == head, kept_ref[block_rows(c), :], other_ref[block_rows(c), :].astype(f32)
+    )
+
+
+def linear_forward(
+    heads, info_ref, second_ref, incoming_ref, kept_ref, other_ref,
+    raw_ref, sent_ref, state_ref, sums_ref,
+):
+    chunks = second_ref.shape[0] // heads
+    half = info_ref[info_ref.shape[0] - 1]
+
+    def chunk(c, states):
+        following = []
+        squares, cross = (0.0, 0.0)
+        raws = []
+        for head in range(heads):
+            q, k, v, (weights, grow, tail, whole) = lightning_piece(second_ref, c * heads + head)
+            prob = (dot_nt(q, k) * weights).astype(bf16)
+            state_low = states[head].astype(bf16)
+            raw = dot(prob, v) + grow * dot(q, state_low)
+            state_ref[head, c] = state_low
+            following.append(
+                whole * states[head] + dot_tn(k, (v.astype(f32) * tail).astype(bf16))
+            )
+            raw_ref[head, block_rows(c), :] = raw
+            raws.append(raw)
+            grad = value_gradient(half, kept_ref, other_ref, head, c)
+            squares = squares + row_sums(raw * raw)[0:1, :]
+            cross = cross + row_sums(raw * grad)[0:1, :]
+        sent_ref[block_rows(c), :] = jnp.where(half == 0, raws[1], raws[0]).astype(bf16)
+        sums_ref[c : c + 1, :] = squares
+        sums_ref[chunks + c : chunks + c + 1, :] = cross
+        return tuple(following)
+
+    over_chunks(chunks, chunk, tuple(incoming_ref[head] for head in range(heads)))
+
+
+def column(columns, c):
+    if isinstance(c, int):
+        return columns[:, c : c + 1]
+    lanes = lax.broadcasted_iota(jnp.int32, columns.shape, 1)
+    return jnp.sum(jnp.where(lanes == c, columns, 0.0), axis=1, keepdims=True)
+
+
+def norm_columns(features, sums_ref):
+    chunks = sums_ref.shape[0] // 2
+    inverse = 1.0 / jnp.sqrt(sums_ref[0:chunks, :] / features + norm_epsilon)
+    return inverse.T, (inverse * inverse * inverse * sums_ref[chunks:, :] / features).T
+
+
+def linear_state_grad(
+    features, heads, info_ref, second_ref, raw_ref, sums_ref, kept_ref, other_ref, state_grad_ref
+):
+    chunks, width = (second_ref.shape[0] // heads, second_ref.shape[2])
+    half = info_ref[info_ref.shape[0] - 1]
+    inverse, cross = norm_columns(features, sums_ref)
+
+    def chunk(c, grads):
+        following = []
+        for head in range(heads):
+            q, _, _, (_, grow, _, whole) = lightning_piece(second_ref, c * heads + head)
+            grad = column(inverse, c) * value_gradient(half, kept_ref, other_ref, head, c)
+            grad = grad - raw_ref[head, block_rows(c), :] * column(cross, c)
+            following.append(whole * grads[head] + dot_tn(q, (grad * grow).astype(bf16)))
+        return tuple(following)
+
+    grads = over_chunks(chunks, chunk, (jnp.zeros((width, width), f32),) * heads, True)
+    for head in range(heads):
+        state_grad_ref[head] = grads[head]
+
+
+def linear_backward(
+    features, heads, info_ref, second_ref, raw_ref, state_ref, sums_ref, kept_ref, other_ref, later_ref,
+    out_ref,
+):
+    chunks = second_ref.shape[0] // heads
+    half = info_ref[info_ref.shape[0] - 1]
+    inverse, cross = norm_columns(features, sums_ref)
+
+    def chunk(c, grads):
+        following = []
+        for head in range(heads):
+            place = c * heads + head
+            q, k, v, (weights, grow, tail, whole) = lightning_piece(second_ref, place)
+            grad = column(inverse, c) * value_gradient(half, kept_ref, other_ref, head, c)
+            grad = grad - raw_ref[head, block_rows(c), :] * column(cross, c)
+            grad_low = grad.astype(bf16)
+            prob = (dot_nt(q, k) * weights).astype(bf16)
+            grad_score = (dot_nt(grad_low, v) * weights).astype(bf16)
+            state_low = grads[head].astype(bf16)
+            query_grad = dot(grad_score, k) + grow * dot_nt(grad_low, state_ref[head, c])
+            key_grad = dot_tn(grad_score, q) + tail * dot_nt(v, state_low)
+            value_grad = dot_tn(prob, grad_low) + tail * dot(k, state_low)
+            following.append(whole * grads[head] + dot_tn(q, (grad * grow).astype(bf16)))
+            out_ref[place, 0:BLOCK, :] = query_grad.astype(bf16)
+            out_ref[place, BLOCK : 2 * BLOCK, :] = key_grad.astype(bf16)
+            out_ref[place, 2 * BLOCK : 3 * BLOCK, :] = value_grad.astype(bf16)
+        return tuple(following)
+
+    over_chunks(chunks, chunk, tuple(later_ref[head] for head in range(heads)), True)
+
+
+TOGETHER = 4
+GROUP = TOGETHER * BLOCK
+
+
+def by_window(info_ref, chunks, window):
+    def step(group, carry):
+        end = TOGETHER * (group + 1)
+        need = end - info_ref[TOGETHER * group]
+        least = 0
+        for blocks in window_sizes(chunks):
+            begin = pl.multiple_of((end - blocks) * BLOCK, 2 * BLOCK)
+            pl.when((need > least) & (need <= blocks))(partial(window, group, begin, blocks))
+            least = blocks
+        return carry
+
+    lax.fori_loop(0, chunks // TOGETHER, step, 0)
+
+
+def window_sizes(chunks):
+    return range(TOGETHER, min(chunks, REACH + TOGETHER) + 1, 2)
+
+
+def window_scores(info_ref, keys, queries, group, begin):
+    shape = (keys.shape[0], queries.shape[0])
+    scores = dot(keys, queries.T) * (LOG2E / math.sqrt(keys.shape[1]))
+    u_pos = begin + lax.broadcasted_iota(jnp.int32, shape, 0)
+    lane = lax.broadcasted_iota(jnp.int32, (1, shape[1]), 1)
+    lowest = jnp.zeros_like(lane)
+    for n in range(TOGETHER):
+        lowest = jnp.where(lane >= n * BLOCK, info_ref[TOGETHER * group + n] * BLOCK, lowest)
+    return scores, (u_pos >= lowest) & (u_pos <= group * GROUP + lane)
+
+
+def group_rows(group):
+    return pl.ds(pl.multiple_of(group * GROUP, GROUP), GROUP)
+
+
+def softmax_masses(info_ref, first_ref, mass_ref, kept_ref, sent_ref, key_s, query_s, grad_s, value_grad_s):
+    chunks, width = (first_ref.shape[0], first_ref.shape[2])
+    for c in range(chunks):
+        here = block_rows(c)
+        query_s[here, :] = first_ref[c, 0:BLOCK, :]
+        key_s[here, :] = first_ref[c, BLOCK : 2 * BLOCK, :]
+        grad_s[here, :] = first_ref[c, 2 * BLOCK :, :]
+        value_grad_s[here, :] = jnp.zeros((BLOCK, width), f32)
+
+    def window(group, begin, blocks):
+        rows = pl.ds(begin, blocks * BLOCK)
+        scores, allowed = window_scores(
+            info_ref, key_s[rows, :], query_s[group_rows(group), :], group, begin
+        )
+        scores = jnp.where(allowed, scores, floor_score)
+        peak = jnp.max(scores, axis=0, keepdims=True)
+        mass = jnp.exp2(scores - peak)
+        total = jnp.sum(mass, axis=0, keepdims=True)
+        mass_ref[pl.ds(group, 1), :] = peak + jnp.log2(total)
+        prob = (mass * (1.0 / total)).astype(bf16)
+        value_grad_s[rows, :] += dot(prob, grad_s[group_rows(group), :])
+
+    by_window(info_ref, chunks, window)
+    half = info_ref[info_ref.shape[0] - 1]
+    for c in range(chunks // 2):
+        low = value_grad_s[block_rows(c), :]
+        high = value_grad_s[block_rows(chunks // 2 + c), :]
+        kept_ref[block_rows(c), :] = jnp.where(half == 0, low, high)
+        sent_ref[block_rows(c), :] = jnp.where(half == 0, high, low).astype(bf16)
+
+
+def softmax_grads(
+    features, info_ref, first_ref, mass_ref, raw_ref, other_ref, sums_ref, other_sums_ref, out_ref,
+    key_s, key_t_s, value_s, value_t_s, query_s, grad_s, key_grad_s,
+):
+    chunks, width = (first_ref.shape[0], first_ref.shape[2])
+    side = chunks // 2
+    scale = 1.0 / math.sqrt(width)
+    half = info_ref[info_ref.shape[0] - 1]
+    inverse, other_inverse = [
+        (1.0 / jnp.sqrt(ref[0:side, :] / features + norm_epsilon)).T for ref in (sums_ref, other_sums_ref)
+    ]
+    for c in range(chunks):
+        here = block_rows(c)
+        there = block_rows(c % side)
+        own = jnp.where(half == 0, raw_ref[0, there, :], raw_ref[1, there, :])
+        own = own * column(inverse, c % side)
+        other = other_ref[there, :].astype(f32) * column(other_inverse, c % side)
+        v = jnp.where(half == c // side, own, other).astype(bf16)
+        value_s[here, :] = v
+        value_t_s[:, here] = v.T
+        query_s[here, :] = first_ref[c, 0:BLOCK, :]
+        key_s[here, :] = first_ref[c, BLOCK : 2 * BLOCK, :]
+        key_t_s[:, here] = first_ref[c, BLOCK : 2 * BLOCK, :].T
+        grad_s[here, :] = first_ref[c, 2 * BLOCK :, :]
+        key_grad_s[here, :] = jnp.zeros((BLOCK, width), f32)
+
+    def window(group, begin, blocks):
+        rows = pl.ds(begin, blocks * BLOCK)
+        queries = query_s[group_rows(group), :]
+        scores, allowed = window_scores(info_ref, key_s[rows, :], queries, group, begin)
+        scores = jnp.where(allowed, scores - mass_ref[pl.ds(group, 1), :], floor_score)
+        prob = jnp.exp2(scores)
+        g_t = grad_s[group_rows(group), :].T
+        attended = dot(value_t_s[:, rows], prob.astype(bf16))
+        delta = jnp.sum(g_t.astype(f32) * attended, axis=0, keepdims=True)
+        grad_prob = dot(value_s[rows, :], g_t)
+        grad_score = (prob * ((grad_prob - delta) * scale)).astype(bf16)
+        key_grad_s[rows, :] += dot(grad_score, queries)
+        query_grad = dot(key_t_s[:, rows], grad_score).T.astype(bf16)
+        for c in range(TOGETHER):
+            out_ref[TOGETHER * group + c, 0:BLOCK, :] = query_grad[block_rows(c), :]
+
+    by_window(info_ref, chunks, window)
+    for c in range(chunks):
+        out_ref[c, BLOCK : 2 * BLOCK, :] = key_grad_s[block_rows(c), :].astype(bf16)
+
+
+def call(kernel, micros, outs, scratch, *operands, prefetch=0, room=8, whole=False):
+    vmem = pl.BlockSpec(memory_space=pltpu.VMEM)
+    smem = pl.BlockSpec(memory_space=pltpu.SMEM)
+    results = [jax.ShapeDtypeStruct(shape, kind) for shape, kind in outs]
+    held = [jax.ShapeDtypeStruct(shape, kind) for shape, kind in scratch]
+    size = sum(
+        a.size * a.dtype.itemsize for a in [*held, *(([*operands, *results]) if whole else [])]
+    )
+    return pl.pallas_call(
+        kernel,
+        out_shape=results,
+        in_specs=[smem] * prefetch + [vmem] * (len(operands) - prefetch),
+        out_specs=[vmem] * len(outs),
+        scratch_shapes=[pltpu.VMEM(shape, kind) for shape, kind in scratch],
+        compiler_params=pltpu.CompilerParams(vmem_limit_bytes=size + room * 1024 * 1024),
+        cost_estimate=pl.CostEstimate(
+            flops=int(micros * 1e9), bytes_accessed=int(micros * 3e6), transcendentals=0
+        ),
+    )(*operands)
+
+
+def swap_matrix(chunks):
+    size = chunks * chunks
+    i = lax.broadcasted_iota(jnp.int32, (size, size), 0)
+    j = lax.broadcasted_iota(jnp.int32, (size, size), 1)
+    return jnp.where(j == (i % chunks) * chunks + i // chunks, 1.0, 0.0).astype(bf16)
+
+
+def pair_order(heads):
+    return [(h % 2) * (heads // 2) + h // 2 for h in range(heads)]
+
+
+def pack(order, *refs):
+    arrays, out_ref = ([ref for ref in refs[:-1] if len(ref.shape) == 3], refs[-1])
+    length, heads, width = arrays[0].shape
+    swap = swap_matrix(heads)
+    for place, ref in enumerate(arrays):
+        for begin in range(0, length, heads):
+            rows = ref[begin : begin + heads].reshape(heads * heads, width)
+            swapped = dot(swap, rows).astype(bf16)
+            row = place * length + begin
+            for h in range(heads):
+                out_ref[order[h], row : row + heads, :] = swapped[h * heads : (h + 1) * heads, :]
+    if len(arrays) == len(refs) - 1:
+        return
+    decay_ref = refs[-2]
+    high, _ = two_parts(decay_ref[...])
+    middle, last = two_parts(decay_ref[...] - high.astype(f32))
+    row = lax.broadcasted_iota(jnp.int32, (PART_ROWS, length), 0)
+    for h in range(heads):
+        tile = jnp.zeros((PART_ROWS, length), f32)
+        for n, part in enumerate((high, middle, last)):
+            tile = jnp.where(row == n, part[h : h + 1, :].astype(f32), tile)
+        out_ref[order[h], len(arrays) * length :, :] = tile.astype(bf16)
+
+
+def unpack(order, in_ref, *outs):
+    length, heads, width = outs[0].shape
+    swap = swap_matrix(heads)
+    for place, out_ref in enumerate(outs):
+        for begin in range(0, length, heads):
+            row = place * length + begin
+            rows = jnp.concatenate(
+                [in_ref[order[h], row : row + heads, :] for h in range(heads)], axis=0
+            )
+            out_ref[begin : begin + heads] = dot(swap, rows).reshape(heads, heads, width)
+
+
+def exchange(x):
+    return lax.all_to_all(x, "seq", 0, 0, tiled=True)
+
+
+def exchange_half(x):
+    side = lax.axis_size("seq") // 2
+    groups = [list(range(side)), list(range(side, 2 * side))]
+    return lax.all_to_all(x, "seq", 0, 0, tiled=True, axis_index_groups=groups)
+
+
+def upward(x):
+    side = lax.axis_size("seq") // 2
+    return lax.ppermute(x, "seq", [(i, i + side) for i in range(side)])
+
+
+def downward(x):
+    side = lax.axis_size("seq") // 2
+    return lax.ppermute(x, "seq", [(i + side, i) for i in range(side)])
+
+
+def swapped(x):
+    side = lax.axis_size("seq") // 2
+    return lax.ppermute(x, "seq", [(i, (i + side) % (2 * side)) for i in range(2 * side)])
+
+
+def over_heads(mine):
+    count = lax.axis_size("head")
+    total = mine
+    for step in range(1, count):
+        total = total + lax.ppermute(mine, "head", [(i, (i + step) % count) for i in range(count)])
+    return total
+
+
+def body(query_one, key_one, value_one, log_decay, query_two, key_two, out_grad, doc_ids):
+    length, heads_here, width = query_one.shape
+    shards = lax.axis_size("seq")
+    if heads_here != shards or length != BLOCK or shards != 16 or width != BLOCK:
+        return ring_body(
+            query_one, key_one, value_one, log_decay, query_two, key_two, out_grad, doc_ids
+        )
+    side = shards // 2
+    heads = heads_here // side
+    half_length = side * length
+    features = heads_here * lax.axis_size("head") * width
+    half = (lax.axis_index("seq") >= side).astype(jnp.int32)
+    starts = jnp.sum((doc_ids[None, :] < doc_ids[:, None]).astype(jnp.int32), axis=1)
+    info = jnp.concatenate([starts, half[None]])
+    straight, paired = (list(range(heads_here)), pair_order(heads_here))
+
+    def packed(order, rows, arrays, *more):
+        arrays = [pltpu.with_memory_space_constraint(array, pltpu.HBM) for array in arrays]
+        return call(
+            partial(pack, order), 3, [((heads_here, rows, width), bf16)], [], *arrays, *more, whole=True
+        )[0]
+
+    first = exchange(packed(paired, 3 * length, (query_two, key_two, out_grad)))
+    second = exchange_half(
+        packed(straight, 3 * length + PART_ROWS, (query_one, key_one, value_one), log_decay)
+    )
+    half_rows = (half_length, width)
+    full_rows = (shards * length, width)
+    masses, grad_kept, grad_sent = call(
+        softmax_masses,
+        6,
+        [
+            ((shards // TOGETHER, GROUP), f32),
+            (half_rows, f32),
+            (half_rows, bf16),
+        ],
+        [(full_rows, bf16), (full_rows, bf16), (full_rows, bf16), (full_rows, f32)],
+        info,
+        first,
+        prefetch=1,
+    )
+    grad_other = swapped(grad_sent)
+    state_shape = (heads, width, width)
+    (state,) = call(partial(linear_state, heads), 1, [(state_shape, f32)], [], second)
+    incoming = upward(state)
+    raw, raw_sent, states, sums = call(
+        partial(linear_forward, heads),
+        4,
+        [
+            ((heads, half_length, width), f32),
+            (half_rows, bf16),
+            ((heads, side, width, width), bf16),
+            ((2 * side, BLOCK), f32),
+        ],
+        [],
+        info,
+        second,
+        incoming,
+        grad_kept,
+        grad_other,
+        prefetch=1,
+    )
+    raw_other = swapped(raw_sent)
+    sums = exchange_half(jnp.broadcast_to(sums[None], (side,) + sums.shape))
+    sums = over_heads(jnp.sum(sums, axis=0))
+    sums_other = swapped(sums[:side])
+    (softmax_grad,) = call(
+        partial(softmax_grads, features),
+        7,
+        [((shards, 2 * BLOCK, width), bf16)],
+        [
+            (full_rows, bf16),
+            ((width, shards * length), bf16),
+            (full_rows, bf16),
+            ((width, shards * length), bf16),
+            (full_rows, bf16),
+            (full_rows, bf16),
+            (full_rows, f32),
+        ],
+        info,
+        first,
+        masses,
+        raw,
+        raw_other,
+        sums,
+        sums_other,
+        prefetch=1,
+    )
+    (state_grad,) = call(
+        partial(linear_state_grad, features, heads),
+        2,
+        [(state_shape, f32)],
+        [],
+        info,
+        second,
+        raw,
+        sums,
+        grad_kept,
+        grad_other,
+        prefetch=1,
+    )
+    later_grad = downward(state_grad)
+    later_grad, softmax_grad = lax.optimization_barrier((later_grad, softmax_grad))
+    softmax_grad = exchange(softmax_grad)
+    (linear_grads,) = call(
+        partial(linear_backward, features, heads),
+        5,
+        [((heads_here, 3 * BLOCK, width), bf16)],
+        [],
+        info,
+        second,
+        raw,
+        states,
+        sums,
+        grad_kept,
+        grad_other,
+        later_grad,
+        prefetch=1,
+    )
+    softmax_grad, linear_grads = lax.optimization_barrier((softmax_grad, linear_grads))
+    linear_grads = exchange_half(linear_grads)
+
+    def unpacked(order, count, received):
+        outs = [((length, heads_here, width), f32)] * count
+        return call(partial(unpack, order), count, outs, [], received, whole=True)
+
+    query_one_grad, key_one_grad, value_one_grad = unpacked(straight, 3, linear_grads)
+    query_two_grad, key_two_grad = unpacked(paired, 2, softmax_grad)
+    return (query_one_grad, key_one_grad, value_one_grad, query_two_grad, key_two_grad)
+
+
 def solution(mesh):
     placed = (
         P("seq", "head", None),
@@ -226,12 +765,6 @@
         body,
         mesh=mesh,
         in_specs=placed,
-        out_specs=(
-            P("seq", "head", None),
-            P("seq", "head", None),
-            P("seq", "head", None),
-            P("seq", "head", None),
-            P("seq", "head", None),
-        ),
+        out_specs=(P("seq", "head", None),) * 5,
         check_vma=False,
     )

time: 920 us -> 182 us (0.20); the launches traced: 903 us -> 179 us
  waiting for transfers between devices: 556 us -> 93.2 us
  matrix products: 81.9 us -> 0 us
  starting transfers between devices: 108 us -> 32.8 us
  other arithmetic: 58.1 us -> 1.11 us
  blocking collectives: 42.6 us -> 0 us
  Pallas kernels: 0 us -> 40.1 us
  between operations: 27.6 us -> 0.79 us
  local copies, waits for them, and re-layouts: 27.6 us -> 11 us
    ppermute x32 -> x6, waiting for transfers between devices: 556 us -> 8.28 us  [the longest x1 7.1 us: upward(): return lax.ppermute(x, 'seq', [(i, i + side) for i in range(side)])]
    ppermute x32 -> x6, starting transfers between devices: 108 us -> 8.24 us  [the longest x1 4.83 us: downward(): return lax.ppermute(x, 'seq', [(i + side, i) for i in range(side)])]
    all_to_all x0 -> x5, waiting for transfers between devices: none -> 84.9 us  [the longest x2 47.5 us: exchange(): return lax.all_to_all(x, 'seq', 0, 0, tiled=True)]
    dot_general x66 -> x0, matrix products: 81.9 us -> none  [the longest x9 12.8 us: scores_work(): jnp.einsum('thd,uhd->htu', query_two, keys_block, preferred_element_type=...]
    select_n x30 -> x0, other arithmetic: 43.7 us -> none  [hop(): jnp.where(position < mine, new, old)]
    pallas_call x0 -> x10, Pallas kernels: none -> 40.1 us  [call(): pl.pallas_call(kernel, out_shape=results, in_specs=[smem] * prefetch + [v...]
    unnamed x1 -> x0, blocking collectives: 40 us -> none
    all_to_all x0 -> x5, starting transfers between devices: none -> 24.5 us  [the longest x3 13 us: exchange_half(): return lax.all_to_all(x, 'seq', 0, 0, tiled=True, axis_index_groups=groups)]
  transfers between devices with their start and end apart: 34 -> 11, of which waited for: 30 -> 7; matrix products, arithmetic and copies ran while one was open for 12% -> 1% of each run, Pallas kernels for 0% -> 16%
where the time goes in v2:
time: 182 us; the launch traced here: 179 us
  waiting for transfers between devices  93.2 us (51%)
  Pallas kernels  40.1 us (22%)
  starting transfers between devices  32.8 us (18%)
  local copies, waits for them, and re-layouts  11 us (6%)
    all_to_all x2, waiting for transfers between devices, exchange(): return lax.all_to_all(x, 'seq', 0, 0, tiled=True)  47.5 us
    pallas_call x10, Pallas kernels, call(): pl.pallas_call(kernel, out_shape=results, in_specs=[smem] * prefetch + [v...  40.1 us
    all_to_all x3, waiting for transfers between devices, exchange_half(): return lax.all_to_all(x, 'seq', 0, 0, tiled=True, axis_index_groups=groups)  37.4 us
    all_to_all x3, starting transfers between devices, exchange_half(): return lax.all_to_all(x, 'seq', 0, 0, tiled=True, axis_index_groups=groups)  13 us
    all_to_all x2, starting transfers between devices, exchange(): return lax.all_to_all(x, 'seq', 0, 0, tiled=True)  11.5 us
    unnamed x32, local copies, waits for them, and re-layouts  10.3 us
    ppermute x1, waiting for transfers between devices, upward(): return lax.ppermute(x, 'seq', [(i, i + side) for i in range(side)])  7.1 us
    ppermute x1, starting transfers between devices, downward(): return lax.ppermute(x, 'seq', [(i + side, i) for i in range(side)])  4.83 us
  transfers between devices with their start and end apart: 11, of which 7 were waited for; matrix products, arithmetic and copies ran while one was open for 1% of the time, Pallas kernels for 16%

profile of v2, /device:TPU:16, one launch (start us, length us, event | category | flops | bytes accessed | tf_op | source)
XLA Modules:
  0.0 178.9 jit_solution(2526899750293383136)
XLA Ops:
  0.6 3.5 %shard_map.121 = bf16[16,384,128]{2,1,0:T(8,128)(2,1)} custom-call(bf16[128,16,128]{2,1,0:T(8,128)(2,1)} %refs_0_.3, bf16[128,16,128]{2,1,0:T(8,128)(2,1)} %refs_1_.3, bf16[128,16,128]{2,1,0:T(8,128)(2,1)} %refs_2_.3), custom_call_target="tpu_custom_call" | custom-call | flops 3000000000 | bytes 9000000 | tf_op jit(solution)/shard_map/pallas_call | solution.py:529
  4.1 7.2 %all-to-all-start.1 = ((bf16[16,384,128]{2,1,0:T(8,128)(2,1)}), bf16[16,384,128]{2,1,0:T(8,128)(2,1)S(1)}, u32[]{:S(2)}, u32[]{:S(2)}) async-start(bf16[16,384,128]{2,1,0:T(8,128)(2,1)} %shard_map.121), calls=%async_computation.1 | async-start | bytes 3145728 | tf_op jit(solution)/shard_map/all_to_all | solution.py:590
  11.4 3.5 %shard_map.119 = bf16[16,400,128]{2,1,0:T(8,128)(2,1)} custom-call(bf16[128,16,128]{2,1,0:T(8,128)(2,1)} %refs_0_.2, bf16[128,16,128]{2,1,0:T(8,128)(2,1)} %refs_1_.2, bf16[128,16,128]{2,1,0:T(8,128)(2,1)} %refs_2_.2, f32[16,128]{1,0:T(8,128)S(1)} %copy-done.4), custom_call_target="tpu_custom_call" | custom-call | flops 3000000000 | bytes 9000000 | tf_op jit(solution)/shard_map/pallas_call | solution.py:529
  14.9 32.7 %all-to-all-done.1.first_ref = bf16[16,384,128]{2,1,0:T(8,128)(2,1)S(1)} async-done(((bf16[16,384,128]{2,1,0:T(8,128)(2,1)}), bf16[16,384,128]{2,1,0:T(8,128)(2,1)S(1)}, u32[]{:S(2)}, u32[]{:S(2)}) %all-to-all-start.1) | async-done | bytes 1572896 | tf_op jit(solution)/shard_map/all_to_all | solution.py:590
  47.6 3.6 %all-to-all-start = ((bf16[16,400,128]{2,1,0:T(8,128)(2,1)}), bf16[16,400,128]{2,1,0:T(8,128)(2,1)S(1)}, u32[]{:S(2)}, u32[]{:S(2)}) async-start(bf16[16,400,128]{2,1,0:T(8,128)(2,1)} %shard_map.119), calls=%async_computation | async-start | bytes 3276800 | tf_op jit(solution)/shard_map/all_to_all | solution.py:596
  51.4 6.3 %shard_map.122 = (f32[4,512]{1,0:T(4,128)S(1)}, f32[1024,128]{1,0:T(8,128)S(1)}, bf16[1024,128]{1,0:T(8,128)(2,1)}) custom-call(s32[17]{0:T(128)S(1)} %pad_add_fusion.info_ref, bf16[16,384,128]{2,1,0:T(8,128)(2,1)S(1)} %all-to-all-done.1.first_ref), custom_call_target="tpu_custom_call" | custom-call | flops 6000000000 | bytes 18000000 | tf_op jit(solution)/shard_map/pallas_call | solution.py:529
  58.6 1.9 %collective-permute-start.1 = (bf16[1024,128]{1,0:T(8,128)(2,1)}, bf16[1024,128]{1,0:T(8,128)(2,1)S(1)}, u32[]{:S(2)}, u32[]{:S(2)}) collective-permute-start(bf16[1024,128]{1,0:T(8,128)(2,1)} %get-tuple-element.22), channel_id=1, source_target_pairs={{0,16},{2,18},{4,20},{6,22},{8,24},{10,26},{12,28},{14,30},{16,0},... | collective-permute-start | bytes 786440 | tf_op jit(solution)/shard_map/ppermute | solution.py:611
  60.5 13.1 %all-to-all-done.second_ref = bf16[16,400,128]{2,1,0:T(8,128)(2,1)S(1)} async-done(((bf16[16,400,128]{2,1,0:T(8,128)(2,1)}), bf16[16,400,128]{2,1,0:T(8,128)(2,1)S(1)}, u32[]{:S(2)}, u32[]{:S(2)}) %all-to-all-start) | async-done | bytes 1638432 | tf_op jit(solution)/shard_map/all_to_all | solution.py:596
  74.3 1.5 collective-permute-start
  75.8 7.1 %collective-permute-done.incoming_ref = f32[2,128,128]{2,1,0:T(8,128)S(1)} collective-permute-done((f32[2,128,128]{2,1,0:T(8,128)S(1)}, f32[2,128,128]{2,1,0:T(8,128)S(1)}, u32[]{:S(2)}, u32[]{:S(2)}) %collective-permute-start) | collective-permute-done | bytes 131104 | tf_op jit(solution)/shard_map/ppermute | solution.py:601
  82.9 6.2 %shard_map.123 = (f32[2,1024,128]{2,1,0:T(8,128)S(1)}, bf16[1024,128]{1,0:T(8,128)(2,1)S(1)}, bf16[2,8,128,128]{3,2,1,0:T(8,128)(2,1)S(1)}, f32[16,128]{1,0:T(8,128)S(1)}) custom-call(s32[17]{0:T(128)S(1)} %pad_add_fusion.info_ref, bf16[16,400,128]{2,1,0:T(8,128)(2,1)S(1)} %all-to-all-done.second_ref, f32[2,128,128]{2,1,0:T(8,128)S(1)} %collective-permute-done.incoming_ref, ...), custom_call_target="tpu_custom_call" | custom-call | flops 4000000000 | bytes 12000000 | tf_op jit(solution)/shard_map/pallas_call | solution.py:529
  92.2 5.8 %all-to-all-start.2 = ((f32[8,16,128]{2,1,0:T(8,128)}), f32[8,16,128]{2,1,0:T(8,128)}, u32[]{:S(2)}, u32[]{:S(2)}) async-start(f32[8,16,128]{2,1,0:T(8,128)} %broadcast_in_dim.16), calls=%async_computation.2 | async-start | bytes 131072 | tf_op jit(solution)/shard_map/all_to_all | solution.py:596
  98.0 5.9 %all-to-all-done.2 = f32[8,16,128]{2,1,0:T(8,128)} async-done(((f32[8,16,128]{2,1,0:T(8,128)}), f32[8,16,128]{2,1,0:T(8,128)}, u32[]{:S(2)}, u32[]{:S(2)}) %all-to-all-start.2) | async-done | bytes 65568 | tf_op jit(solution)/shard_map/all_to_all | solution.py:596
  108.3 1.9 %shard_map.124 = f32[2,128,128]{2,1,0:T(8,128)S(1)} custom-call(s32[17]{0:T(128)S(1)} %pad_add_fusion.info_ref, bf16[16,400,128]{2,1,0:T(8,128)(2,1)S(1)} %all-to-all-done.second_ref, f32[2,1024,128]{2,1,0:T(8,128)S(1)} %copy-done.6, f32[16,128]{1,0:T(8,128)S(1)} %add.3.sums_ref, f32[1024,128]{1,0:T(8,128)S(1)} %copy-done.11, ...), custom_call_target="tpu_custom_call" | custom-call | flops 2000000000 | bytes 6000000 | tf_op jit(solution)/shard_map/pallas_call | solution.py:529
  110.2 4.8 %collective-permute-start.3 = (f32[2,128,128]{2,1,0:T(8,128)S(1)}, f32[2,128,128]{2,1,0:T(8,128)S(1)}, u32[]{:S(2)}, u32[]{:S(2)}) collective-permute-start(f32[2,128,128]{2,1,0:T(8,128)S(1)} %shard_map.124), channel_id=1, source_target_pairs={{16,0},{18,2},{20,4},{22,6},{24,8},{26,10},{28,12},{30,14},{17,1},... | collective-permute-start | bytes 393224 | tf_op jit(solution)/shard_map/ppermute | solution.py:606
  115.1 8.0 %shard_map.125 = bf16[16,256,128]{2,1,0:T(8,128)(2,1)S(1)} custom-call(s32[17]{0:T(128)S(1)} %pad_add_fusion.info_ref, bf16[16,384,128]{2,1,0:T(8,128)(2,1)S(1)} %all-to-all-done.1.first_ref, f32[4,512]{1,0:T(4,128)S(1)} %get-tuple-element.25.mass_ref, f32[2,1024,128]{2,1,0:T(8,128)S(1)} %copy-done.7, bf16[1024,128]{1,0:T(8,128)(2,1)} %collective-permute-done.4.other_ref, ...), custom_call_target="tpu_custom_call" | custom-call | flops 7000000000 | bytes 21000000 | tf_op jit(solution)/shard_map/pallas_call | solution.py:529
  124.7 4.3 %all-to-all-start.3 = ((bf16[16,256,128]{2,1,0:T(8,128)(2,1)}), bf16[16,256,128]{2,1,0:T(8,128)(2,1)S(1)}, u32[]{:S(2)}, u32[]{:S(2)}) async-start(bf16[16,256,128]{2,1,0:T(8,128)(2,1)} %copy-done), calls=%async_computation.3 | async-start | bytes 2097152 | tf_op jit(solution)/shard_map/all_to_all | solution.py:590
  130.0 1.2 copy-done.8
  132.2 6.1 %shard_map.126 = bf16[16,384,128]{2,1,0:T(8,128)(2,1)} custom-call(s32[17]{0:T(128)S(1)} %pad_add_fusion.info_ref, bf16[16,400,128]{2,1,0:T(8,128)(2,1)S(1)} %all-to-all-done.second_ref, f32[2,1024,128]{2,1,0:T(8,128)S(1)} %copy-done.8, bf16[2,8,128,128]{3,2,1,0:T(8,128)(2,1)S(1)} %copy-done.14, f32[16,128]{1,0:T(8,128)S(1)} %add.3.sums_ref, ...), custom_call_target="tpu_custom_call" | custom-call | flops 5000000000 | bytes 15000000 | tf_op jit(solution)/shard_map/pallas_call | solution.py:529
  138.3 14.8 %all-to-all-done.3.in_ref = bf16[16,256,128]{2,1,0:T(8,128)(2,1)S(1)} async-done(((bf16[16,256,128]{2,1,0:T(8,128)(2,1)}), bf16[16,256,128]{2,1,0:T(8,128)(2,1)S(1)}, u32[]{:S(2)}, u32[]{:S(2)}) %all-to-all-start.3) | async-done | bytes 1048608 | tf_op jit(solution)/shard_map/all_to_all | solution.py:590
  153.1 3.6 %all-to-all-start.4 = ((bf16[16,384,128]{2,1,0:T(8,128)(2,1)}), bf16[16,384,128]{2,1,0:T(8,128)(2,1)S(1)}, u32[]{:S(2)}, u32[]{:S(2)}) async-start(bf16[16,384,128]{2,1,0:T(8,128)(2,1)} %shard_map.126), calls=%async_computation.4 | async-start | bytes 3145728 | tf_op jit(solution)/shard_map/all_to_all | solution.py:596
  156.7 1.8 shard_map.128
  158.5 18.3 %all-to-all-done.4.in_ref = bf16[16,384,128]{2,1,0:T(8,128)(2,1)S(1)} async-done(((bf16[16,384,128]{2,1,0:T(8,128)(2,1)}), bf16[16,384,128]{2,1,0:T(8,128)(2,1)S(1)}, u32[]{:S(2)}, u32[]{:S(2)}) %all-to-all-start.4) | async-done | bytes 1572896 | tf_op jit(solution)/shard_map/all_to_all | solution.py:596
  176.8 2.1 %shard_map.127 = (f32[128,16,128]{2,1,0:T(8,128)}, f32[128,16,128]{2,1,0:T(8,128)}, f32[128,16,128]{2,1,0:T(8,128)}) custom-call(bf16[16,384,128]{2,1,0:T(8,128)(2,1)S(1)} %all-to-all-done.4.in_ref), custom_call_target="tpu_custom_call" | custom-call | flops 3000000000 | bytes 9000000 | tf_op jit(solution)/shard_map/pallas_call | solution.py:529
  (46 shorter events, 12.7 us)
Async XLA Ops:
  4.1 7.2 %copy-start.4 = (f32[16,128]{1,0:T(8,128)S(1)}, f32[16,128]{1,0:T(8,128)}, u32[]{:S(2)}) copy-start(f32[16,128]{1,0:T(8,128)} %refs_3_.1) | copy-start | bytes 24580
  4.1 43.5 %all-to-all-start.1 = ((bf16[16,384,128]{2,1,0:T(8,128)(2,1)}), bf16[16,384,128]{2,1,0:T(8,128)(2,1)S(1)}, u32[]{:S(2)}, u32[]{:S(2)}) async-start(bf16[16,384,128]{2,1,0:T(8,128)(2,1)} %shard_map.121), calls=%async_computation.1 | async-start | bytes 3145728 | tf_op jit(solution)/shard_map/all_to_all | solution.py:590
  14.9 36.3 %copy-start.15 = (s32[16]{0:T(128)S(1)}, s32[16]{0:T(128)}, u32[]{:S(2)}) copy-start(s32[16]{0:T(128)} %param.15) | copy-start | bytes 196
  47.6 26.1 %all-to-all-start = ((bf16[16,400,128]{2,1,0:T(8,128)(2,1)}), bf16[16,400,128]{2,1,0:T(8,128)(2,1)S(1)}, u32[]{:S(2)}, u32[]{:S(2)}) async-start(bf16[16,400,128]{2,1,0:T(8,128)(2,1)} %shard_map.119), calls=%async_computation | async-start | bytes 3276800 | tf_op jit(solution)/shard_map/all_to_all | solution.py:596
  57.8 0.8 copy-start.9
  58.6 24.3 %collective-permute-start.1 = (bf16[1024,128]{1,0:T(8,128)(2,1)}, bf16[1024,128]{1,0:T(8,128)(2,1)S(1)}, u32[]{:S(2)}, u32[]{:S(2)}) collective-permute-start(bf16[1024,128]{1,0:T(8,128)(2,1)} %get-tuple-element.22), channel_id=1, source_target_pairs={{0,16},{2,18},{4,20},{6,22},{8,24},{10,26},{12,28},{14,30},{16,0},... | collective-permute-start | bytes 786440 | tf_op jit(solution)/shard_map/ppermute | solution.py:611
  73.6 9.2 %copy-start.10 = (f32[1024,128]{1,0:T(8,128)S(1)}, f32[1024,128]{1,0:T(8,128)}, u32[]{:S(2)}) copy-start(f32[1024,128]{1,0:T(8,128)} %copy-done.9) | copy-start | bytes 1572868
  74.3 8.6 %collective-permute-start = (f32[2,128,128]{2,1,0:T(8,128)S(1)}, f32[2,128,128]{2,1,0:T(8,128)S(1)}, u32[]{:S(2)}, u32[]{:S(2)}) collective-permute-start(f32[2,128,128]{2,1,0:T(8,128)S(1)} %shard_map.120), channel_id=1, source_target_pairs={{0,16},{2,18},{4,20},{6,22},{8,24},{10,26},{12,28},{14,30},{1,17},... | collective-permute-start | bytes 393224 | tf_op jit(solution)/shard_map/ppermute | solution.py:601
  89.8 1.0 copy-start.5
  92.2 11.7 %all-to-all-start.2 = ((f32[8,16,128]{2,1,0:T(8,128)}), f32[8,16,128]{2,1,0:T(8,128)}, u32[]{:S(2)}, u32[]{:S(2)}) async-start(f32[8,16,128]{2,1,0:T(8,128)} %broadcast_in_dim.16), calls=%async_computation.2 | async-start | bytes 131072 | tf_op jit(solution)/shard_map/all_to_all | solution.py:596
  98.0 17.0 %collective-permute-start.4 = (bf16[1024,128]{1,0:T(8,128)(2,1)}, bf16[1024,128]{1,0:T(8,128)(2,1)}, u32[]{:S(2)}, u32[]{:S(2)}) collective-permute-start(bf16[1024,128]{1,0:T(8,128)(2,1)} %copy-done.1), channel_id=1, source_target_pairs={{0,16},{2,18},{4,20},{6,22},{8,24},{10,26},{12,28},{14,30},{16,0},... | collective-permute-start | bytes 786440 | tf_op jit(solution)/shard_map/ppermute | solution.py:611
  104.8 1.2 collective-permute-start.2
  106.0 9.0 %collective-permute-start.5 = (f32[8,128]{1,0:T(8,128)S(1)}, f32[8,128]{1,0:T(8,128)S(1)}, u32[]{:S(2)}, u32[]{:S(2)}) collective-permute-start(f32[8,128]{1,0:T(8,128)S(1)} %slice.4), channel_id=1, source_target_pairs={{0,16},{2,18},{4,20},{6,22},{8,24},{10,26},{12,28},{14,30},{16,0},... | collective-permute-start | bytes 12296 | tf_op jit(solution)/shard_map/ppermute | solution.py:611
  106.0 1.2 copy-start.6
  107.2 1.0 copy-start.11
  108.3 6.8 %copy-start.7 = (f32[2,1024,128]{2,1,0:T(8,128)S(1)}, f32[2,1024,128]{2,1,0:T(8,128)}, u32[]{:S(2)}) copy-start(f32[2,1024,128]{2,1,0:T(8,128)} %copy-done.5) | copy-start | bytes 3145732
  110.2 13.9 %collective-permute-start.3 = (f32[2,128,128]{2,1,0:T(8,128)S(1)}, f32[2,128,128]{2,1,0:T(8,128)S(1)}, u32[]{:S(2)}, u32[]{:S(2)}) collective-permute-start(f32[2,128,128]{2,1,0:T(8,128)S(1)} %shard_map.124), channel_id=1, source_target_pairs={{16,0},{18,2},{20,4},{22,6},{24,8},{26,10},{28,12},{30,14},{17,1},... | collective-permute-start | bytes 393224 | tf_op jit(solution)/shard_map/ppermute | solution.py:606
  123.1 1.0 copy-start
  124.1 5.0 %copy-start.12 = (f32[1024,128]{1,0:T(8,128)S(1)}, f32[1024,128]{1,0:T(8,128)}, u32[]{:S(2)}) copy-start(f32[1024,128]{1,0:T(8,128)} %copy-done.9) | copy-start | bytes 1572868
  124.7 28.4 %all-to-all-start.3 = ((bf16[16,256,128]{2,1,0:T(8,128)(2,1)}), bf16[16,256,128]{2,1,0:T(8,128)(2,1)S(1)}, u32[]{:S(2)}, u32[]{:S(2)}) async-start(bf16[16,256,128]{2,1,0:T(8,128)(2,1)} %copy-done), calls=%async_computation.3 | async-start | bytes 2097152 | tf_op jit(solution)/shard_map/all_to_all | solution.py:590
  129.0 0.9 copy-start.3
  130.0 1.2 copy-start.8
  131.2 1.0 copy-start.14
  153.1 23.7 %all-to-all-start.4 = ((bf16[16,384,128]{2,1,0:T(8,128)(2,1)}), bf16[16,384,128]{2,1,0:T(8,128)(2,1)S(1)}, u32[]{:S(2)}, u32[]{:S(2)}) async-start(bf16[16,384,128]{2,1,0:T(8,128)(2,1)} %shard_map.126), calls=%async_computation.4 | async-start | bytes 3145728 | tf_op jit(solution)/shard_map/all_to_all | solution.py:596
  (3 other events, 2.2 us)

commit v3 on v2

--- a/solution.py
+++ b/solution.py
@@ -241,10 +241,14 @@
     return dot_nt(ones, high) + dot_nt(ones, low)
 
 
+def decay_column(parts):
+    log_row = jnp.sum(parts.astype(f32), axis=0, keepdims=True)
+    return jnp.sum(jnp.where(lower_mask(BLOCK), log_row, 0.0), axis=1, keepdims=True)
+
+
 def chunk_decays(parts):
     lower = lower_mask(BLOCK)
-    log_row = jnp.sum(parts.astype(f32), axis=0, keepdims=True)
-    column = jnp.sum(jnp.where(lower, log_row, 0.0), axis=1, keepdims=True)
+    column = decay_column(parts)
     upper = lax.broadcasted_iota(jnp.int32, (BLOCK, BLOCK), 0) <= lax.broadcasted_iota(
         jnp.int32, (BLOCK, BLOCK), 1
     )
@@ -305,37 +309,49 @@
     )
 
 
-def linear_forward(
-    heads, info_ref, second_ref, incoming_ref, kept_ref, other_ref,
-    raw_ref, sent_ref, state_ref, sums_ref,
+def linear_local(heads, second_ref, raw_ref):
+    chunks, width = (second_ref.shape[0] // heads, second_ref.shape[2])
+
+    def chunk(c, states):
+        following = []
+        for head in range(heads):
+            q, k, v, (weights, grow, tail, whole) = lightning_piece(second_ref, c * heads + head)
+            prob = (dot_nt(q, k) * weights).astype(bf16)
+            raw = dot(prob, v) + grow * dot(q, states[head].astype(bf16))
+            raw_ref[head, block_rows(c), :] = raw
+            following.append(
+                whole * states[head] + dot_tn(k, (v.astype(f32) * tail).astype(bf16))
+            )
+        return tuple(following)
+
+    over_chunks(chunks, chunk, (jnp.zeros((width, width), f32),) * heads)
+
+
+def linear_output(
+    heads, info_ref, second_ref, incoming_ref, local_ref, kept_ref, other_ref, raw_ref, sent_ref, sums_ref
 ):
     chunks = second_ref.shape[0] // heads
     half = info_ref[info_ref.shape[0] - 1]
-
-    def chunk(c, states):
-        following = []
-        squares, cross = (0.0, 0.0)
+    incoming = [incoming_ref[head].astype(bf16) for head in range(heads)]
+    carried = [jnp.ones((1, 1), f32)] * heads
+    for c in range(chunks):
+        here = block_rows(c)
         raws = []
+        squares, products = (0.0, 0.0)
         for head in range(heads):
-            q, k, v, (weights, grow, tail, whole) = lightning_piece(second_ref, c * heads + head)
-            prob = (dot_nt(q, k) * weights).astype(bf16)
-            state_low = states[head].astype(bf16)
-            raw = dot(prob, v) + grow * dot(q, state_low)
-            state_ref[head, c] = state_low
-            following.append(
-                whole * states[head] + dot_tn(k, (v.astype(f32) * tail).astype(bf16))
-            )
-            raw_ref[head, block_rows(c), :] = raw
-            raws.append(raw)
+            place = c * heads + head
+            logs = decay_column(second_ref[place, second_ref.shape[1] - PART_ROWS :, :])
+            outer = dot(second_ref[place, 0:BLOCK, :], incoming[head])
+            raw = local_ref[head, here, :] + (carried[head] * jnp.exp(logs)) * outer
+            carried[head] = carried[head] * jnp.exp(logs[BLOCK - 1 : BLOCK, :])
             grad = value_gradient(half, kept_ref, other_ref, head, c)
-            squares = squares + row_sums(raw * raw)[0:1, :]
-            cross = cross + row_sums(raw * grad)[0:1, :]
-        sent_ref[block_rows(c), :] = jnp.where(half == 0, raws[1], raws[0]).astype(bf16)
-        sums_ref[c : c + 1, :] = squares
-        sums_ref[chunks + c : chunks + c + 1, :] = cross
-        return tuple(following)
-
-    over_chunks(chunks, chunk, tuple(incoming_ref[head] for head in range(heads)))
+            squares = squares + raw * raw
+            products = products + raw * grad
+            raws.append(raw.astype(bf16))
+            raw_ref[head, here, :] = raws[head]
+        sent_ref[here, :] = jnp.where(half == 0, raws[1], raws[0])
+        sums_ref[c : c + 1, :] = row_sums(squares)[0:1, :]
+        sums_ref[chunks + c : chunks + c + 1, :] = row_sums(products)[0:1, :]
 
 
 def column(columns, c):
@@ -363,7 +379,7 @@
         for head in range(heads):
             q, _, _, (_, grow, _, whole) = lightning_piece(second_ref, c * heads + head)
             grad = column(inverse, c) * value_gradient(half, kept_ref, other_ref, head, c)
-            grad = grad - raw_ref[head, block_rows(c), :] * column(cross, c)
+            grad = grad - raw_ref[head, block_rows(c), :].astype(f32) * column(cross, c)
             following.append(whole * grads[head] + dot_tn(q, (grad * grow).astype(bf16)))
         return tuple(following)
 
@@ -373,10 +389,22 @@
 
 
 def linear_backward(
-    features, heads, info_ref, second_ref, raw_ref, state_ref, sums_ref, kept_ref, other_ref, later_ref,
-    out_ref,
+    features, heads, info_ref, second_ref, raw_ref, incoming_ref, sums_ref, kept_ref, other_ref, later_ref,
+    out_ref, state_s,
 ):
     chunks = second_ref.shape[0] // heads
+
+    def before(c, states):
+        following = []
+        for head in range(heads):
+            _, k, v, (_, _, tail, whole) = lightning_piece(second_ref, c * heads + head)
+            state_s[head, c] = states[head].astype(bf16)
+            following.append(
+                whole * states[head] + dot_tn(k, (v.astype(f32) * tail).astype(bf16))
+            )
+        return tuple(following)
+
+    over_chunks(chunks, before, tuple(incoming_ref[head] for head in range(heads)))
     half = info_ref[info_ref.shape[0] - 1]
     inverse, cross = norm_columns(features, sums_ref)
 
@@ -386,12 +414,12 @@
             place = c * heads + head
             q, k, v, (weights, grow, tail, whole) = lightning_piece(second_ref, place)
             grad = column(inverse, c) * value_gradient(half, kept_ref, other_ref, head, c)
-            grad = grad - raw_ref[head, block_rows(c), :] * column(cross, c)
+            grad = grad - raw_ref[head, block_rows(c), :].astype(f32) * column(cross, c)
             grad_low = grad.astype(bf16)
             prob = (dot_nt(q, k) * weights).astype(bf16)
             grad_score = (dot_nt(grad_low, v) * weights).astype(bf16)
             state_low = grads[head].astype(bf16)
-            query_grad = dot(grad_score, k) + grow * dot_nt(grad_low, state_ref[head, c])
+            query_grad = dot(grad_score, k) + grow * dot_nt(grad_low, state_s[head, c])
             key_grad = dot_tn(grad_score, q) + tail * dot_nt(v, state_low)
             value_grad = dot_tn(prob, grad_low) + tail * dot(k, state_low)
             following.append(whole * grads[head] + dot_tn(q, (grad * grow).astype(bf16)))
@@ -413,7 +441,7 @@
         need = end - info_ref[TOGETHER * group]
         least = 0
         for blocks in window_sizes(chunks):
-            begin = pl.multiple_of((end - blocks) * BLOCK, 2 * BLOCK)
+            begin = end - blocks
             pl.when((need > least) & (need <= blocks))(partial(window, group, begin, blocks))
             least = blocks
         return carry
@@ -436,23 +464,23 @@
     return scores, (u_pos >= lowest) & (u_pos <= group * GROUP + lane)
 
 
-def group_rows(group):
-    return pl.ds(pl.multiple_of(group * GROUP, GROUP), GROUP)
-
-
-def softmax_masses(info_ref, first_ref, mass_ref, kept_ref, sent_ref, key_s, query_s, grad_s, value_grad_s):
+def blocks_of(first_ref, place, block, count):
+    rows = first_ref[pl.ds(block, count), place * BLOCK : (place + 1) * BLOCK, :]
+    return rows.reshape(count * BLOCK, first_ref.shape[2])
+
+
+def softmax_masses(info_ref, first_ref, mass_ref, kept_ref, sent_ref, value_grad_s):
     chunks, width = (first_ref.shape[0], first_ref.shape[2])
-    for c in range(chunks):
-        here = block_rows(c)
-        query_s[here, :] = first_ref[c, 0:BLOCK, :]
-        key_s[here, :] = first_ref[c, BLOCK : 2 * BLOCK, :]
-        grad_s[here, :] = first_ref[c, 2 * BLOCK :, :]
-        value_grad_s[here, :] = jnp.zeros((BLOCK, width), f32)
+    value_grad_s[...] = jnp.zeros_like(value_grad_s)
 
     def window(group, begin, blocks):
-        rows = pl.ds(begin, blocks * BLOCK)
+        rows = pl.ds(pl.multiple_of(begin * BLOCK, 2 * BLOCK), blocks * BLOCK)
         scores, allowed = window_scores(
-            info_ref, key_s[rows, :], query_s[group_rows(group), :], group, begin
+            info_ref,
+            blocks_of(first_ref, 1, begin, blocks),
+            blocks_of(first_ref, 0, TOGETHER * group, TOGETHER),
+            group,
+            begin * BLOCK,
         )
         scores = jnp.where(allowed, scores, floor_score)
         peak = jnp.max(scores, axis=0, keepdims=True)
@@ -460,7 +488,7 @@
         total = jnp.sum(mass, axis=0, keepdims=True)
         mass_ref[pl.ds(group, 1), :] = peak + jnp.log2(total)
         prob = (mass * (1.0 / total)).astype(bf16)
-        value_grad_s[rows, :] += dot(prob, grad_s[group_rows(group), :])
+        value_grad_s[rows, :] += dot(prob, blocks_of(first_ref, 2, TOGETHER * group, TOGETHER))
 
     by_window(info_ref, chunks, window)
     half = info_ref[info_ref.shape[0] - 1]
@@ -473,7 +501,7 @@
 
 def softmax_grads(
     features, info_ref, first_ref, mass_ref, raw_ref, other_ref, sums_ref, other_sums_ref, out_ref,
-    key_s, key_t_s, value_s, value_t_s, query_s, grad_s, key_grad_s,
+    key_t_s, value_s, value_t_s, key_grad_s,
 ):
     chunks, width = (first_ref.shape[0], first_ref.shape[2])
     side = chunks // 2
@@ -486,24 +514,22 @@
         here = block_rows(c)
         there = block_rows(c % side)
         own = jnp.where(half == 0, raw_ref[0, there, :], raw_ref[1, there, :])
-        own = own * column(inverse, c % side)
+        own = own.astype(f32) * column(inverse, c % side)
         other = other_ref[there, :].astype(f32) * column(other_inverse, c % side)
         v = jnp.where(half == c // side, own, other).astype(bf16)
         value_s[here, :] = v
         value_t_s[:, here] = v.T
-        query_s[here, :] = first_ref[c, 0:BLOCK, :]
-        key_s[here, :] = first_ref[c, BLOCK : 2 * BLOCK, :]
         key_t_s[:, here] = first_ref[c, BLOCK : 2 * BLOCK, :].T
-        grad_s[here, :] = first_ref[c, 2 * BLOCK :, :]
         key_grad_s[here, :] = jnp.zeros((BLOCK, width), f32)
 
     def window(group, begin, blocks):
-        rows = pl.ds(begin, blocks * BLOCK)
-        queries = query_s[group_rows(group), :]
-        scores, allowed = window_scores(info_ref, key_s[rows, :], queries, group, begin)
+        rows = pl.ds(pl.multiple_of(begin * BLOCK, 2 * BLOCK), blocks * BLOCK)
+        queries = blocks_of(first_ref, 0, TOGETHER * group, TOGETHER)
+        keys = blocks_of(first_ref, 1, begin, blocks)
+        scores, allowed = window_scores(info_ref, keys, queries, group, begin * BLOCK)
         scores = jnp.where(allowed, scores - mass_ref[pl.ds(group, 1), :], floor_score)
         prob = jnp.exp2(scores)
-        g_t = grad_s[group_rows(group), :].T
+        g_t = blocks_of(first_ref, 2, TOGETHER * group, TOGETHER).T
         attended = dot(value_t_s[:, rows], prob.astype(bf16))
         delta = jnp.sum(g_t.astype(f32) * attended, axis=0, keepdims=True)
         grad_prob = dot(value_s[rows, :], g_t)
@@ -642,9 +668,9 @@
         )[0]
 
     first = exchange(packed(paired, 3 * length, (query_two, key_two, out_grad)))
-    second = exchange_half(
-        packed(straight, 3 * length + PART_ROWS, (query_one, key_one, value_one), log_decay)
-    )
+    second = packed(straight, 3 * length + PART_ROWS, (query_one, key_one, value_one), log_decay)
+    second, first = lax.optimization_barrier((second, first))
+    second = exchange_half(second)
     half_rows = (half_length, width)
     full_rows = (shards * length, width)
     masses, grad_kept, grad_sent = call(
@@ -655,7 +681,7 @@
             (half_rows, f32),
             (half_rows, bf16),
         ],
-        [(full_rows, bf16), (full_rows, bf16), (full_rows, bf16), (full_rows, f32)],
+        [(full_rows, f32)],
         info,
         first,
         prefetch=1,
@@ -664,19 +690,17 @@
     state_shape = (heads, width, width)
     (state,) = call(partial(linear_state, heads), 1, [(state_shape, f32)], [], second)
     incoming = upward(state)
-    raw, raw_sent, states, sums = call(
-        partial(linear_forward, heads),
-        4,
-        [
-            ((heads, half_length, width), f32),
-            (half_rows, bf16),
-            ((heads, side, width, width), bf16),
-            ((2 * side, BLOCK), f32),
-        ],
+    head_rows = (heads, half_length, width)
+    (local,) = call(partial(linear_local, heads), 4, [(head_rows, f32)], [], second)
+    raw, raw_sent, sums = call(
+        partial(linear_output, heads),
+        2,
+        [(head_rows, bf16), (half_rows, bf16), ((2 * side, BLOCK), f32)],
         [],
         info,
         second,
         incoming,
+        local,
         grad_kept,
         grad_other,
         prefetch=1,
@@ -690,12 +714,9 @@
         7,
         [((shards, 2 * BLOCK, width), bf16)],
         [
-            (full_rows, bf16),
             ((width, shards * length), bf16),
             (full_rows, bf16),
             ((width, shards * length), bf16),
-            (full_rows, bf16),
-            (full_rows, bf16),
             (full_rows, f32),
         ],
         info,
@@ -727,11 +748,11 @@
         partial(linear_backward, features, heads),
         5,
         [((heads_here, 3 * BLOCK, width), bf16)],
-        [],
+        [((heads, side, width, width), bf16)],
         info,
         second,
         raw,
-        states,
+        incoming,
         sums,
         grad_kept,
         grad_other,

time: 182 us -> 177 us (0.973)
  Pallas kernels: 40.1 us -> 38 us
    ppermute x1, waiting for transfers between devices: 7.1 us -> 4.39 us  [upward(): return lax.ppermute(x, 'seq', [(i, i + side) for i in range(side)])]
    pallas_call x10 -> x11, Pallas kernels: 40.1 us -> 38 us  [call(): pl.pallas_call(kernel, out_shape=results, in_specs=[smem] * prefetch + [v...]
  transfers between devices with their start and end apart: 11 -> 11, of which waited for: 7 -> 7; matrix products, arithmetic and copies ran while one was open for 1% -> 1% of each run, Pallas kernels for 16% -> 17%
where the time goes in v3:
time: 177 us; the launch traced here: 174 us
  waiting for transfers between devices  91.6 us (52%)
  Pallas kernels  38 us (21%)
  starting transfers between devices  32.9 us (19%)
  local copies, waits for them, and re-layouts  9.51 us (5%)
    all_to_all x2, waiting for transfers between devices, exchange(): return lax.all_to_all(x, 'seq', 0, 0, tiled=True)  47.9 us
    all_to_all x3, waiting for transfers between devices, exchange_half(): return lax.all_to_all(x, 'seq', 0, 0, tiled=True, axis_index_groups=groups)  38.2 us
    pallas_call x11, Pallas kernels, call(): pl.pallas_call(kernel, out_shape=results, in_specs=[smem] * prefetch + [v...  38 us
    all_to_all x3, starting transfers between devices, exchange_half(): return lax.all_to_all(x, 'seq', 0, 0, tiled=True, axis_index_groups=groups)  13 us
    all_to_all x2, starting transfers between devices, exchange(): return lax.all_to_all(x, 'seq', 0, 0, tiled=True)  11.6 us
    unnamed x32, local copies, waits for them, and re-layouts  8.87 us
    ppermute x1, starting transfers between devices, downward(): return lax.ppermute(x, 'seq', [(i + side, i) for i in range(side)])  4.83 us
    ppermute x1, waiting for transfers between devices, upward(): return lax.ppermute(x, 'seq', [(i, i + side) for i in range(side)])  4.39 us
  transfers between devices with their start and end apart: 11, of which 7 were waited for; matrix products, arithmetic and copies ran while one was open for 1% of the time, Pallas kernels for 17%

profile of v3, /device:TPU:16, one launch (start us, length us, event | category | flops | bytes accessed | tf_op | source)
XLA Modules:
  0.0 173.9 jit_solution(17597096499838002851)
XLA Ops:
  0.6 3.5 %shard_map.120 = bf16[16,384,128]{2,1,0:T(8,128)(2,1)} custom-call(bf16[128,16,128]{2,1,0:T(8,128)(2,1)} %refs_0_.3, bf16[128,16,128]{2,1,0:T(8,128)(2,1)} %refs_1_.3, bf16[128,16,128]{2,1,0:T(8,128)(2,1)} %refs_2_.3), custom_call_target="tpu_custom_call" | custom-call | flops 3000000000 | bytes 9000000 | tf_op jit(solution)/shard_map/pallas_call | solution.py:555
  4.1 7.2 %all-to-all-start = ((bf16[16,384,128]{2,1,0:T(8,128)(2,1)}), bf16[16,384,128]{2,1,0:T(8,128)(2,1)S(1)}, u32[]{:S(2)}, u32[]{:S(2)}) async-start(bf16[16,384,128]{2,1,0:T(8,128)(2,1)} %shard_map.120), calls=%async_computation | async-start | bytes 3145728 | tf_op jit(solution)/shard_map/all_to_all | solution.py:616
  11.4 3.5 %shard_map.119 = bf16[16,400,128]{2,1,0:T(8,128)(2,1)} custom-call(bf16[128,16,128]{2,1,0:T(8,128)(2,1)} %refs_0_.2, bf16[128,16,128]{2,1,0:T(8,128)(2,1)} %refs_1_.2, bf16[128,16,128]{2,1,0:T(8,128)(2,1)} %refs_2_.2, f32[16,128]{1,0:T(8,128)S(1)} %copy-done.6), custom_call_target="tpu_custom_call" | custom-call | flops 3000000000 | bytes 9000000 | tf_op jit(solution)/shard_map/pallas_call | solution.py:555
  14.9 32.7 %all-to-all-done.first_ref = bf16[16,384,128]{2,1,0:T(8,128)(2,1)S(1)} async-done(((bf16[16,384,128]{2,1,0:T(8,128)(2,1)}), bf16[16,384,128]{2,1,0:T(8,128)(2,1)S(1)}, u32[]{:S(2)}, u32[]{:S(2)}) %all-to-all-start) | async-done | bytes 1572896 | tf_op jit(solution)/shard_map/all_to_all | solution.py:616
  47.6 3.6 %all-to-all-start.1 = ((bf16[16,400,128]{2,1,0:T(8,128)(2,1)}), bf16[16,400,128]{2,1,0:T(8,128)(2,1)S(1)}, u32[]{:S(2)}, u32[]{:S(2)}) async-start(bf16[16,400,128]{2,1,0:T(8,128)(2,1)} %shard_map.119), calls=%async_computation.1 | async-start | bytes 3276800 | tf_op jit(solution)/shard_map/all_to_all | solution.py:622
  51.4 5.7 %shard_map.123 = (f32[4,512]{1,0:T(4,128)S(1)}, f32[1024,128]{1,0:T(8,128)S(1)}, bf16[1024,128]{1,0:T(8,128)(2,1)}) custom-call(s32[17]{0:T(128)S(1)} %pad_add_fusion.info_ref, bf16[16,384,128]{2,1,0:T(8,128)(2,1)S(1)} %all-to-all-done.first_ref), custom_call_target="tpu_custom_call" | custom-call | flops 6000000000 | bytes 18000000 | tf_op jit(solution)/shard_map/pallas_call | solution.py:555
  57.9 1.9 %collective-permute-start.1 = (bf16[1024,128]{1,0:T(8,128)(2,1)}, bf16[1024,128]{1,0:T(8,128)(2,1)S(1)}, u32[]{:S(2)}, u32[]{:S(2)}) collective-permute-start(bf16[1024,128]{1,0:T(8,128)(2,1)} %get-tuple-element.25), channel_id=1, source_target_pairs={{0,16},{2,18},{4,20},{6,22},{8,24},{10,26},{12,28},{14,30},{16,0},... | collective-permute-start | bytes 786440 | tf_op jit(solution)/shard_map/ppermute | solution.py:637
  59.8 13.8 %all-to-all-done.1.second_ref = bf16[16,400,128]{2,1,0:T(8,128)(2,1)S(1)} async-done(((bf16[16,400,128]{2,1,0:T(8,128)(2,1)}), bf16[16,400,128]{2,1,0:T(8,128)(2,1)S(1)}, u32[]{:S(2)}, u32[]{:S(2)}) %all-to-all-start.1) | async-done | bytes 1638432 | tf_op jit(solution)/shard_map/all_to_all | solution.py:622
  74.3 1.6 collective-permute-start
  75.9 2.7 %shard_map.122.local_ref = f32[2,1024,128]{2,1,0:T(8,128)S(1)} custom-call(bf16[16,400,128]{2,1,0:T(8,128)(2,1)S(1)} %all-to-all-done.1.second_ref), custom_call_target="tpu_custom_call" | custom-call | flops 4000000000 | bytes 12000000 | tf_op jit(solution)/shard_map/pallas_call | solution.py:555
  78.6 4.4 %collective-permute-done.incoming_ref = f32[2,128,128]{2,1,0:T(8,128)S(1)} collective-permute-done((f32[2,128,128]{2,1,0:T(8,128)S(1)}, f32[2,128,128]{2,1,0:T(8,128)S(1)}, u32[]{:S(2)}, u32[]{:S(2)}) %collective-permute-start) | collective-permute-done | bytes 131104 | tf_op jit(solution)/shard_map/ppermute | solution.py:627
  83.0 2.5 %shard_map.124 = (bf16[2,1024,128]{2,1,0:T(8,128)(2,1)S(1)}, bf16[1024,128]{1,0:T(8,128)(2,1)S(1)}, f32[16,128]{1,0:T(8,128)S(1)}) custom-call(s32[17]{0:T(128)S(1)} %pad_add_fusion.info_ref, bf16[16,400,128]{2,1,0:T(8,128)(2,1)S(1)} %all-to-all-done.1.second_ref, f32[2,128,128]{2,1,0:T(8,128)S(1)} %collective-permute-done.incoming_ref, ...), custom_call_target="tpu_custom_call" | custom-call | flops 2000000000 | bytes 6000000 | tf_op jit(solution)/shard_map/pallas_call | solution.py:555
  87.6 5.8 %all-to-all-start.2 = ((f32[8,16,128]{2,1,0:T(8,128)}), f32[8,16,128]{2,1,0:T(8,128)}, u32[]{:S(2)}, u32[]{:S(2)}) async-start(f32[8,16,128]{2,1,0:T(8,128)} %broadcast_in_dim.16), calls=%async_computation.2 | async-start | bytes 131072 | tf_op jit(solution)/shard_map/all_to_all | solution.py:622
  93.4 5.9 %all-to-all-done.2 = f32[8,16,128]{2,1,0:T(8,128)} async-done(((f32[8,16,128]{2,1,0:T(8,128)}), f32[8,16,128]{2,1,0:T(8,128)}, u32[]{:S(2)}, u32[]{:S(2)}) %all-to-all-start.2) | async-done | bytes 65568 | tf_op jit(solution)/shard_map/all_to_all | solution.py:622
  103.5 1.9 %shard_map.125 = f32[2,128,128]{2,1,0:T(8,128)S(1)} custom-call(s32[17]{0:T(128)S(1)} %pad_add_fusion.info_ref, bf16[16,400,128]{2,1,0:T(8,128)(2,1)S(1)} %all-to-all-done.1.second_ref, bf16[2,1024,128]{2,1,0:T(8,128)(2,1)S(1)} %copy-done.12, f32[16,128]{1,0:T(8,128)S(1)} %add.3.sums_ref, f32[1024,128]{1,0:T(8,128)S(1)} %copy-done.9, ...), custom_call_target="tpu_custom_call" | custom-call | flops 2000000000 | bytes 6000000 | tf_op jit(solution)/shard_map/pallas_call | solution.py:555
  105.4 4.8 %collective-permute-start.3 = (f32[2,128,128]{2,1,0:T(8,128)S(1)}, f32[2,128,128]{2,1,0:T(8,128)S(1)}, u32[]{:S(2)}, u32[]{:S(2)}) collective-permute-start(f32[2,128,128]{2,1,0:T(8,128)S(1)} %shard_map.125), channel_id=1, source_target_pairs={{16,0},{18,2},{20,4},{22,6},{24,8},{26,10},{28,12},{30,14},{17,1},... | collective-permute-start | bytes 393224 | tf_op jit(solution)/shard_map/ppermute | solution.py:632
  110.3 7.3 %shard_map.126 = bf16[16,256,128]{2,1,0:T(8,128)(2,1)S(1)} custom-call(s32[17]{0:T(128)S(1)} %pad_add_fusion.info_ref, bf16[16,384,128]{2,1,0:T(8,128)(2,1)S(1)} %all-to-all-done.first_ref, f32[4,512]{1,0:T(4,128)S(1)} %get-tuple-element.28.mass_ref, bf16[2,1024,128]{2,1,0:T(8,128)(2,1)S(1)} %copy-done.13, ...), custom_call_target="tpu_custom_call" | custom-call | flops 7000000000 | bytes 21000000 | tf_op jit(solution)/shard_map/pallas_call | solution.py:555
  119.2 4.3 %all-to-all-start.3 = ((bf16[16,256,128]{2,1,0:T(8,128)(2,1)}), bf16[16,256,128]{2,1,0:T(8,128)(2,1)S(1)}, u32[]{:S(2)}, u32[]{:S(2)}) async-start(bf16[16,256,128]{2,1,0:T(8,128)(2,1)} %copy-done), calls=%async_computation.3 | async-start | bytes 2097152 | tf_op jit(solution)/shard_map/all_to_all | solution.py:616
  126.4 6.4 %shard_map.127 = bf16[16,384,128]{2,1,0:T(8,128)(2,1)} custom-call(s32[17]{0:T(128)S(1)} %pad_add_fusion.info_ref, bf16[16,400,128]{2,1,0:T(8,128)(2,1)S(1)} %all-to-all-done.1.second_ref, bf16[2,1024,128]{2,1,0:T(8,128)(2,1)S(1)} %copy-done.14, f32[2,128,128]{2,1,0:T(8,128)S(1)} %copy-done.3, f32[16,128]{1,0:T(8,128)S(1)} %add.3.sums_ref, ...), custom_call_target="tpu_custom_call" | custom-call | flops 5000000000 | bytes 15000000 | tf_op jit(solution)/shard_map/pallas_call | solution.py:555
  132.8 15.2 %all-to-all-done.3.in_ref = bf16[16,256,128]{2,1,0:T(8,128)(2,1)S(1)} async-done(((bf16[16,256,128]{2,1,0:T(8,128)(2,1)}), bf16[16,256,128]{2,1,0:T(8,128)(2,1)S(1)}, u32[]{:S(2)}, u32[]{:S(2)}) %all-to-all-start.3) | async-done | bytes 1048608 | tf_op jit(solution)/shard_map/all_to_all | solution.py:616
  148.0 3.6 %all-to-all-start.4 = ((bf16[16,384,128]{2,1,0:T(8,128)(2,1)}), bf16[16,384,128]{2,1,0:T(8,128)(2,1)S(1)}, u32[]{:S(2)}, u32[]{:S(2)}) async-start(bf16[16,384,128]{2,1,0:T(8,128)(2,1)} %shard_map.127), calls=%async_computation.4 | async-start | bytes 3145728 | tf_op jit(solution)/shard_map/all_to_all | solution.py:622
  151.7 1.8 %shard_map.129 = (f32[128,16,128]{2,1,0:T(8,128)}, f32[128,16,128]{2,1,0:T(8,128)}) custom-call(bf16[16,256,128]{2,1,0:T(8,128)(2,1)S(1)} %all-to-all-done.3.in_ref), custom_call_target="tpu_custom_call" | custom-call | flops 2000000000 | bytes 6000000 | tf_op jit(solution)/shard_map/pallas_call | solution.py:555
  153.4 18.4 %all-to-all-done.4.in_ref = bf16[16,384,128]{2,1,0:T(8,128)(2,1)S(1)} async-done(((bf16[16,384,128]{2,1,0:T(8,128)(2,1)}), bf16[16,384,128]{2,1,0:T(8,128)(2,1)S(1)}, u32[]{:S(2)}, u32[]{:S(2)}) %all-to-all-start.4) | async-done | bytes 1572896 | tf_op jit(solution)/shard_map/all_to_all | solution.py:622
  171.8 2.1 %shard_map.128 = (f32[128,16,128]{2,1,0:T(8,128)}, f32[128,16,128]{2,1,0:T(8,128)}, f32[128,16,128]{2,1,0:T(8,128)}) custom-call(bf16[16,384,128]{2,1,0:T(8,128)(2,1)S(1)} %all-to-all-done.4.in_ref), custom_call_target="tpu_custom_call" | custom-call | flops 3000000000 | bytes 9000000 | tf_op jit(solution)/shard_map/pallas_call | solution.py:555
  (47 shorter events, 12.4 us)
Async XLA Ops:
  4.1 7.2 %copy-start.6 = (f32[16,128]{1,0:T(8,128)S(1)}, f32[16,128]{1,0:T(8,128)}, u32[]{:S(2)}) copy-start(f32[16,128]{1,0:T(8,128)} %refs_3_.1) | copy-start | bytes 24580
  4.1 43.5 %all-to-all-start = ((bf16[16,384,128]{2,1,0:T(8,128)(2,1)}), bf16[16,384,128]{2,1,0:T(8,128)(2,1)S(1)}, u32[]{:S(2)}, u32[]{:S(2)}) async-start(bf16[16,384,128]{2,1,0:T(8,128)(2,1)} %shard_map.120), calls=%async_computation | async-start | bytes 3145728 | tf_op jit(solution)/shard_map/all_to_all | solution.py:616
  14.9 36.3 %copy-start.15 = (s32[16]{0:T(128)S(1)}, s32[16]{0:T(128)}, u32[]{:S(2)}) copy-start(s32[16]{0:T(128)} %param.15) | copy-start | bytes 196
  47.6 26.1 %all-to-all-start.1 = ((bf16[16,400,128]{2,1,0:T(8,128)(2,1)}), bf16[16,400,128]{2,1,0:T(8,128)(2,1)S(1)}, u32[]{:S(2)}, u32[]{:S(2)}) async-start(bf16[16,400,128]{2,1,0:T(8,128)(2,1)} %shard_map.119), calls=%async_computation.1 | async-start | bytes 3276800 | tf_op jit(solution)/shard_map/all_to_all | solution.py:622
  57.1 0.8 copy-start.7
  57.9 20.7 %collective-permute-start.1 = (bf16[1024,128]{1,0:T(8,128)(2,1)}, bf16[1024,128]{1,0:T(8,128)(2,1)S(1)}, u32[]{:S(2)}, u32[]{:S(2)}) collective-permute-start(bf16[1024,128]{1,0:T(8,128)(2,1)} %get-tuple-element.25), channel_id=1, source_target_pairs={{0,16},{2,18},{4,20},{6,22},{8,24},{10,26},{12,28},{14,30},{16,0},... | collective-permute-start | bytes 786440 | tf_op jit(solution)/shard_map/ppermute | solution.py:637
  74.3 8.7 %copy-start.8 = (f32[1024,128]{1,0:T(8,128)S(1)}, f32[1024,128]{1,0:T(8,128)}, u32[]{:S(2)}) copy-start(f32[1024,128]{1,0:T(8,128)} %copy-done.7) | copy-start | bytes 1572868
  74.3 8.7 %collective-permute-start = (f32[2,128,128]{2,1,0:T(8,128)S(1)}, f32[2,128,128]{2,1,0:T(8,128)S(1)}, u32[]{:S(2)}, u32[]{:S(2)}) collective-permute-start(f32[2,128,128]{2,1,0:T(8,128)S(1)} %shard_map.121), channel_id=1, source_target_pairs={{0,16},{2,18},{4,20},{6,22},{8,24},{10,26},{12,28},{14,30},{1,17},... | collective-permute-start | bytes 393224 | tf_op jit(solution)/shard_map/ppermute | solution.py:627
  83.0 2.5 %copy-start.2 = (f32[2,128,128]{2,1,0:T(8,128)}, f32[2,128,128]{2,1,0:T(8,128)S(1)}, u32[]{:S(2)}) copy-start(f32[2,128,128]{2,1,0:T(8,128)S(1)} %collective-permute-done.incoming_ref) | copy-start | bytes 393220
  87.6 11.7 %all-to-all-start.2 = ((f32[8,16,128]{2,1,0:T(8,128)}), f32[8,16,128]{2,1,0:T(8,128)}, u32[]{:S(2)}, u32[]{:S(2)}) async-start(f32[8,16,128]{2,1,0:T(8,128)} %broadcast_in_dim.16), calls=%async_computation.2 | async-start | bytes 131072 | tf_op jit(solution)/shard_map/all_to_all | solution.py:622
  93.4 16.8 %collective-permute-start.4 = (bf16[1024,128]{1,0:T(8,128)(2,1)}, bf16[1024,128]{1,0:T(8,128)(2,1)}, u32[]{:S(2)}, u32[]{:S(2)}) collective-permute-start(bf16[1024,128]{1,0:T(8,128)(2,1)} %copy-done.1), channel_id=1, source_target_pairs={{0,16},{2,18},{4,20},{6,22},{8,24},{10,26},{12,28},{14,30},{16,0},... | collective-permute-start | bytes 786440 | tf_op jit(solution)/shard_map/ppermute | solution.py:637
  100.2 1.2 collective-permute-start.2
  101.4 8.8 %collective-permute-start.5 = (f32[8,128]{1,0:T(8,128)S(1)}, f32[8,128]{1,0:T(8,128)S(1)}, u32[]{:S(2)}, u32[]{:S(2)}) collective-permute-start(f32[8,128]{1,0:T(8,128)S(1)} %slice.4), channel_id=1, source_target_pairs={{0,16},{2,18},{4,20},{6,22},{8,24},{10,26},{12,28},{14,30},{16,0},... | collective-permute-start | bytes 12296 | tf_op jit(solution)/shard_map/ppermute | solution.py:637
  101.4 1.0 copy-start.9
  102.5 1.0 copy-start.12
  103.5 6.8 %copy-start.13 = (bf16[2,1024,128]{2,1,0:T(8,128)(2,1)S(1)}, bf16[2,1024,128]{2,1,0:T(8,128)(2,1)}, u32[]{:S(2)}) copy-start(bf16[2,1024,128]{2,1,0:T(8,128)(2,1)} %copy-done.11) | copy-start | bytes 1572868
  105.4 13.2 %collective-permute-start.3 = (f32[2,128,128]{2,1,0:T(8,128)S(1)}, f32[2,128,128]{2,1,0:T(8,128)S(1)}, u32[]{:S(2)}, u32[]{:S(2)}) collective-permute-start(f32[2,128,128]{2,1,0:T(8,128)S(1)} %shard_map.125), channel_id=1, source_target_pairs={{16,0},{18,2},{20,4},{22,6},{24,8},{26,10},{28,12},{30,14},{17,1},... | collective-permute-start | bytes 393224 | tf_op jit(solution)/shard_map/ppermute | solution.py:632
  117.6 1.0 copy-start
  118.6 5.0 %copy-start.10 = (f32[1024,128]{1,0:T(8,128)S(1)}, f32[1024,128]{1,0:T(8,128)}, u32[]{:S(2)}) copy-start(f32[1024,128]{1,0:T(8,128)} %copy-done.7) | copy-start | bytes 1572868
  119.2 28.8 %all-to-all-start.3 = ((bf16[16,256,128]{2,1,0:T(8,128)(2,1)}), bf16[16,256,128]{2,1,0:T(8,128)(2,1)S(1)}, u32[]{:S(2)}, u32[]{:S(2)}) async-start(bf16[16,256,128]{2,1,0:T(8,128)(2,1)} %copy-done), calls=%async_computation.3 | async-start | bytes 2097152 | tf_op jit(solution)/shard_map/all_to_all | solution.py:616
  123.6 0.9 copy-start.3
  124.5 0.9 copy-start.5
  125.4 1.0 copy-start.14
  148.0 23.8 %all-to-all-start.4 = ((bf16[16,384,128]{2,1,0:T(8,128)(2,1)}), bf16[16,384,128]{2,1,0:T(8,128)(2,1)S(1)}, u32[]{:S(2)}, u32[]{:S(2)}) async-start(bf16[16,384,128]{2,1,0:T(8,128)(2,1)} %shard_map.127), calls=%async_computation.4 | async-start | bytes 3145728 | tf_op jit(solution)/shard_map/all_to_all | solution.py:622
  (3 other events, 2.2 us)

commit v4 on v3

--- a/solution.py
+++ b/solution.py
@@ -334,6 +334,8 @@
     half = info_ref[info_ref.shape[0] - 1]
     incoming = [incoming_ref[head].astype(bf16) for head in range(heads)]
     carried = [jnp.ones((1, 1), f32)] * heads
+    columns = jnp.zeros((BLOCK, BLOCK), f32)
+    lanes = lax.broadcasted_iota(jnp.int32, (BLOCK, BLOCK), 1)
     for c in range(chunks):
         here = block_rows(c)
         raws = []
@@ -350,8 +352,10 @@
             raws.append(raw.astype(bf16))
             raw_ref[head, here, :] = raws[head]
         sent_ref[here, :] = jnp.where(half == 0, raws[1], raws[0])
-        sums_ref[c : c + 1, :] = row_sums(squares)[0:1, :]
-        sums_ref[chunks + c : chunks + c + 1, :] = row_sums(products)[0:1, :]
+        for place, part in ((c, squares), (chunks + c, products)):
+            total = jnp.sum(part, axis=1, keepdims=True)
+            columns = jnp.where(lanes == place, total, columns)
+    sums_ref[...] = columns.T[0 : 2 * chunks, :]
 
 
 def column(columns, c):

time: 177 us -> 176 us (level)
  no operation moved by 1% of the time
where the time goes in v4:
time: 176 us; the launch traced here: 173 us
  waiting for transfers between devices  92 us (52%)
  Pallas kernels  36.6 us (21%)
  starting transfers between devices  33.1 us (19%)
  local copies, waits for them, and re-layouts  9.5 us (5%)
    all_to_all x2, waiting for transfers between devices, exchange(): return lax.all_to_all(x, 'seq', 0, 0, tiled=True)  48.1 us
    all_to_all x3, waiting for transfers between devices, exchange_half(): return lax.all_to_all(x, 'seq', 0, 0, tiled=True, axis_index_groups=groups)  38.3 us
    pallas_call x11, Pallas kernels, call(): pl.pallas_call(kernel, out_shape=results, in_specs=[smem] * prefetch + [v...  36.6 us
    all_to_all x3, starting transfers between devices, exchange_half(): return lax.all_to_all(x, 'seq', 0, 0, tiled=True, axis_index_groups=groups)  13.1 us
    all_to_all x2, starting transfers between devices, exchange(): return lax.all_to_all(x, 'seq', 0, 0, tiled=True)  11.7 us
    unnamed x32, local copies, waits for them, and re-layouts  8.86 us
    ppermute x1, starting transfers between devices, downward(): return lax.ppermute(x, 'seq', [(i + side, i) for i in range(side)])  4.83 us
    ppermute x1, waiting for transfers between devices, upward(): return lax.ppermute(x, 'seq', [(i, i + side) for i in range(side)])  4.39 us
  transfers between devices with their start and end apart: 11, of which 7 were waited for; matrix products, arithmetic and copies ran while one was open for 1% of the time, Pallas kernels for 17%

profile of v4, /device:TPU:16, one launch (start us, length us, event | category | flops | bytes accessed | tf_op | source)
XLA Modules:
  0.0 173.2 jit_solution(5833278589165844834)
XLA Ops:
  0.6 3.5 %shard_map.120 = bf16[16,384,128]{2,1,0:T(8,128)(2,1)} custom-call(bf16[128,16,128]{2,1,0:T(8,128)(2,1)} %refs_0_.3, bf16[128,16,128]{2,1,0:T(8,128)(2,1)} %refs_1_.3, bf16[128,16,128]{2,1,0:T(8,128)(2,1)} %refs_2_.3), custom_call_target="tpu_custom_call" | custom-call | flops 3000000000 | bytes 9000000 | tf_op jit(solution)/shard_map/pallas_call | solution.py:559
  4.1 7.2 %all-to-all-start = ((bf16[16,384,128]{2,1,0:T(8,128)(2,1)}), bf16[16,384,128]{2,1,0:T(8,128)(2,1)S(1)}, u32[]{:S(2)}, u32[]{:S(2)}) async-start(bf16[16,384,128]{2,1,0:T(8,128)(2,1)} %shard_map.120), calls=%async_computation | async-start | bytes 3145728 | tf_op jit(solution)/shard_map/all_to_all | solution.py:620
  11.4 3.5 %shard_map.119 = bf16[16,400,128]{2,1,0:T(8,128)(2,1)} custom-call(bf16[128,16,128]{2,1,0:T(8,128)(2,1)} %refs_0_.2, bf16[128,16,128]{2,1,0:T(8,128)(2,1)} %refs_1_.2, bf16[128,16,128]{2,1,0:T(8,128)(2,1)} %refs_2_.2, f32[16,128]{1,0:T(8,128)S(1)} %copy-done.6), custom_call_target="tpu_custom_call" | custom-call | flops 3000000000 | bytes 9000000 | tf_op jit(solution)/shard_map/pallas_call | solution.py:559
  14.9 32.7 %all-to-all-done.first_ref = bf16[16,384,128]{2,1,0:T(8,128)(2,1)S(1)} async-done(((bf16[16,384,128]{2,1,0:T(8,128)(2,1)}), bf16[16,384,128]{2,1,0:T(8,128)(2,1)S(1)}, u32[]{:S(2)}, u32[]{:S(2)}) %all-to-all-start) | async-done | bytes 1572896 | tf_op jit(solution)/shard_map/all_to_all | solution.py:620
  47.6 3.6 %all-to-all-start.1 = ((bf16[16,400,128]{2,1,0:T(8,128)(2,1)}), bf16[16,400,128]{2,1,0:T(8,128)(2,1)S(1)}, u32[]{:S(2)}, u32[]{:S(2)}) async-start(bf16[16,400,128]{2,1,0:T(8,128)(2,1)} %shard_map.119), calls=%async_computation.1 | async-start | bytes 3276800 | tf_op jit(solution)/shard_map/all_to_all | solution.py:626
  51.4 5.4 %shard_map.123 = (f32[4,512]{1,0:T(4,128)S(1)}, f32[1024,128]{1,0:T(8,128)S(1)}, bf16[1024,128]{1,0:T(8,128)(2,1)}) custom-call(s32[17]{0:T(128)S(1)} %pad_add_fusion.info_ref, bf16[16,384,128]{2,1,0:T(8,128)(2,1)S(1)} %all-to-all-done.first_ref), custom_call_target="tpu_custom_call" | custom-call | flops 6000000000 | bytes 18000000 | tf_op jit(solution)/shard_map/pallas_call | solution.py:559
  57.6 1.9 %collective-permute-start.1 = (bf16[1024,128]{1,0:T(8,128)(2,1)}, bf16[1024,128]{1,0:T(8,128)(2,1)S(1)}, u32[]{:S(2)}, u32[]{:S(2)}) collective-permute-start(bf16[1024,128]{1,0:T(8,128)(2,1)} %get-tuple-element.25), channel_id=1, source_target_pairs={{0,16},{2,18},{4,20},{6,22},{8,24},{10,26},{12,28},{14,30},{16,0},... | collective-permute-start | bytes 786440 | tf_op jit(solution)/shard_map/ppermute | solution.py:641
  59.5 14.1 %all-to-all-done.1.second_ref = bf16[16,400,128]{2,1,0:T(8,128)(2,1)S(1)} async-done(((bf16[16,400,128]{2,1,0:T(8,128)(2,1)}), bf16[16,400,128]{2,1,0:T(8,128)(2,1)S(1)}, u32[]{:S(2)}, u32[]{:S(2)}) %all-to-all-start.1) | async-done | bytes 1638432 | tf_op jit(solution)/shard_map/all_to_all | solution.py:626
  74.3 1.6 collective-permute-start
  75.9 2.7 %shard_map.122.local_ref = f32[2,1024,128]{2,1,0:T(8,128)S(1)} custom-call(bf16[16,400,128]{2,1,0:T(8,128)(2,1)S(1)} %all-to-all-done.1.second_ref), custom_call_target="tpu_custom_call" | custom-call | flops 4000000000 | bytes 12000000 | tf_op jit(solution)/shard_map/pallas_call | solution.py:559
  78.6 4.4 %collective-permute-done.incoming_ref = f32[2,128,128]{2,1,0:T(8,128)S(1)} collective-permute-done((f32[2,128,128]{2,1,0:T(8,128)S(1)}, f32[2,128,128]{2,1,0:T(8,128)S(1)}, u32[]{:S(2)}, u32[]{:S(2)}) %collective-permute-start) | collective-permute-done | bytes 131104 | tf_op jit(solution)/shard_map/ppermute | solution.py:631
  83.0 1.7 %shard_map.124 = (bf16[2,1024,128]{2,1,0:T(8,128)(2,1)S(1)}, bf16[1024,128]{1,0:T(8,128)(2,1)S(1)}, f32[16,128]{1,0:T(8,128)S(1)}) custom-call(s32[17]{0:T(128)S(1)} %pad_add_fusion.info_ref, bf16[16,400,128]{2,1,0:T(8,128)(2,1)S(1)} %all-to-all-done.1.second_ref, f32[2,128,128]{2,1,0:T(8,128)S(1)} %collective-permute-done.incoming_ref, ...), custom_call_target="tpu_custom_call" | custom-call | flops 2000000000 | bytes 6000000 | tf_op jit(solution)/shard_map/pallas_call | solution.py:559
  86.9 5.8 %all-to-all-start.2 = ((f32[8,16,128]{2,1,0:T(8,128)}), f32[8,16,128]{2,1,0:T(8,128)}, u32[]{:S(2)}, u32[]{:S(2)}) async-start(f32[8,16,128]{2,1,0:T(8,128)} %broadcast_in_dim.16), calls=%async_computation.2 | async-start | bytes 131072 | tf_op jit(solution)/shard_map/all_to_all | solution.py:626
  92.7 5.9 %all-to-all-done.2 = f32[8,16,128]{2,1,0:T(8,128)} async-done(((f32[8,16,128]{2,1,0:T(8,128)}), f32[8,16,128]{2,1,0:T(8,128)}, u32[]{:S(2)}, u32[]{:S(2)}) %all-to-all-start.2) | async-done | bytes 65568 | tf_op jit(solution)/shard_map/all_to_all | solution.py:626
  102.8 1.9 %shard_map.125 = f32[2,128,128]{2,1,0:T(8,128)S(1)} custom-call(s32[17]{0:T(128)S(1)} %pad_add_fusion.info_ref, bf16[16,400,128]{2,1,0:T(8,128)(2,1)S(1)} %all-to-all-done.1.second_ref, bf16[2,1024,128]{2,1,0:T(8,128)(2,1)S(1)} %copy-done.12, f32[16,128]{1,0:T(8,128)S(1)} %add.3.sums_ref, f32[1024,128]{1,0:T(8,128)S(1)} %copy-done.9, ...), custom_call_target="tpu_custom_call" | custom-call | flops 2000000000 | bytes 6000000 | tf_op jit(solution)/shard_map/pallas_call | solution.py:559
  104.7 4.8 %collective-permute-start.3 = (f32[2,128,128]{2,1,0:T(8,128)S(1)}, f32[2,128,128]{2,1,0:T(8,128)S(1)}, u32[]{:S(2)}, u32[]{:S(2)}) collective-permute-start(f32[2,128,128]{2,1,0:T(8,128)S(1)} %shard_map.125), channel_id=1, source_target_pairs={{16,0},{18,2},{20,4},{22,6},{24,8},{26,10},{28,12},{30,14},{17,1},... | collective-permute-start | bytes 393224 | tf_op jit(solution)/shard_map/ppermute | solution.py:636
  109.5 7.0 %shard_map.126 = bf16[16,256,128]{2,1,0:T(8,128)(2,1)S(1)} custom-call(s32[17]{0:T(128)S(1)} %pad_add_fusion.info_ref, bf16[16,384,128]{2,1,0:T(8,128)(2,1)S(1)} %all-to-all-done.first_ref, f32[4,512]{1,0:T(4,128)S(1)} %get-tuple-element.28.mass_ref, bf16[2,1024,128]{2,1,0:T(8,128)(2,1)S(1)} %copy-done.13, ...), custom_call_target="tpu_custom_call" | custom-call | flops 7000000000 | bytes 21000000 | tf_op jit(solution)/shard_map/pallas_call | solution.py:559
  118.2 4.4 %all-to-all-start.3 = ((bf16[16,256,128]{2,1,0:T(8,128)(2,1)}), bf16[16,256,128]{2,1,0:T(8,128)(2,1)S(1)}, u32[]{:S(2)}, u32[]{:S(2)}) async-start(bf16[16,256,128]{2,1,0:T(8,128)(2,1)} %copy-done), calls=%async_computation.3 | async-start | bytes 2097152 | tf_op jit(solution)/shard_map/all_to_all | solution.py:620
  125.5 6.4 %shard_map.127 = bf16[16,384,128]{2,1,0:T(8,128)(2,1)} custom-call(s32[17]{0:T(128)S(1)} %pad_add_fusion.info_ref, bf16[16,400,128]{2,1,0:T(8,128)(2,1)S(1)} %all-to-all-done.1.second_ref, bf16[2,1024,128]{2,1,0:T(8,128)(2,1)S(1)} %copy-done.14, f32[2,128,128]{2,1,0:T(8,128)S(1)} %copy-done.3, f32[16,128]{1,0:T(8,128)S(1)} %add.3.sums_ref, ...), custom_call_target="tpu_custom_call" | custom-call | flops 5000000000 | bytes 15000000 | tf_op jit(solution)/shard_map/pallas_call | solution.py:559
  131.9 15.5 %all-to-all-done.3.in_ref = bf16[16,256,128]{2,1,0:T(8,128)(2,1)S(1)} async-done(((bf16[16,256,128]{2,1,0:T(8,128)(2,1)}), bf16[16,256,128]{2,1,0:T(8,128)(2,1)S(1)}, u32[]{:S(2)}, u32[]{:S(2)}) %all-to-all-start.3) | async-done | bytes 1048608 | tf_op jit(solution)/shard_map/all_to_all | solution.py:620
  147.4 3.7 %all-to-all-start.4 = ((bf16[16,384,128]{2,1,0:T(8,128)(2,1)}), bf16[16,384,128]{2,1,0:T(8,128)(2,1)S(1)}, u32[]{:S(2)}, u32[]{:S(2)}) async-start(bf16[16,384,128]{2,1,0:T(8,128)(2,1)} %shard_map.127), calls=%async_computation.4 | async-start | bytes 3145728 | tf_op jit(solution)/shard_map/all_to_all | solution.py:626
  151.1 1.8 %shard_map.129 = (f32[128,16,128]{2,1,0:T(8,128)}, f32[128,16,128]{2,1,0:T(8,128)}) custom-call(bf16[16,256,128]{2,1,0:T(8,128)(2,1)S(1)} %all-to-all-done.3.in_ref), custom_call_target="tpu_custom_call" | custom-call | flops 2000000000 | bytes 6000000 | tf_op jit(solution)/shard_map/pallas_call | solution.py:559
  152.9 18.2 %all-to-all-done.4.in_ref = bf16[16,384,128]{2,1,0:T(8,128)(2,1)S(1)} async-done(((bf16[16,384,128]{2,1,0:T(8,128)(2,1)}), bf16[16,384,128]{2,1,0:T(8,128)(2,1)S(1)}, u32[]{:S(2)}, u32[]{:S(2)}) %all-to-all-start.4) | async-done | bytes 1572896 | tf_op jit(solution)/shard_map/all_to_all | solution.py:626
  171.1 2.1 %shard_map.128 = (f32[128,16,128]{2,1,0:T(8,128)}, f32[128,16,128]{2,1,0:T(8,128)}, f32[128,16,128]{2,1,0:T(8,128)}) custom-call(bf16[16,384,128]{2,1,0:T(8,128)(2,1)S(1)} %all-to-all-done.4.in_ref), custom_call_target="tpu_custom_call" | custom-call | flops 3000000000 | bytes 9000000 | tf_op jit(solution)/shard_map/pallas_call | solution.py:559
  (47 shorter events, 12.4 us)
Async XLA Ops:
  4.1 7.2 %copy-start.6 = (f32[16,128]{1,0:T(8,128)S(1)}, f32[16,128]{1,0:T(8,128)}, u32[]{:S(2)}) copy-start(f32[16,128]{1,0:T(8,128)} %refs_3_.1) | copy-start | bytes 24580
  4.1 43.5 %all-to-all-start = ((bf16[16,384,128]{2,1,0:T(8,128)(2,1)}), bf16[16,384,128]{2,1,0:T(8,128)(2,1)S(1)}, u32[]{:S(2)}, u32[]{:S(2)}) async-start(bf16[16,384,128]{2,1,0:T(8,128)(2,1)} %shard_map.120), calls=%async_computation | async-start | bytes 3145728 | tf_op jit(solution)/shard_map/all_to_all | solution.py:620
  14.9 36.3 %copy-start.15 = (s32[16]{0:T(128)S(1)}, s32[16]{0:T(128)}, u32[]{:S(2)}) copy-start(s32[16]{0:T(128)} %param.15) | copy-start | bytes 196
  47.6 26.1 %all-to-all-start.1 = ((bf16[16,400,128]{2,1,0:T(8,128)(2,1)}), bf16[16,400,128]{2,1,0:T(8,128)(2,1)S(1)}, u32[]{:S(2)}, u32[]{:S(2)}) async-start(bf16[16,400,128]{2,1,0:T(8,128)(2,1)} %shard_map.119), calls=%async_computation.1 | async-start | bytes 3276800 | tf_op jit(solution)/shard_map/all_to_all | solution.py:626
  56.8 0.8 copy-start.7
  57.6 21.0 %collective-permute-start.1 = (bf16[1024,128]{1,0:T(8,128)(2,1)}, bf16[1024,128]{1,0:T(8,128)(2,1)S(1)}, u32[]{:S(2)}, u32[]{:S(2)}) collective-permute-start(bf16[1024,128]{1,0:T(8,128)(2,1)} %get-tuple-element.25), channel_id=1, source_target_pairs={{0,16},{2,18},{4,20},{6,22},{8,24},{10,26},{12,28},{14,30},{16,0},... | collective-permute-start | bytes 786440 | tf_op jit(solution)/shard_map/ppermute | solution.py:641
  74.3 8.7 %copy-start.8 = (f32[1024,128]{1,0:T(8,128)S(1)}, f32[1024,128]{1,0:T(8,128)}, u32[]{:S(2)}) copy-start(f32[1024,128]{1,0:T(8,128)} %copy-done.7) | copy-start | bytes 1572868
  74.3 8.7 %collective-permute-start = (f32[2,128,128]{2,1,0:T(8,128)S(1)}, f32[2,128,128]{2,1,0:T(8,128)S(1)}, u32[]{:S(2)}, u32[]{:S(2)}) collective-permute-start(f32[2,128,128]{2,1,0:T(8,128)S(1)} %shard_map.121), channel_id=1, source_target_pairs={{0,16},{2,18},{4,20},{6,22},{8,24},{10,26},{12,28},{14,30},{1,17},... | collective-permute-start | bytes 393224 | tf_op jit(solution)/shard_map/ppermute | solution.py:631
  83.0 1.8 %copy-start.2 = (f32[2,128,128]{2,1,0:T(8,128)}, f32[2,128,128]{2,1,0:T(8,128)S(1)}, u32[]{:S(2)}) copy-start(f32[2,128,128]{2,1,0:T(8,128)S(1)} %collective-permute-done.incoming_ref) | copy-start | bytes 393220
  86.9 11.7 %all-to-all-start.2 = ((f32[8,16,128]{2,1,0:T(8,128)}), f32[8,16,128]{2,1,0:T(8,128)}, u32[]{:S(2)}, u32[]{:S(2)}) async-start(f32[8,16,128]{2,1,0:T(8,128)} %broadcast_in_dim.16), calls=%async_computation.2 | async-start | bytes 131072 | tf_op jit(solution)/shard_map/all_to_all | solution.py:626
  92.7 16.8 %collective-permute-start.4 = (bf16[1024,128]{1,0:T(8,128)(2,1)}, bf16[1024,128]{1,0:T(8,128)(2,1)}, u32[]{:S(2)}, u32[]{:S(2)}) collective-permute-start(bf16[1024,128]{1,0:T(8,128)(2,1)} %copy-done.1), channel_id=1, source_target_pairs={{0,16},{2,18},{4,20},{6,22},{8,24},{10,26},{12,28},{14,30},{16,0},... | collective-permute-start | bytes 786440 | tf_op jit(solution)/shard_map/ppermute | solution.py:641
  99.5 1.2 collective-permute-start.2
  100.7 8.8 %collective-permute-start.5 = (f32[8,128]{1,0:T(8,128)S(1)}, f32[8,128]{1,0:T(8,128)S(1)}, u32[]{:S(2)}, u32[]{:S(2)}) collective-permute-start(f32[8,128]{1,0:T(8,128)S(1)} %slice.4), channel_id=1, source_target_pairs={{0,16},{2,18},{4,20},{6,22},{8,24},{10,26},{12,28},{14,30},{16,0},... | collective-permute-start | bytes 12296 | tf_op jit(solution)/shard_map/ppermute | solution.py:641
  100.7 1.0 copy-start.9
  101.7 1.0 copy-start.12
  102.8 6.8 %copy-start.13 = (bf16[2,1024,128]{2,1,0:T(8,128)(2,1)S(1)}, bf16[2,1024,128]{2,1,0:T(8,128)(2,1)}, u32[]{:S(2)}) copy-start(bf16[2,1024,128]{2,1,0:T(8,128)(2,1)} %copy-done.11) | copy-start | bytes 1572868
  104.7 12.9 %collective-permute-start.3 = (f32[2,128,128]{2,1,0:T(8,128)S(1)}, f32[2,128,128]{2,1,0:T(8,128)S(1)}, u32[]{:S(2)}, u32[]{:S(2)}) collective-permute-start(f32[2,128,128]{2,1,0:T(8,128)S(1)} %shard_map.125), channel_id=1, source_target_pairs={{16,0},{18,2},{20,4},{22,6},{24,8},{26,10},{28,12},{30,14},{17,1},... | collective-permute-start | bytes 393224 | tf_op jit(solution)/shard_map/ppermute | solution.py:636
  116.6 1.0 copy-start
  117.5 5.1 %copy-start.10 = (f32[1024,128]{1,0:T(8,128)S(1)}, f32[1024,128]{1,0:T(8,128)}, u32[]{:S(2)}) copy-start(f32[1024,128]{1,0:T(8,128)} %copy-done.7) | copy-start | bytes 1572868
  118.2 29.2 %all-to-all-start.3 = ((bf16[16,256,128]{2,1,0:T(8,128)(2,1)}), bf16[16,256,128]{2,1,0:T(8,128)(2,1)S(1)}, u32[]{:S(2)}, u32[]{:S(2)}) async-start(bf16[16,256,128]{2,1,0:T(8,128)(2,1)} %copy-done), calls=%async_computation.3 | async-start | bytes 2097152 | tf_op jit(solution)/shard_map/all_to_all | solution.py:620
  122.6 0.9 copy-start.3
  123.5 0.9 copy-start.5
  124.4 1.0 copy-start.14
  147.4 23.7 %all-to-all-start.4 = ((bf16[16,384,128]{2,1,0:T(8,128)(2,1)}), bf16[16,384,128]{2,1,0:T(8,128)(2,1)S(1)}, u32[]{:S(2)}, u32[]{:S(2)}) async-start(bf16[16,384,128]{2,1,0:T(8,128)(2,1)} %shard_map.127), calls=%async_computation.4 | async-start | bytes 3145728 | tf_op jit(solution)/shard_map/all_to_all | solution.py:626
  (3 other events, 2.2 us)

commit v5 on v4

--- a/solution.py
+++ b/solution.py
@@ -732,6 +732,8 @@
         sums_other,
         prefetch=1,
     )
+    raw_in_hbm = pltpu.with_memory_space_constraint(raw, pltpu.HBM)
+    kept_in_hbm = pltpu.with_memory_space_constraint(grad_kept, pltpu.HBM)
     (state_grad,) = call(
         partial(linear_state_grad, features, heads),
         2,
@@ -739,9 +741,9 @@
         [],
         info,
         second,
-        raw,
+        raw_in_hbm,
         sums,
-        grad_kept,
+        kept_in_hbm,
         grad_other,
         prefetch=1,
     )
@@ -755,10 +757,10 @@
         [((heads, side, width, width), bf16)],
         info,
         second,
-        raw,
+        raw_in_hbm,
         incoming,
         sums,
-        grad_kept,
+        kept_in_hbm,
         grad_other,
         later_grad,
         prefetch=1,

time: 176 us -> 175 us (level)
  local copies, waits for them, and re-layouts: 9.5 us -> 5.48 us
  Pallas kernels: 36.6 us -> 39.8 us
    unnamed x32 -> x24, local copies, waits for them, and re-layouts: 8.86 us -> 4.84 us
    pallas_call x11, Pallas kernels: 36.6 us -> 39.8 us  [call(): pl.pallas_call(kernel, out_shape=results, in_specs=[smem] * prefetch + [v...]
  transfers between devices with their start and end apart: 11 -> 11, of which waited for: 7 -> 7; matrix products, arithmetic and copies ran while one was open for 1% -> 1% of each run, Pallas kernels for 17% -> 19%
where the time goes in v5:
time: 175 us; the launch traced here: 172 us
  waiting for transfers between devices  91.8 us (52%)
  Pallas kernels  39.8 us (23%)
  starting transfers between devices  32.9 us (19%)
  local copies, waits for them, and re-layouts  5.48 us (3%)
    all_to_all x2, waiting for transfers between devices, exchange(): return lax.all_to_all(x, 'seq', 0, 0, tiled=True)  48.8 us
    pallas_call x11, Pallas kernels, call(): pl.pallas_call(kernel, out_shape=results, in_specs=[smem] * prefetch + [v...  39.8 us
    all_to_all x3, waiting for transfers between devices, exchange_half(): return lax.all_to_all(x, 'seq', 0, 0, tiled=True, axis_index_groups=groups)  37.5 us
    all_to_all x3, starting transfers between devices, exchange_half(): return lax.all_to_all(x, 'seq', 0, 0, tiled=True, axis_index_groups=groups)  13 us
    all_to_all x2, starting transfers between devices, exchange(): return lax.all_to_all(x, 'seq', 0, 0, tiled=True)  11.6 us
    unnamed x24, local copies, waits for them, and re-layouts  4.84 us
    ppermute x1, starting transfers between devices, downward(): return lax.ppermute(x, 'seq', [(i + side, i) for i in range(side)])  4.82 us
    ppermute x1, waiting for transfers between devices, upward(): return lax.ppermute(x, 'seq', [(i, i + side) for i in range(side)])  4.39 us
  transfers between devices with their start and end apart: 11, of which 7 were waited for; matrix products, arithmetic and copies ran while one was open for 1% of the time, Pallas kernels for 19%

profile of v5, /device:TPU:16, one launch (start us, length us, event | category | flops | bytes accessed | tf_op | source)
XLA Modules:
  0.0 171.9 jit_solution(16071673866173652468)
XLA Ops:
  0.6 3.5 %shard_map.120 = bf16[16,384,128]{2,1,0:T(8,128)(2,1)} custom-call(bf16[128,16,128]{2,1,0:T(8,128)(2,1)} %refs_0_.3, bf16[128,16,128]{2,1,0:T(8,128)(2,1)} %refs_1_.3, bf16[128,16,128]{2,1,0:T(8,128)(2,1)} %refs_2_.3), custom_call_target="tpu_custom_call" | custom-call | flops 3000000000 | bytes 9000000 | tf_op jit(solution)/shard_map/pallas_call | solution.py:559
  4.1 7.2 %all-to-all-start = ((bf16[16,384,128]{2,1,0:T(8,128)(2,1)}), bf16[16,384,128]{2,1,0:T(8,128)(2,1)S(1)}, u32[]{:S(2)}, u32[]{:S(2)}) async-start(bf16[16,384,128]{2,1,0:T(8,128)(2,1)} %shard_map.120), calls=%async_computation | async-start | bytes 3145728 | tf_op jit(solution)/shard_map/all_to_all | solution.py:620
  11.3 3.5 %shard_map.119 = bf16[16,400,128]{2,1,0:T(8,128)(2,1)} custom-call(bf16[128,16,128]{2,1,0:T(8,128)(2,1)} %refs_0_.2, bf16[128,16,128]{2,1,0:T(8,128)(2,1)} %refs_1_.2, bf16[128,16,128]{2,1,0:T(8,128)(2,1)} %refs_2_.2, f32[16,128]{1,0:T(8,128)S(1)} %copy-done.6), custom_call_target="tpu_custom_call" | custom-call | flops 3000000000 | bytes 9000000 | tf_op jit(solution)/shard_map/pallas_call | solution.py:559
  14.9 32.7 %all-to-all-done.first_ref = bf16[16,384,128]{2,1,0:T(8,128)(2,1)S(1)} async-done(((bf16[16,384,128]{2,1,0:T(8,128)(2,1)}), bf16[16,384,128]{2,1,0:T(8,128)(2,1)S(1)}, u32[]{:S(2)}, u32[]{:S(2)}) %all-to-all-start) | async-done | bytes 1572896 | tf_op jit(solution)/shard_map/all_to_all | solution.py:620
  47.6 3.6 %all-to-all-start.1 = ((bf16[16,400,128]{2,1,0:T(8,128)(2,1)}), bf16[16,400,128]{2,1,0:T(8,128)(2,1)S(1)}, u32[]{:S(2)}, u32[]{:S(2)}) async-start(bf16[16,400,128]{2,1,0:T(8,128)(2,1)} %shard_map.119), calls=%async_computation.1 | async-start | bytes 3276800 | tf_op jit(solution)/shard_map/all_to_all | solution.py:626
  51.4 6.3 %shard_map.123 = (f32[4,512]{1,0:T(4,128)S(1)}, f32[1024,128]{1,0:T(8,128)S(1)}, bf16[1024,128]{1,0:T(8,128)(2,1)}) custom-call(s32[17]{0:T(128)S(1)} %pad_add_fusion.info_ref, bf16[16,384,128]{2,1,0:T(8,128)(2,1)S(1)} %all-to-all-done.first_ref), custom_call_target="tpu_custom_call" | custom-call | flops 6000000000 | bytes 18000000 | tf_op jit(solution)/shard_map/pallas_call | solution.py:559
  58.5 1.9 %collective-permute-start.1 = (bf16[1024,128]{1,0:T(8,128)(2,1)}, bf16[1024,128]{1,0:T(8,128)(2,1)S(1)}, u32[]{:S(2)}, u32[]{:S(2)}) collective-permute-start(bf16[1024,128]{1,0:T(8,128)(2,1)} %get-tuple-element.25), channel_id=1, source_target_pairs={{0,16},{2,18},{4,20},{6,22},{8,24},{10,26},{12,28},{14,30},{16,0},... | collective-permute-start | bytes 786440 | tf_op jit(solution)/shard_map/ppermute | solution.py:641
  60.4 13.2 %all-to-all-done.1.second_ref = bf16[16,400,128]{2,1,0:T(8,128)(2,1)S(1)} async-done(((bf16[16,400,128]{2,1,0:T(8,128)(2,1)}), bf16[16,400,128]{2,1,0:T(8,128)(2,1)S(1)}, u32[]{:S(2)}, u32[]{:S(2)}) %all-to-all-start.1) | async-done | bytes 1638432 | tf_op jit(solution)/shard_map/all_to_all | solution.py:626
  74.3 1.6 collective-permute-start
  75.9 2.7 %shard_map.122.local_ref = f32[2,1024,128]{2,1,0:T(8,128)S(1)} custom-call(bf16[16,400,128]{2,1,0:T(8,128)(2,1)S(1)} %all-to-all-done.1.second_ref), custom_call_target="tpu_custom_call" | custom-call | flops 4000000000 | bytes 12000000 | tf_op jit(solution)/shard_map/pallas_call | solution.py:559
  78.6 4.4 %collective-permute-done.incoming_ref = f32[2,128,128]{2,1,0:T(8,128)S(1)} collective-permute-done((f32[2,128,128]{2,1,0:T(8,128)S(1)}, f32[2,128,128]{2,1,0:T(8,128)S(1)}, u32[]{:S(2)}, u32[]{:S(2)}) %collective-permute-start) | collective-permute-done | bytes 131104 | tf_op jit(solution)/shard_map/ppermute | solution.py:631
  83.0 1.7 %shard_map.124 = (bf16[2,1024,128]{2,1,0:T(8,128)(2,1)S(1)}, bf16[1024,128]{1,0:T(8,128)(2,1)S(1)}, f32[16,128]{1,0:T(8,128)S(1)}) custom-call(s32[17]{0:T(128)S(1)} %pad_add_fusion.info_ref, bf16[16,400,128]{2,1,0:T(8,128)(2,1)S(1)} %all-to-all-done.1.second_ref, f32[2,128,128]{2,1,0:T(8,128)S(1)} %collective-permute-done.incoming_ref, ...), custom_call_target="tpu_custom_call" | custom-call | flops 2000000000 | bytes 6000000 | tf_op jit(solution)/shard_map/pallas_call | solution.py:559
  86.9 5.8 %all-to-all-start.2 = ((f32[8,16,128]{2,1,0:T(8,128)}), f32[8,16,128]{2,1,0:T(8,128)}, u32[]{:S(2)}, u32[]{:S(2)}) async-start(f32[8,16,128]{2,1,0:T(8,128)} %broadcast_in_dim.16), calls=%async_computation.2 | async-start | bytes 131072 | tf_op jit(solution)/shard_map/all_to_all | solution.py:626
  92.7 5.9 %all-to-all-done.2 = f32[8,16,128]{2,1,0:T(8,128)} async-done(((f32[8,16,128]{2,1,0:T(8,128)}), f32[8,16,128]{2,1,0:T(8,128)}, u32[]{:S(2)}, u32[]{:S(2)}) %all-to-all-start.2) | async-done | bytes 65568 | tf_op jit(solution)/shard_map/all_to_all | solution.py:626
  100.7 2.6 %shard_map.125 = f32[2,128,128]{2,1,0:T(8,128)S(1)} custom-call(s32[17]{0:T(128)S(1)} %pad_add_fusion.info_ref, bf16[16,400,128]{2,1,0:T(8,128)(2,1)S(1)} %all-to-all-done.1.second_ref, bf16[2,1024,128]{2,1,0:T(8,128)(2,1)} %copy-done.9, f32[16,128]{1,0:T(8,128)S(1)} %add.3.sums_ref, f32[1024,128]{1,0:T(8,128)} %copy-done.7, ...), custom_call_target="tpu_custom_call" | custom-call | flops 2000000000 | bytes 6000000 | tf_op jit(solution)/shard_map/pallas_call | solution.py:559
  103.3 4.8 %collective-permute-start.3 = (f32[2,128,128]{2,1,0:T(8,128)S(1)}, f32[2,128,128]{2,1,0:T(8,128)S(1)}, u32[]{:S(2)}, u32[]{:S(2)}) collective-permute-start(f32[2,128,128]{2,1,0:T(8,128)S(1)} %shard_map.125), channel_id=1, source_target_pairs={{16,0},{18,2},{20,4},{22,6},{24,8},{26,10},{28,12},{30,14},{17,1},... | collective-permute-start | bytes 393224 | tf_op jit(solution)/shard_map/ppermute | solution.py:636
  108.2 8.0 %shard_map.126 = bf16[16,256,128]{2,1,0:T(8,128)(2,1)S(1)} custom-call(s32[17]{0:T(128)S(1)} %pad_add_fusion.info_ref, bf16[16,384,128]{2,1,0:T(8,128)(2,1)S(1)} %all-to-all-done.first_ref, f32[4,512]{1,0:T(4,128)S(1)} %get-tuple-element.28.mass_ref, bf16[2,1024,128]{2,1,0:T(8,128)(2,1)S(1)} %copy-done.10, ...), custom_call_target="tpu_custom_call" | custom-call | flops 7000000000 | bytes 21000000 | tf_op jit(solution)/shard_map/pallas_call | solution.py:559
  117.8 4.3 %all-to-all-start.3 = ((bf16[16,256,128]{2,1,0:T(8,128)(2,1)}), bf16[16,256,128]{2,1,0:T(8,128)(2,1)S(1)}, u32[]{:S(2)}, u32[]{:S(2)}) async-start(bf16[16,256,128]{2,1,0:T(8,128)(2,1)} %copy-done), calls=%async_computation.3 | async-start | bytes 2097152 | tf_op jit(solution)/shard_map/all_to_all | solution.py:620
  123.0 7.1 %shard_map.127 = bf16[16,384,128]{2,1,0:T(8,128)(2,1)} custom-call(s32[17]{0:T(128)S(1)} %pad_add_fusion.info_ref, bf16[16,400,128]{2,1,0:T(8,128)(2,1)S(1)} %all-to-all-done.1.second_ref, bf16[2,1024,128]{2,1,0:T(8,128)(2,1)} %copy-done.9, f32[2,128,128]{2,1,0:T(8,128)S(1)} %copy-done.3, f32[16,128]{1,0:T(8,128)S(1)} %add.3.sums_ref, ...), custom_call_target="tpu_custom_call" | custom-call | flops 5000000000 | bytes 15000000 | tf_op jit(solution)/shard_map/pallas_call | solution.py:559
  130.0 16.1 %all-to-all-done.3.in_ref = bf16[16,256,128]{2,1,0:T(8,128)(2,1)S(1)} async-done(((bf16[16,256,128]{2,1,0:T(8,128)(2,1)}), bf16[16,256,128]{2,1,0:T(8,128)(2,1)S(1)}, u32[]{:S(2)}, u32[]{:S(2)}) %all-to-all-start.3) | async-done | bytes 1048608 | tf_op jit(solution)/shard_map/all_to_all | solution.py:620
  146.1 3.6 %all-to-all-start.4 = ((bf16[16,384,128]{2,1,0:T(8,128)(2,1)}), bf16[16,384,128]{2,1,0:T(8,128)(2,1)S(1)}, u32[]{:S(2)}, u32[]{:S(2)}) async-start(bf16[16,384,128]{2,1,0:T(8,128)(2,1)} %shard_map.127), calls=%async_computation.4 | async-start | bytes 3145728 | tf_op jit(solution)/shard_map/all_to_all | solution.py:626
  149.7 1.8 %shard_map.129 = (f32[128,16,128]{2,1,0:T(8,128)}, f32[128,16,128]{2,1,0:T(8,128)}) custom-call(bf16[16,256,128]{2,1,0:T(8,128)(2,1)S(1)} %all-to-all-done.3.in_ref), custom_call_target="tpu_custom_call" | custom-call | flops 2000000000 | bytes 6000000 | tf_op jit(solution)/shard_map/pallas_call | solution.py:559
  151.5 18.3 %all-to-all-done.4.in_ref = bf16[16,384,128]{2,1,0:T(8,128)(2,1)S(1)} async-done(((bf16[16,384,128]{2,1,0:T(8,128)(2,1)}), bf16[16,384,128]{2,1,0:T(8,128)(2,1)S(1)}, u32[]{:S(2)}, u32[]{:S(2)}) %all-to-all-start.4) | async-done | bytes 1572896 | tf_op jit(solution)/shard_map/all_to_all | solution.py:626
  169.8 2.1 %shard_map.128 = (f32[128,16,128]{2,1,0:T(8,128)}, f32[128,16,128]{2,1,0:T(8,128)}, f32[128,16,128]{2,1,0:T(8,128)}) custom-call(bf16[16,384,128]{2,1,0:T(8,128)(2,1)S(1)} %all-to-all-done.4.in_ref), custom_call_target="tpu_custom_call" | custom-call | flops 3000000000 | bytes 9000000 | tf_op jit(solution)/shard_map/pallas_call | solution.py:559
  (39 shorter events, 8.4 us)
Async XLA Ops:
  4.1 7.2 %copy-start.6 = (f32[16,128]{1,0:T(8,128)S(1)}, f32[16,128]{1,0:T(8,128)}, u32[]{:S(2)}) copy-start(f32[16,128]{1,0:T(8,128)} %refs_3_.1) | copy-start | bytes 24580
  4.1 43.5 %all-to-all-start = ((bf16[16,384,128]{2,1,0:T(8,128)(2,1)}), bf16[16,384,128]{2,1,0:T(8,128)(2,1)S(1)}, u32[]{:S(2)}, u32[]{:S(2)}) async-start(bf16[16,384,128]{2,1,0:T(8,128)(2,1)} %shard_map.120), calls=%async_computation | async-start | bytes 3145728 | tf_op jit(solution)/shard_map/all_to_all | solution.py:620
  14.9 36.3 %copy-start.11 = (s32[16]{0:T(128)S(1)}, s32[16]{0:T(128)}, u32[]{:S(2)}) copy-start(s32[16]{0:T(128)} %param.15) | copy-start | bytes 196
  47.6 26.1 %all-to-all-start.1 = ((bf16[16,400,128]{2,1,0:T(8,128)(2,1)}), bf16[16,400,128]{2,1,0:T(8,128)(2,1)S(1)}, u32[]{:S(2)}, u32[]{:S(2)}) async-start(bf16[16,400,128]{2,1,0:T(8,128)(2,1)} %shard_map.119), calls=%async_computation.1 | async-start | bytes 3276800 | tf_op jit(solution)/shard_map/all_to_all | solution.py:626
  57.7 0.8 copy-start.7
  58.5 20.1 %collective-permute-start.1 = (bf16[1024,128]{1,0:T(8,128)(2,1)}, bf16[1024,128]{1,0:T(8,128)(2,1)S(1)}, u32[]{:S(2)}, u32[]{:S(2)}) collective-permute-start(bf16[1024,128]{1,0:T(8,128)(2,1)} %get-tuple-element.25), channel_id=1, source_target_pairs={{0,16},{2,18},{4,20},{6,22},{8,24},{10,26},{12,28},{14,30},{16,0},... | collective-permute-start | bytes 786440 | tf_op jit(solution)/shard_map/ppermute | solution.py:641
  74.3 8.7 %copy-start.8 = (f32[1024,128]{1,0:T(8,128)S(1)}, f32[1024,128]{1,0:T(8,128)}, u32[]{:S(2)}) copy-start(f32[1024,128]{1,0:T(8,128)} %copy-done.7) | copy-start | bytes 1572868
  74.3 8.7 %collective-permute-start = (f32[2,128,128]{2,1,0:T(8,128)S(1)}, f32[2,128,128]{2,1,0:T(8,128)S(1)}, u32[]{:S(2)}, u32[]{:S(2)}) collective-permute-start(f32[2,128,128]{2,1,0:T(8,128)S(1)} %shard_map.121), channel_id=1, source_target_pairs={{0,16},{2,18},{4,20},{6,22},{8,24},{10,26},{12,28},{14,30},{1,17},... | collective-permute-start | bytes 393224 | tf_op jit(solution)/shard_map/ppermute | solution.py:631
  83.0 1.8 %copy-start.2 = (f32[2,128,128]{2,1,0:T(8,128)}, f32[2,128,128]{2,1,0:T(8,128)S(1)}, u32[]{:S(2)}) copy-start(f32[2,128,128]{2,1,0:T(8,128)S(1)} %collective-permute-done.incoming_ref) | copy-start | bytes 393220
  84.7 0.7 copy-start.1
  85.4 0.8 copy-start.9
  86.9 11.7 %all-to-all-start.2 = ((f32[8,16,128]{2,1,0:T(8,128)}), f32[8,16,128]{2,1,0:T(8,128)}, u32[]{:S(2)}, u32[]{:S(2)}) async-start(f32[8,16,128]{2,1,0:T(8,128)} %broadcast_in_dim.16), calls=%async_computation.2 | async-start | bytes 131072 | tf_op jit(solution)/shard_map/all_to_all | solution.py:626
  92.7 15.5 %collective-permute-start.4 = (bf16[1024,128]{1,0:T(8,128)(2,1)}, bf16[1024,128]{1,0:T(8,128)(2,1)}, u32[]{:S(2)}, u32[]{:S(2)}) collective-permute-start(bf16[1024,128]{1,0:T(8,128)(2,1)} %copy-done.1), channel_id=1, source_target_pairs={{0,16},{2,18},{4,20},{6,22},{8,24},{10,26},{12,28},{14,30},{16,0},... | collective-permute-start | bytes 786440 | tf_op jit(solution)/shard_map/ppermute | solution.py:641
  99.5 1.2 collective-permute-start.2
  100.7 7.5 %collective-permute-start.5 = (f32[8,128]{1,0:T(8,128)S(1)}, f32[8,128]{1,0:T(8,128)S(1)}, u32[]{:S(2)}, u32[]{:S(2)}) collective-permute-start(f32[8,128]{1,0:T(8,128)S(1)} %slice.4), channel_id=1, source_target_pairs={{0,16},{2,18},{4,20},{6,22},{8,24},{10,26},{12,28},{14,30},{16,0},... | collective-permute-start | bytes 12296 | tf_op jit(solution)/shard_map/ppermute | solution.py:641
  100.7 7.5 %copy-start.10 = (bf16[2,1024,128]{2,1,0:T(8,128)(2,1)S(1)}, bf16[2,1024,128]{2,1,0:T(8,128)(2,1)}, u32[]{:S(2)}) copy-start(bf16[2,1024,128]{2,1,0:T(8,128)(2,1)} %copy-done.9) | copy-start | bytes 1572868
  103.3 13.8 %collective-permute-start.3 = (f32[2,128,128]{2,1,0:T(8,128)S(1)}, f32[2,128,128]{2,1,0:T(8,128)S(1)}, u32[]{:S(2)}, u32[]{:S(2)}) collective-permute-start(f32[2,128,128]{2,1,0:T(8,128)S(1)} %shard_map.125), channel_id=1, source_target_pairs={{16,0},{18,2},{20,4},{22,6},{24,8},{26,10},{28,12},{30,14},{17,1},... | collective-permute-start | bytes 393224 | tf_op jit(solution)/shard_map/ppermute | solution.py:636
  116.1 1.0 copy-start
  117.1 5.0 %copy-start.3 = (f32[2,128,128]{2,1,0:T(8,128)S(1)}, f32[2,128,128]{2,1,0:T(8,128)}, u32[]{:S(2)}) copy-start(f32[2,128,128]{2,1,0:T(8,128)} %copy-done.2) | copy-start | bytes 393220
  117.1 0.7 copy-start.4
  117.8 28.4 %all-to-all-start.3 = ((bf16[16,256,128]{2,1,0:T(8,128)(2,1)}), bf16[16,256,128]{2,1,0:T(8,128)(2,1)S(1)}, u32[]{:S(2)}, u32[]{:S(2)}) async-start(bf16[16,256,128]{2,1,0:T(8,128)(2,1)} %copy-done), calls=%async_computation.3 | async-start | bytes 2097152 | tf_op jit(solution)/shard_map/all_to_all | solution.py:620
  122.1 0.9 copy-start.5
  146.1 23.7 %all-to-all-start.4 = ((bf16[16,384,128]{2,1,0:T(8,128)(2,1)}), bf16[16,384,128]{2,1,0:T(8,128)(2,1)S(1)}, u32[]{:S(2)}, u32[]{:S(2)}) async-start(bf16[16,384,128]{2,1,0:T(8,128)(2,1)} %shard_map.127), calls=%async_computation.4 | async-start | bytes 3145728 | tf_op jit(solution)/shard_map/all_to_all | solution.py:626

commit v6 on v5

--- a/solution.py
+++ b/solution.py
@@ -616,6 +616,36 @@
             out_ref[begin : begin + heads] = dot(swap, rows).reshape(heads, heads, width)
 
 
+PIECES = 2
+
+
+def streamed_pack(order, arrays):
+    length, heads, width = arrays[0].shape
+    part = length // PIECES
+
+    def kernel(*refs):
+        swap = swap_matrix(heads)
+        out_ref = refs[-1]
+        for place, ref in enumerate(refs[:-1]):
+            for begin in range(0, part, heads):
+                rows = ref[begin : begin + heads].reshape(heads * heads, width)
+                swapped = dot(swap, rows).astype(bf16)
+                for h in range(heads):
+                    out_ref[order[h], place, begin : begin + heads, :] = swapped[
+                        h * heads : (h + 1) * heads, :
+                    ]
+
+    packed = pl.pallas_call(
+        kernel,
+        grid=(PIECES,),
+        out_shape=jax.ShapeDtypeStruct((heads, len(arrays), length, width), bf16),
+        in_specs=[pl.BlockSpec((part, heads, width), lambda n: (n, 0, 0))] * len(arrays),
+        out_specs=pl.BlockSpec((heads, len(arrays), part, width), lambda n: (0, 0, n, 0)),
+        compiler_params=pltpu.CompilerParams(vmem_limit_bytes=16 * 1024 * 1024),
+    )(*[pltpu.with_memory_space_constraint(array, pltpu.HBM) for array in arrays])
+    return packed.reshape(heads, len(arrays) * length, width)
+
+
 def exchange(x):
     return lax.all_to_all(x, "seq", 0, 0, tiled=True)
 
@@ -671,7 +701,7 @@
             partial(pack, order), 3, [((heads_here, rows, width), bf16)], [], *arrays, *more, whole=True
         )[0]
 
-    first = exchange(packed(paired, 3 * length, (query_two, key_two, out_grad)))
+    first = exchange(streamed_pack(paired, (query_two, key_two, out_grad)))
     second = packed(straight, 3 * length + PART_ROWS, (query_one, key_one, value_one), log_decay)
     second, first = lax.optimization_barrier((second, first))
     second = exchange_half(second)
@@ -733,6 +763,7 @@
         prefetch=1,
     )
     raw_in_hbm = pltpu.with_memory_space_constraint(raw, pltpu.HBM)
+    other_in_hbm = pltpu.with_memory_space_constraint(grad_other, pltpu.HBM)
     kept_in_hbm = pltpu.with_memory_space_constraint(grad_kept, pltpu.HBM)
     (state_grad,) = call(
         partial(linear_state_grad, features, heads),
@@ -744,7 +775,7 @@
         raw_in_hbm,
         sums,
         kept_in_hbm,
-        grad_other,
+        other_in_hbm,
         prefetch=1,
     )
     later_grad = downward(state_grad)
@@ -761,7 +792,7 @@
         incoming,
         sums,
         kept_in_hbm,
-        grad_other,
+        other_in_hbm,
         later_grad,
         prefetch=1,
     )

time: 175 us -> 174 us (level)
    pallas_call x11 -> x10, Pallas kernels: 39.8 us -> 36.1 us  [call(): pl.pallas_call(kernel, out_shape=results, in_specs=[smem] * prefetch + [v...]
    pallas_call x0 -> x1, Pallas kernels: none -> 3.21 us  [streamed_pack(): pl.pallas_call(kernel, grid=(PIECES,), out_shape=jax.ShapeDtypeStruct((he...]
    unnamed x24 -> x26, local copies, waits for them, and re-layouts: 4.84 us -> 4.83 us
where the time goes in v6:
time: 174 us; the launch traced here: 171 us
  waiting for transfers between devices  91.9 us (53%)
  Pallas kernels  39.3 us (23%)
  starting transfers between devices  32.9 us (19%)
  local copies, waits for them, and re-layouts  5.46 us (3%)
    all_to_all x2, waiting for transfers between devices, exchange(): return lax.all_to_all(x, 'seq', 0, 0, tiled=True)  48.9 us
    all_to_all x3, waiting for transfers between devices, exchange_half(): return lax.all_to_all(x, 'seq', 0, 0, tiled=True, axis_index_groups=groups)  37.5 us
    pallas_call x10, Pallas kernels, call(): pl.pallas_call(kernel, out_shape=results, in_specs=[smem] * prefetch + [v...  36.1 us
    all_to_all x3, starting transfers between devices, exchange_half(): return lax.all_to_all(x, 'seq', 0, 0, tiled=True, axis_index_groups=groups)  13 us
    all_to_all x2, starting transfers between devices, exchange(): return lax.all_to_all(x, 'seq', 0, 0, tiled=True)  11.5 us
    unnamed x26, local copies, waits for them, and re-layouts  4.83 us
    ppermute x1, starting transfers between devices, downward(): return lax.ppermute(x, 'seq', [(i + side, i) for i in range(side)])  4.83 us
    ppermute x1, waiting for transfers between devices, upward(): return lax.ppermute(x, 'seq', [(i, i + side) for i in range(side)])  4.38 us
  transfers between devices with their start and end apart: 11, of which 7 were waited for; matrix products, arithmetic and copies ran while one was open for 1% of the time, Pallas kernels for 19%

profile of v6, /device:TPU:16, one launch (start us, length us, event | category | flops | bytes accessed | tf_op | source)
XLA Modules:
  0.0 171.5 jit_solution(16486045056118660384)
XLA Ops:
  0.6 3.2 %shard_map.120 = bf16[16,3,128,128]{3,2,1,0:T(8,128)(2,1)} custom-call(bf16[128,16,128]{2,1,0:T(8,128)(2,1)} %refs_0_.3, bf16[128,16,128]{2,1,0:T(8,128)(2,1)} %refs_1_.3, bf16[128,16,128]{2,1,0:T(8,128)(2,1)} %refs_2_.3), custom_call_target="tpu_custom_call" | custom-call | tf_op jit(solution)/shard_map/pallas_call | solution.py:638
  3.8 7.2 %all-to-all-start = ((bf16[16,384,128]{2,1,0:T(8,128)(2,1)}), bf16[16,384,128]{2,1,0:T(8,128)(2,1)S(1)}, u32[]{:S(2)}, u32[]{:S(2)}) async-start(bf16[16,384,128]{2,1,0:T(8,128)(2,1)} %bitcast.1), calls=%async_computation | async-start | bytes 3145728 | tf_op jit(solution)/shard_map/all_to_all | solution.py:650
  11.1 3.5 %shard_map.119 = bf16[16,400,128]{2,1,0:T(8,128)(2,1)} custom-call(bf16[128,16,128]{2,1,0:T(8,128)(2,1)} %refs_0_.2, bf16[128,16,128]{2,1,0:T(8,128)(2,1)} %refs_1_.2, bf16[128,16,128]{2,1,0:T(8,128)(2,1)} %refs_2_.2, f32[16,128]{1,0:T(8,128)S(1)} %copy-done.7), custom_call_target="tpu_custom_call" | custom-call | flops 3000000000 | bytes 9000000 | tf_op jit(solution)/shard_map/pallas_call | solution.py:559
  14.6 32.7 %all-to-all-done.first_ref = bf16[16,384,128]{2,1,0:T(8,128)(2,1)S(1)} async-done(((bf16[16,384,128]{2,1,0:T(8,128)(2,1)}), bf16[16,384,128]{2,1,0:T(8,128)(2,1)S(1)}, u32[]{:S(2)}, u32[]{:S(2)}) %all-to-all-start) | async-done | bytes 1572896 | tf_op jit(solution)/shard_map/all_to_all | solution.py:650
  47.3 3.6 %all-to-all-start.1 = ((bf16[16,400,128]{2,1,0:T(8,128)(2,1)}), bf16[16,400,128]{2,1,0:T(8,128)(2,1)S(1)}, u32[]{:S(2)}, u32[]{:S(2)}) async-start(bf16[16,400,128]{2,1,0:T(8,128)(2,1)} %shard_map.119), calls=%async_computation.1 | async-start | bytes 3276800 | tf_op jit(solution)/shard_map/all_to_all | solution.py:656
  51.2 6.2 %shard_map.123 = (f32[4,512]{1,0:T(4,128)S(1)}, f32[1024,128]{1,0:T(8,128)S(1)}, bf16[1024,128]{1,0:T(8,128)(2,1)}) custom-call(s32[17]{0:T(128)S(1)} %pad_add_fusion.info_ref, bf16[16,384,128]{2,1,0:T(8,128)(2,1)S(1)} %all-to-all-done.first_ref), custom_call_target="tpu_custom_call" | custom-call | flops 6000000000 | bytes 18000000 | tf_op jit(solution)/shard_map/pallas_call | solution.py:559
  58.2 1.9 %collective-permute-start.1 = (bf16[1024,128]{1,0:T(8,128)(2,1)}, bf16[1024,128]{1,0:T(8,128)(2,1)S(1)}, u32[]{:S(2)}, u32[]{:S(2)}) collective-permute-start(bf16[1024,128]{1,0:T(8,128)(2,1)} %get-tuple-element.25), channel_id=1, source_target_pairs={{0,16},{2,18},{4,20},{6,22},{8,24},{10,26},{12,28},{14,30},{16,0},... | collective-permute-start | bytes 786440 | tf_op jit(solution)/shard_map/ppermute | solution.py:671
  60.1 13.2 %all-to-all-done.1.second_ref = bf16[16,400,128]{2,1,0:T(8,128)(2,1)S(1)} async-done(((bf16[16,400,128]{2,1,0:T(8,128)(2,1)}), bf16[16,400,128]{2,1,0:T(8,128)(2,1)S(1)}, u32[]{:S(2)}, u32[]{:S(2)}) %all-to-all-start.1) | async-done | bytes 1638432 | tf_op jit(solution)/shard_map/all_to_all | solution.py:656
  74.0 1.6 collective-permute-start
  75.6 2.7 %shard_map.122.local_ref = f32[2,1024,128]{2,1,0:T(8,128)S(1)} custom-call(bf16[16,400,128]{2,1,0:T(8,128)(2,1)S(1)} %all-to-all-done.1.second_ref), custom_call_target="tpu_custom_call" | custom-call | flops 4000000000 | bytes 12000000 | tf_op jit(solution)/shard_map/pallas_call | solution.py:559
  78.4 4.4 %collective-permute-done.incoming_ref = f32[2,128,128]{2,1,0:T(8,128)S(1)} collective-permute-done((f32[2,128,128]{2,1,0:T(8,128)S(1)}, f32[2,128,128]{2,1,0:T(8,128)S(1)}, u32[]{:S(2)}, u32[]{:S(2)}) %collective-permute-start) | collective-permute-done | bytes 131104 | tf_op jit(solution)/shard_map/ppermute | solution.py:661
  82.7 1.7 %shard_map.124 = (bf16[2,1024,128]{2,1,0:T(8,128)(2,1)S(1)}, bf16[1024,128]{1,0:T(8,128)(2,1)S(1)}, f32[16,128]{1,0:T(8,128)S(1)}) custom-call(s32[17]{0:T(128)S(1)} %pad_add_fusion.info_ref, bf16[16,400,128]{2,1,0:T(8,128)(2,1)S(1)} %all-to-all-done.1.second_ref, f32[2,128,128]{2,1,0:T(8,128)S(1)} %collective-permute-done.incoming_ref, ...), custom_call_target="tpu_custom_call" | custom-call | flops 2000000000 | bytes 6000000 | tf_op jit(solution)/shard_map/pallas_call | solution.py:559
  86.6 5.8 %all-to-all-start.2 = ((f32[8,16,128]{2,1,0:T(8,128)}), f32[8,16,128]{2,1,0:T(8,128)}, u32[]{:S(2)}, u32[]{:S(2)}) async-start(f32[8,16,128]{2,1,0:T(8,128)} %broadcast_in_dim.16), calls=%async_computation.2 | async-start | bytes 131072 | tf_op jit(solution)/shard_map/all_to_all | solution.py:656
  92.4 5.9 %all-to-all-done.2 = f32[8,16,128]{2,1,0:T(8,128)} async-done(((f32[8,16,128]{2,1,0:T(8,128)}), f32[8,16,128]{2,1,0:T(8,128)}, u32[]{:S(2)}, u32[]{:S(2)}) %all-to-all-start.2) | async-done | bytes 65568 | tf_op jit(solution)/shard_map/all_to_all | solution.py:656
  100.4 2.7 %shard_map.125 = f32[2,128,128]{2,1,0:T(8,128)S(1)} custom-call(s32[17]{0:T(128)S(1)} %pad_add_fusion.info_ref, bf16[16,400,128]{2,1,0:T(8,128)(2,1)S(1)} %all-to-all-done.1.second_ref, bf16[2,1024,128]{2,1,0:T(8,128)(2,1)} %copy-done.10, f32[16,128]{1,0:T(8,128)S(1)} %add.3.sums_ref, f32[1024,128]{1,0:T(8,128)} %copy-done.8, bf16[1024,128]{1,0:T(8,128)(2,1)} %copy-done.1), custom_call_target="tpu_custom_call" | custom-call | flops 2000000000 | bytes 6000000 | tf_op jit(solution)/shard_map/pallas_call | solution.py:559
  103.1 4.8 %collective-permute-start.3 = (f32[2,128,128]{2,1,0:T(8,128)S(1)}, f32[2,128,128]{2,1,0:T(8,128)S(1)}, u32[]{:S(2)}, u32[]{:S(2)}) collective-permute-start(f32[2,128,128]{2,1,0:T(8,128)S(1)} %shard_map.125), channel_id=1, source_target_pairs={{16,0},{18,2},{20,4},{22,6},{24,8},{26,10},{28,12},{30,14},{17,1},... | collective-permute-start | bytes 393224 | tf_op jit(solution)/shard_map/ppermute | solution.py:666
  108.0 7.6 %shard_map.126 = bf16[16,256,128]{2,1,0:T(8,128)(2,1)S(1)} custom-call(s32[17]{0:T(128)S(1)} %pad_add_fusion.info_ref, bf16[16,384,128]{2,1,0:T(8,128)(2,1)S(1)} %all-to-all-done.first_ref, f32[4,512]{1,0:T(4,128)S(1)} %get-tuple-element.28.mass_ref, bf16[2,1024,128]{2,1,0:T(8,128)(2,1)S(1)} %copy-done.11, ...), custom_call_target="tpu_custom_call" | custom-call | flops 7000000000 | bytes 21000000 | tf_op jit(solution)/shard_map/pallas_call | solution.py:559
  117.1 4.3 %all-to-all-start.3 = ((bf16[16,256,128]{2,1,0:T(8,128)(2,1)}), bf16[16,256,128]{2,1,0:T(8,128)(2,1)S(1)}, u32[]{:S(2)}, u32[]{:S(2)}) async-start(bf16[16,256,128]{2,1,0:T(8,128)(2,1)} %copy-done), calls=%async_computation.3 | async-start | bytes 2097152 | tf_op jit(solution)/shard_map/all_to_all | solution.py:650
  122.4 7.1 %shard_map.127 = bf16[16,384,128]{2,1,0:T(8,128)(2,1)} custom-call(s32[17]{0:T(128)S(1)} %pad_add_fusion.info_ref, bf16[16,400,128]{2,1,0:T(8,128)(2,1)S(1)} %all-to-all-done.1.second_ref, bf16[2,1024,128]{2,1,0:T(8,128)(2,1)} %copy-done.10, f32[2,128,128]{2,1,0:T(8,128)S(1)} %copy-done.4, f32[16,128]{1,0:T(8,128)S(1)} %add.3.sums_ref, ...), custom_call_target="tpu_custom_call" | custom-call | flops 5000000000 | bytes 15000000 | tf_op jit(solution)/shard_map/pallas_call | solution.py:559
  129.5 16.2 %all-to-all-done.3.in_ref = bf16[16,256,128]{2,1,0:T(8,128)(2,1)S(1)} async-done(((bf16[16,256,128]{2,1,0:T(8,128)(2,1)}), bf16[16,256,128]{2,1,0:T(8,128)(2,1)S(1)}, u32[]{:S(2)}, u32[]{:S(2)}) %all-to-all-start.3) | async-done | bytes 1048608 | tf_op jit(solution)/shard_map/all_to_all | solution.py:650
  145.7 3.6 %all-to-all-start.4 = ((bf16[16,384,128]{2,1,0:T(8,128)(2,1)}), bf16[16,384,128]{2,1,0:T(8,128)(2,1)S(1)}, u32[]{:S(2)}, u32[]{:S(2)}) async-start(bf16[16,384,128]{2,1,0:T(8,128)(2,1)} %shard_map.127), calls=%async_computation.4 | async-start | bytes 3145728 | tf_op jit(solution)/shard_map/all_to_all | solution.py:656
  149.3 1.8 %shard_map.129 = (f32[128,16,128]{2,1,0:T(8,128)}, f32[128,16,128]{2,1,0:T(8,128)}) custom-call(bf16[16,256,128]{2,1,0:T(8,128)(2,1)S(1)} %all-to-all-done.3.in_ref), custom_call_target="tpu_custom_call" | custom-call | flops 2000000000 | bytes 6000000 | tf_op jit(solution)/shard_map/pallas_call | solution.py:559
  151.1 18.3 %all-to-all-done.4.in_ref = bf16[16,384,128]{2,1,0:T(8,128)(2,1)S(1)} async-done(((bf16[16,384,128]{2,1,0:T(8,128)(2,1)}), bf16[16,384,128]{2,1,0:T(8,128)(2,1)S(1)}, u32[]{:S(2)}, u32[]{:S(2)}) %all-to-all-start.4) | async-done | bytes 1572896 | tf_op jit(solution)/shard_map/all_to_all | solution.py:656
  169.4 2.1 %shard_map.128 = (f32[128,16,128]{2,1,0:T(8,128)}, f32[128,16,128]{2,1,0:T(8,128)}, f32[128,16,128]{2,1,0:T(8,128)}) custom-call(bf16[16,384,128]{2,1,0:T(8,128)(2,1)S(1)} %all-to-all-done.4.in_ref), custom_call_target="tpu_custom_call" | custom-call | flops 3000000000 | bytes 9000000 | tf_op jit(solution)/shard_map/pallas_call | solution.py:559
  (41 shorter events, 8.4 us)
Async XLA Ops:
  3.8 7.2 %copy-start.7 = (f32[16,128]{1,0:T(8,128)S(1)}, f32[16,128]{1,0:T(8,128)}, u32[]{:S(2)}) copy-start(f32[16,128]{1,0:T(8,128)} %refs_3_.1) | copy-start | bytes 24580
  3.8 43.5 %all-to-all-start = ((bf16[16,384,128]{2,1,0:T(8,128)(2,1)}), bf16[16,384,128]{2,1,0:T(8,128)(2,1)S(1)}, u32[]{:S(2)}, u32[]{:S(2)}) async-start(bf16[16,384,128]{2,1,0:T(8,128)(2,1)} %bitcast.1), calls=%async_computation | async-start | bytes 3145728 | tf_op jit(solution)/shard_map/all_to_all | solution.py:650
  14.6 36.3 %copy-start.12 = (s32[16]{0:T(128)S(1)}, s32[16]{0:T(128)}, u32[]{:S(2)}) copy-start(s32[16]{0:T(128)} %param.15) | copy-start | bytes 196
  47.3 26.1 %all-to-all-start.1 = ((bf16[16,400,128]{2,1,0:T(8,128)(2,1)}), bf16[16,400,128]{2,1,0:T(8,128)(2,1)S(1)}, u32[]{:S(2)}, u32[]{:S(2)}) async-start(bf16[16,400,128]{2,1,0:T(8,128)(2,1)} %shard_map.119), calls=%async_computation.1 | async-start | bytes 3276800 | tf_op jit(solution)/shard_map/all_to_all | solution.py:656
  57.4 0.8 copy-start.8
  58.2 20.1 %collective-permute-start.1 = (bf16[1024,128]{1,0:T(8,128)(2,1)}, bf16[1024,128]{1,0:T(8,128)(2,1)S(1)}, u32[]{:S(2)}, u32[]{:S(2)}) collective-permute-start(bf16[1024,128]{1,0:T(8,128)(2,1)} %get-tuple-element.25), channel_id=1, source_target_pairs={{0,16},{2,18},{4,20},{6,22},{8,24},{10,26},{12,28},{14,30},{16,0},... | collective-permute-start | bytes 786440 | tf_op jit(solution)/shard_map/ppermute | solution.py:671
  74.0 8.7 %copy-start.9 = (f32[1024,128]{1,0:T(8,128)S(1)}, f32[1024,128]{1,0:T(8,128)}, u32[]{:S(2)}) copy-start(f32[1024,128]{1,0:T(8,128)} %copy-done.8) | copy-start | bytes 1572868
  74.0 8.7 %collective-permute-start = (f32[2,128,128]{2,1,0:T(8,128)S(1)}, f32[2,128,128]{2,1,0:T(8,128)S(1)}, u32[]{:S(2)}, u32[]{:S(2)}) collective-permute-start(f32[2,128,128]{2,1,0:T(8,128)S(1)} %shard_map.121), channel_id=1, source_target_pairs={{0,16},{2,18},{4,20},{6,22},{8,24},{10,26},{12,28},{14,30},{1,17},... | collective-permute-start | bytes 393224 | tf_op jit(solution)/shard_map/ppermute | solution.py:661
  78.3 6.1 %copy-start.1 = (bf16[1024,128]{1,0:T(8,128)(2,1)}, bf16[1024,128]{1,0:T(8,128)(2,1)S(1)}, u32[]{:S(2)}) copy-start(bf16[1024,128]{1,0:T(8,128)(2,1)S(1)} %collective-permute-done.1.other_ref) | copy-start | bytes 786436
  82.7 1.7 %copy-start.3 = (f32[2,128,128]{2,1,0:T(8,128)}, f32[2,128,128]{2,1,0:T(8,128)S(1)}, u32[]{:S(2)}) copy-start(f32[2,128,128]{2,1,0:T(8,128)S(1)} %collective-permute-done.incoming_ref) | copy-start | bytes 393220
  84.5 0.7 copy-start.2
  85.2 0.8 copy-start.10
  86.6 11.7 %all-to-all-start.2 = ((f32[8,16,128]{2,1,0:T(8,128)}), f32[8,16,128]{2,1,0:T(8,128)}, u32[]{:S(2)}, u32[]{:S(2)}) async-start(f32[8,16,128]{2,1,0:T(8,128)} %broadcast_in_dim.16), calls=%async_computation.2 | async-start | bytes 131072 | tf_op jit(solution)/shard_map/all_to_all | solution.py:656
  92.4 15.5 %collective-permute-start.4 = (bf16[1024,128]{1,0:T(8,128)(2,1)}, bf16[1024,128]{1,0:T(8,128)(2,1)S(1)}, u32[]{:S(2)}, u32[]{:S(2)}) collective-permute-start(bf16[1024,128]{1,0:T(8,128)(2,1)} %copy-done.2), channel_id=1, source_target_pairs={{0,16},{2,18},{4,20},{6,22},{8,24},{10,26},{12,28},{14,30},{16,0},... | collective-permute-start | bytes 786440 | tf_op jit(solution)/shard_map/ppermute | solution.py:671
  99.2 1.2 collective-permute-start.2
  100.4 7.5 %collective-permute-start.5 = (f32[8,128]{1,0:T(8,128)S(1)}, f32[8,128]{1,0:T(8,128)S(1)}, u32[]{:S(2)}, u32[]{:S(2)}) collective-permute-start(f32[8,128]{1,0:T(8,128)S(1)} %slice.4), channel_id=1, source_target_pairs={{0,16},{2,18},{4,20},{6,22},{8,24},{10,26},{12,28},{14,30},{16,0},... | collective-permute-start | bytes 12296 | tf_op jit(solution)/shard_map/ppermute | solution.py:671
  100.4 7.6 %copy-start.11 = (bf16[2,1024,128]{2,1,0:T(8,128)(2,1)S(1)}, bf16[2,1024,128]{2,1,0:T(8,128)(2,1)}, u32[]{:S(2)}) copy-start(bf16[2,1024,128]{2,1,0:T(8,128)(2,1)} %copy-done.10) | copy-start | bytes 1572868
  103.1 13.4 %collective-permute-start.3 = (f32[2,128,128]{2,1,0:T(8,128)S(1)}, f32[2,128,128]{2,1,0:T(8,128)S(1)}, u32[]{:S(2)}, u32[]{:S(2)}) collective-permute-start(f32[2,128,128]{2,1,0:T(8,128)S(1)} %shard_map.125), channel_id=1, source_target_pairs={{16,0},{18,2},{20,4},{22,6},{24,8},{26,10},{28,12},{30,14},{17,1},... | collective-permute-start | bytes 393224 | tf_op jit(solution)/shard_map/ppermute | solution.py:666
  115.5 1.0 copy-start
  116.5 5.0 %copy-start.4 = (f32[2,128,128]{2,1,0:T(8,128)S(1)}, f32[2,128,128]{2,1,0:T(8,128)}, u32[]{:S(2)}) copy-start(f32[2,128,128]{2,1,0:T(8,128)} %copy-done.3) | copy-start | bytes 393220
  116.5 0.6 copy-start.5
  117.1 28.5 %all-to-all-start.3 = ((bf16[16,256,128]{2,1,0:T(8,128)(2,1)}), bf16[16,256,128]{2,1,0:T(8,128)(2,1)S(1)}, u32[]{:S(2)}, u32[]{:S(2)}) async-start(bf16[16,256,128]{2,1,0:T(8,128)(2,1)} %copy-done), calls=%async_computation.3 | async-start | bytes 2097152 | tf_op jit(solution)/shard_map/all_to_all | solution.py:650
  121.5 0.9 copy-start.6
  145.7 23.7 %all-to-all-start.4 = ((bf16[16,384,128]{2,1,0:T(8,128)(2,1)}), bf16[16,384,128]{2,1,0:T(8,128)(2,1)S(1)}, u32[]{:S(2)}, u32[]{:S(2)}) async-start(bf16[16,384,128]{2,1,0:T(8,128)(2,1)} %shard_map.127), calls=%async_computation.4 | async-start | bytes 3145728 | tf_op jit(solution)/shard_map/all_to_all | solution.py:656
